TPU v7x, 32 devices: a whole 2x2x4 slice. The times are simulated.
32 devices in a mesh: rep: 2 (over y), gx: 4 (over z), gy: 2 (over x), gz: 2 (over core).
Axes of the slice: x: 2, y: 2, z: 4, core: 2. Of those that a mesh axis runs over, the one named last changes fastest.
Arguments:
- positions: float32 [3, 16, 4, 128], P(None, ('rep', 'gx'), 'gy', 'gz'), parts along dimension 1, may hold values from 0 to 6
- features: float32 [64, 16, 4, 128], P(None, ('rep', 'gx'), 'gy', 'gz'), parts along dimension 1, may hold values from -6 to 6
- nbr_index: int32 [48, 16, 4, 128], P(None, ('rep', 'gx'), 'gy', 'gz'), parts along dimension 1, may hold values from 0 to 863, as said below
- nbr_count: int32 [16, 4, 128], P(('rep', 'gx'), 'gy', 'gz'), parts along dimension 0, may hold values from 28 to 48, as said below
- bin_counts: int32 [16, 4, 4], P('rep'), parts along dimension 0, may hold values from 2 to 32, as said below
- w_self: float32 [64, 64], replicated, may hold values from -0.75 to 0.75
- w_pair: float32 [64, 64], replicated, may hold values from -0.75 to 0.75
- w_radial: float32 [8, 64], replicated, may hold values from -2 to 2
- w_tensor: float32 [64, 64], replicated, may hold values from -0.75 to 0.75
- w_mix: float32 [128, 64], replicated, may hold values from -0.5 to 0.5
- w_out: float32 [64], replicated, may hold values from -0.75 to 0.75
Outputs:
- forces: float32 [3, 16, 4, 128], P(None, ('rep', 'gx'), 'gy', 'gz'), parts along dimension 1
- atom_energy: float32 [16, 4, 128], P(('rep', 'gx'), 'gy', 'gz'), parts along dimension 0
There are 2 independent parts, one for each index of `rep`. A program takes and returns all parts, laid end to end along the dimension named above; an argument that names none is the same for every part. Nothing has to cross between parts.
Inputs may be any that keep to these rules, and one draw needn't show every extreme that they name: The atoms of a bin fill its slots 0 to bin_counts - 1. `nbr_index`: A code o * 32 + t names slot t of the bin at offset o = 9 (dx + 1) + 3 (dy + 1) + (dz + 1) from the atom's own bin, periodically; t is below that bin's count, and the code never names the atom itself. Neighbour slots 0 to nbr_count - 1 of an atom are valid.
All inputs are finite; a program needn't handle non-finite values.
Results may differ from a plain program's by a relative error of at most 0.0003.
Values sent between devices are 32-bit elements; how exact they have to be, the bound alone decides.
No kernel may reach another device: no remote copies, remote signals or barrier semaphores. Data moves between devices by JAX's collectives and lax.ppermute only.
A program may use at most 128 MiB of HBM per device.

v0:
```python
import jax
import jax.numpy as jnp
from jax import lax
from jax.sharding import PartitionSpec as P

SLOTS = 32


cell_side = 6.0
cutoff = 6.0
soften = 0.25
env_norm = 0.25
block_rows = 128
highest = lax.Precision.HIGHEST


def padded(shard, sides, width):
    for axis, dim in sides:
        peers, length = (lax.axis_size(axis), shard.shape[dim])
        up = [(i, (i + 1) % peers) for i in range(peers)]
        down = [(j, i) for i, j in up]
        last = lax.slice_in_dim(shard, length - width, length, axis=dim)
        leading = lax.slice_in_dim(shard, 0, width, axis=dim)
        before = lax.ppermute(last, axis, up)
        after = lax.ppermute(leading, axis, down)
        shard = jnp.concatenate([before, shard, after], axis=dim)
    return shard


def atom_energy(vectors, pair_terms, self_terms, edge_mask, w_radial, w_tensor, w_mix, w_out):
    squared = jnp.sum(vectors * vectors, axis=0) + soften
    distance = jnp.sqrt(squared)
    direction = vectors / distance[None]
    envelope = jnp.square(jnp.maximum(1.0 - squared / (cutoff * cutoff), 0.0)) * edge_mask
    basis_count = w_radial.shape[0]
    spacing = cutoff / (basis_count - 1)
    centres = jnp.arange(basis_count, dtype=jnp.float32) * spacing
    radial = jnp.exp(-jnp.square((distance[None] - centres[:, None, None]) / spacing))
    latent_in = (
        self_terms[:, None, :]
        + pair_terms
        + jnp.einsum("nf,nka->fka", w_radial, radial, precision=highest)
    )
    latent = jax.nn.silu(latent_in) * envelope[None]
    tensor_weights = jnp.einsum("fc,fka->cka", w_tensor, latent, precision=highest)
    channels = tensor_weights.shape[0] // 2
    vec_weights = tensor_weights[:channels]
    ten_weights = tensor_weights[channels:]
    identity = jnp.eye(3, dtype=jnp.float32)
    quadrupole = (
        direction[:, None] * direction[None, :] - identity[:, :, None, None] / 3.0
    ).reshape((9,) + direction.shape[1:])
    vec_sums = env_norm * jnp.einsum("cka,dka->cda", vec_weights, direction, precision=highest)
    ten_sums = env_norm * jnp.einsum("cka,xka->cxa", ten_weights, quadrupole, precision=highest)
    vec_scalar = vec_weights * jnp.einsum("cda,dka->cka", vec_sums, direction, precision=highest)
    ten_scalar = ten_weights * jnp.einsum("cxa,xka->cka", ten_sums, quadrupole, precision=highest)
    feat_width = latent.shape[0]
    mixture = jnp.einsum("fg,fka->gka", w_mix[:feat_width], latent, precision=highest)
    mixture = mixture + jnp.einsum(
        "cg,cka->gka", w_mix[feat_width : feat_width + channels], vec_scalar, precision=highest
    )
    mixture = mixture + jnp.einsum(
        "cg,cka->gka", w_mix[feat_width + channels :], ten_scalar, precision=highest
    )
    refined = latent + jax.nn.silu(mixture) * envelope[None]
    edge_energy = jnp.einsum("f,fka->ka", w_out, refined, precision=highest)
    return jnp.sum(edge_energy, axis=0)


def grow_z(arrays):
    return padded(arrays, (("gz", 3),), SLOTS)


def grow_xy(arrays, width):
    return padded(arrays, (("gx", 1), ("gy", 2)), width)


def fold_axis(grown, dim, inner, width):
    core = lax.slice_in_dim(grown, 2 * width, 2 * width + inner, axis=dim)
    lower = lax.slice_in_dim(grown, 0, width, axis=dim)
    upper = lax.slice_in_dim(grown, inner + 3 * width, inner + 4 * width, axis=dim)
    lower_pad = [(0, 0)] * grown.ndim
    upper_pad = [(0, 0)] * grown.ndim
    lower_pad[dim] = (0, inner - width)
    upper_pad[dim] = (inner - width, 0)
    return core + jnp.pad(lower, lower_pad) + jnp.pad(upper, upper_pad)


def fold_z(gradient):
    grown = padded(gradient, (("gz", 3),), SLOTS)
    return fold_axis(grown, 3, gradient.shape[3] - 2 * SLOTS, SLOTS)


def fold_xy(gradient, width):
    grown = padded(gradient, (("gx", 1), ("gy", 2)), width)
    along_x = fold_axis(grown, 1, gradient.shape[1] - 2 * width, width)
    return fold_axis(along_x, 2, gradient.shape[2] - 2 * width, width)


def local(
    positions,
    features,
    nbr_index,
    nbr_count,
    bin_counts,
    w_self,
    w_pair,
    w_radial,
    w_tensor,
    w_mix,
    w_out,
):
    cells_x = positions.shape[1]
    cells_y = positions.shape[2]
    cells_z = positions.shape[3] // SLOTS
    nbr_slots = nbr_index.shape[0]
    state = jnp.concatenate([positions, features], axis=0)
    width = 1
    grown = grow_xy(grow_z(state), width)
    ext_x = cells_x + 2 * width
    ext_y = cells_y + 2 * width
    ext_z = cells_z + 2
    ext_count = ext_x * ext_y * ext_z * SLOTS
    flat_state = grown.reshape(grown.shape[0], ext_count)
    ext_pos = flat_state[:3]
    ext_feat = flat_state[3:]
    pair_ext = jnp.einsum("fg,fn->gn", w_pair, ext_feat, precision=highest)
    x_index = lax.axis_index("gx")
    y_index = lax.axis_index("gy")
    z_index = lax.axis_index("gz")
    all_x = bin_counts.shape[0]
    columns = lax.dynamic_slice(
        bin_counts, (0, y_index * cells_y, z_index * cells_z), (all_x, cells_y, cells_z)
    )
    own_counts = lax.dynamic_slice_in_dim(columns, x_index * cells_x, cells_x, 0)
    cand_counts = own_counts.reshape(-1)
    cand_codes = nbr_index.reshape(nbr_slots, -1)
    cand_limits = nbr_count.reshape(-1)
    candidates = cand_counts.shape[0] * SLOTS
    index_q = jnp.arange(candidates, dtype=jnp.int32)
    cell_q = index_q // SLOTS
    slot_q = index_q % SLOTS
    row_x = cell_q // (cells_y * cells_z)
    row_y = cell_q // cells_z % cells_y
    row_z = cell_q % cells_z
    cand_ext = (((row_x + 1) * ext_y + row_y + width) * ext_z + row_z + 1) * SLOTS + slot_q
    running = jnp.cumsum(cand_counts)
    atom_total = running[-1]
    list_length = (candidates + block_rows - 1) // block_rows * block_rows
    list_rank = jnp.arange(list_length, dtype=jnp.int32)
    passed = (running[None, :] <= list_rank[:, None]).astype(jnp.int32)
    cell_pick = jnp.sum(passed, axis=1)
    earlier = jnp.sum(passed * cand_counts[None, :], axis=1)
    cand_pick = jnp.where(list_rank < atom_total, cell_pick * SLOTS + list_rank - earlier, 0)
    block_total = (atom_total + block_rows - 1) // block_rows
    neighbour_rank = jnp.arange(nbr_slots, dtype=jnp.int32)[:, None]

    def one_block(block_id, gradient):
        first = block_id * block_rows
        chosen = lax.dynamic_slice_in_dim(cand_pick, first, block_rows)
        row_live = first + jnp.arange(block_rows, dtype=jnp.int32) < atom_total
        nbr_codes = jnp.take(cand_codes, chosen, axis=1)
        limits = jnp.take(cand_limits, chosen)
        own_slot = jnp.take(cand_ext, chosen)
        own_bin = own_slot // SLOTS
        offset = nbr_codes // SLOTS
        nbr_slot = nbr_codes % SLOTS
        step_x = offset // 9 - 1
        step_y = offset // 3 % 3 - 1
        step_z = offset % 3 - 1
        nbr_ext = (own_bin[None, :] + (step_x * ext_y + step_y) * ext_z + step_z) * SLOTS + nbr_slot
        nbr_flat = nbr_ext.reshape(-1)
        image_shift = cell_side * jnp.stack([step_x, step_y, step_z]).astype(jnp.float32)
        vectors = (
            jnp.take(ext_pos, nbr_flat, axis=1).reshape(3, nbr_slots, block_rows)
            - jnp.take(ext_pos, own_slot, axis=1)[:, None, :]
            + image_shift
        )
        pair_terms = jnp.take(pair_ext, nbr_flat, axis=1).reshape(-1, nbr_slots, block_rows)
        self_terms = jnp.einsum(
            "fg,fa->ga", w_self, jnp.take(ext_feat, own_slot, axis=1), precision=highest
        )
        edge_mask = ((neighbour_rank < limits[None, :]) & row_live[None, :]).astype(jnp.float32)

        def energy_of(moved):
            return atom_energy(
                moved, pair_terms, self_terms, edge_mask, w_radial, w_tensor, w_mix, w_out
            )

        atom_values, backward = jax.vjp(energy_of, vectors)
        (pulled,) = backward(jnp.ones_like(atom_values))
        position_part = gradient[:3].at[:, nbr_flat].add(pulled.reshape(3, -1))
        position_part = position_part.at[:, own_slot].add(-jnp.sum(pulled, axis=1))
        energy_part = gradient[3].at[own_slot].add(atom_values)
        return jnp.concatenate([position_part, energy_part[None]], axis=0)

    gradient = lax.fori_loop(0, block_total, one_block, jnp.zeros((4, ext_count), jnp.float32))
    gradient = gradient.reshape(4, ext_x, ext_y, ext_z * SLOTS)
    folded = fold_z(fold_xy(gradient, width))
    return (-folded[:3], folded[3])


def solution(mesh):
    return jax.shard_map(
        local,
        mesh=mesh,
        in_specs=(
            P(None, ("rep", "gx"), "gy", "gz"),
            P(None, ("rep", "gx"), "gy", "gz"),
            P(None, ("rep", "gx"), "gy", "gz"),
            P(("rep", "gx"), "gy", "gz"),
            P("rep", None, None),
            P(),
            P(),
            P(),
            P(),
            P(),
            P(),
        ),
        out_specs=(P(None, ("rep", "gx"), "gy", "gz"), P(("rep", "gx"), "gy", "gz")),
        check_vma=False,
    )
```

profile of v0, /device:TPU:0, one launch (start us, length us, event | category | flops | bytes accessed | tf_op | source)
XLA Modules:
  0.0 525.7 jit_solution(17289474923349380983)
XLA Ops:
  31.6 473.6 %while.14 = (s32[]{:T(128)}, f32[4,2048]{1,0:T(4,128)S(1)}, s32[]{:T(128)}, s32[256]{0:T(256)S(1)}, s32[48,256]{0,1:T(8,128)}, /*index=5*/f32[64,2048]{0,1:T(8,1...) while((s32[]{:T(128)}, f32[4,2048]{1,0:T(4,128)S(1)}, ...), condition=%wide.region_16.18_spmd.clone, body=%wide.region_3.17_spmd.clone.sunk | while | flops 2095567616 | bytes 164013264 | solution.py:197
  44.6 20.9 %gather_fusion.5 = f32[6144,64]{1,0:T(8,128)} fusion(f32[64,2048]{0,1:T(8,128)S(1)} %get-tuple-element.714, s32[6144]{0:T(1024)S(1)} %broadcast_clamp_fusion.2), kind=kCustom, calls=%fused_computation.4.clone.clone.1 | custom fusion | bytes 3170304 | tf_op jit(solution)/shard_map/while/body/jit(_take)/gather | solution.py:179
  67.9 22.1 %gather_fusion.4 = f32[6144,3]{1,0:T(8,128)} fusion(f32[3,2048]{0,1:T(8,128)} %get-tuple-element.715, s32[6144]{0:T(1024)S(1)} %broadcast_clamp_fusion.2), kind=kCustom, calls=%fused_computation.5.clone.clone.1 | custom fusion | bytes 172032 | tf_op jit(solution)/shard_map/while/body/jit(_take)/gather | solution.py:175
  105.7 5.0 fusion.288
  110.7 4.0 copy.461
  114.7 5.0 fusion.291
  120.3 5.0 fusion.292
  129.1 4.0 fusion.293
  133.1 4.9 fusion.289
  144.8 5.9 %multiply_reduce_fusion.7 = (f32[48,128]{1,0:T(8,128)}, f32[64,48,128]{2,0,1:T(8,128)}, f32[48,128,64]{1,2,0:T(8,128)S(1)}) fusion(f32[64]{0:T(128)S(1)} %copy-done.41, f32[48,128]{1,0:T(8,128)} %copy-done.30, f32[48,128,64]{1,2,0:T(8,128)S(1)} %fusion.290, f32[48,128,64]{1,2,0:T(8,128)S(1)} %copy-done.19, f32[128,64]{0,1:T(8,128)} %get-tuple-element.747, ...), kind=kOutput, calls=%fused_computation.40.clone.1 | convolution fusion | flops 309848064 | bytes 7971072 | tf_op jit(solution)/shard_map/while/body/jvp(fg,fka->gka)/dot_general | solution.py:58
  165.3 4.0 copy.464
  169.3 4.4 fusion.302
  183.6 5.9 %fusion.295 = f32[128,32,48]{2,1,0:T(8,128)} fusion(f32[128,3,32]{2,1,0:T(4,128)} %copy-done.15, f32[3,48,128]{1,0,2:T(4,128)S(1)} %copy.460), kind=kOutput, calls=%fused_computation.296.clone.1 | convolution fusion | flops 7077888 | bytes 909312 | tf_op jit(solution)/shard_map/while/body/transpose(jvp(cka,dka->cda))/dot_general | solution.py:53
  196.0 3.9 copy.466
  213.4 4.8 fusion.296
  230.4 33.9 %scatter_fusion.1 = f32[3,2048]{0,1:T(8,128)S(1)} fusion(f32[3,2048]{0,1:T(8,128)S(1)} %copy-done.9, s32[6144]{0:T(1024)S(1)} %bitcast.448, f32[6144,3]{1,0:T(8,128)} %copy.472), kind=kCustom, calls=%fused_computation.7.clone.clone.1 | custom fusion | flops 18432 | bytes 245760 | tf_op jit(solution)/shard_map/while/body/scatter-add | solution.py:192
  279.5 20.9 %gather_fusion.5 = f32[6144,64]{1,0:T(8,128)} fusion(f32[64,2048]{0,1:T(8,128)S(1)} %get-tuple-element.714, s32[6144]{0:T(1024)S(1)} %broadcast_clamp_fusion.2), kind=kCustom, calls=%fused_computation.4.clone.clone.1 | custom fusion | bytes 3170304 | tf_op jit(solution)/shard_map/while/body/jit(_take)/gather | solution.py:179
  302.7 22.1 %gather_fusion.4 = f32[6144,3]{1,0:T(8,128)} fusion(f32[3,2048]{0,1:T(8,128)} %get-tuple-element.715, s32[6144]{0:T(1024)S(1)} %broadcast_clamp_fusion.2), kind=kCustom, calls=%fused_computation.5.clone.clone.1 | custom fusion | bytes 172032 | tf_op jit(solution)/shard_map/while/body/jit(_take)/gather | solution.py:175
  340.1 5.0 fusion.288
  345.1 4.0 copy.461
  349.0 5.0 fusion.291
  354.7 5.2 fusion.292
  363.7 4.0 fusion.293
  367.7 4.9 fusion.289
  379.4 5.7 %multiply_reduce_fusion.7 = (f32[48,128]{1,0:T(8,128)}, f32[64,48,128]{2,0,1:T(8,128)}, f32[48,128,64]{1,2,0:T(8,128)S(1)}) fusion(f32[64]{0:T(128)S(1)} %copy-done.41, f32[48,128]{1,0:T(8,128)} %copy-done.30, f32[48,128,64]{1,2,0:T(8,128)S(1)} %fusion.290, f32[48,128,64]{1,2,0:T(8,128)S(1)} %copy-done.19, f32[128,64]{0,1:T(8,128)} %get-tuple-element.747, ...), kind=kOutput, calls=%fused_computation.40.clone.1 | convolution fusion | flops 309848064 | bytes 7971072 | tf_op jit(solution)/shard_map/while/body/jvp(fg,fka->gka)/dot_general | solution.py:58
  399.6 4.0 copy.464
  403.7 4.4 fusion.302
  418.0 6.1 %fusion.295 = f32[128,32,48]{2,1,0:T(8,128)} fusion(f32[128,3,32]{2,1,0:T(4,128)} %copy-done.15, f32[3,48,128]{1,0,2:T(4,128)S(1)} %copy.460), kind=kOutput, calls=%fused_computation.296.clone.1 | convolution fusion | flops 7077888 | bytes 909312 | tf_op jit(solution)/shard_map/while/body/transpose(jvp(cka,dka->cda))/dot_general | solution.py:53
  430.6 3.9 copy.466
  447.9 4.8 fusion.296
  465.0 35.7 %scatter_fusion.1 = f32[3,2048]{0,1:T(8,128)S(1)} fusion(f32[3,2048]{0,1:T(8,128)S(1)} %copy-done.9, s32[6144]{0:T(1024)S(1)} %bitcast.448, f32[6144,3]{1,0:T(8,128)} %copy.472), kind=kCustom, calls=%fused_computation.7.clone.clone.1 | custom fusion | flops 18432 | bytes 245760 | tf_op jit(solution)/shard_map/while/body/scatter-add | solution.py:192
  505.3 6.3 %collective-permute-start.6 = (f32[4,1,4,128]{3,2,1,0:T(4,128)S(1)}, f32[4,1,4,128]{3,2,1,0:T(4,128)S(1)}, u32[]{:S(2)}, u32[]{:S(2)}) collective-permute-start(f32[4,1,4,128]{3,2,1,0:T(4,128)S(1)} %get-tuple-element.510), channel_id=1, source_target_pairs={{0,4},{4,8},{8,12},{12,0},{1,5},{5,9},{9,13},{13,1},{2,6},{6,10},{... | collective-permute-start | bytes 24584 | tf_op jit(solution)/shard_map/ppermute | solution.py:24
  (370 shorter events, 243.7 us)
Async XLA Ops:
  0.6 26.5 %copy-start = (f32[64,64]{1,0:T(8,128)S(1)}, f32[64,64]{1,0:T(8,128)}, u32[]{:S(2)}) copy-start(f32[64,64]{1,0:T(8,128)} %param.21) | copy-start | bytes 49156
  2.5 5.3 %collective-permute-start = (f32[67,2,2,32]{3,2,1,0:T(2,128)S(1)}, f32[67,2,2,32]{3,2,1,0:T(2,128)S(1)}, u32[]{:S(2)}, u32[]{:S(2)}) collective-permute-start(f32[67,2,2,32]{3,2,1,0:T(2,128)S(1)} %get-tuple-element.505), channel_id=1, source_target_pairs={{0,1},{1,0},{2,3},{3,2},{4,5},{5,4},{6,7},{7,6},{8,9},{9,8},{10,11... | collective-permute-start | bytes 102920 | tf_op jit(solution)/shard_map/ppermute | solution.py:24
  3.0 4.8 collective-permute-start.1
  8.2 7.6 %collective-permute-start.2 = (f32[67,1,2,128]{3,2,1,0:T(2,128)S(1)}, f32[67,1,2,128]{3,2,1,0:T(2,128)S(1)}, u32[]{:S(2)}, u32[]{:S(2)}) collective-permute-start(f32[67,1,2,128]{3,2,1,0:T(2,128)S(1)} %get-tuple-element.503), channel_id=1, source_target_pairs={{0,4},{4,8},{8,12},{12,0},{1,5},{5,9},{9,13},{13,1},{2,6},{6,10},{... | collective-permute-start | bytes 205832 | tf_op jit(solution)/shard_map/ppermute | solution.py:24
  11.3 5.3 %collective-permute-start.3 = (f32[67,1,2,128]{3,2,1,0:T(2,128)S(1)}, f32[67,1,2,128]{3,2,1,0:T(2,128)S(1)}, u32[]{:S(2)}, u32[]{:S(2)}) collective-permute-start(f32[67,1,2,128]{3,2,1,0:T(2,128)S(1)} %get-tuple-element.504), channel_id=1, source_target_pairs={{4,0},{8,4},{12,8},{0,12},{5,1},{9,5},{13,9},{1,13},{6,2},{10,6},{... | collective-permute-start | bytes 205832 | tf_op jit(solution)/shard_map/ppermute | solution.py:25
  17.2 6.5 %collective-permute-start.4 = (f32[67,4,1,128]{3,2,1,0:T(1,128)S(1)}, f32[67,4,1,128]{3,2,1,0:T(1,128)S(1)}, u32[]{:S(2)}, u32[]{:S(2)}) collective-permute-start(f32[67,4,1,128]{3,2,1,0:T(1,128)S(1)} %get-tuple-element.501), channel_id=1, source_target_pairs={{0,2},{2,0},{1,3},{3,1},{4,6},{6,4},{5,7},{7,5},{8,10},{10,8},{9,1... | collective-permute-start | bytes 411656 | tf_op jit(solution)/shard_map/ppermute | solution.py:24
  18.8 6.4 %collective-permute-start.5 = (f32[67,4,1,128]{3,2,1,0:T(1,128)S(1)}, f32[67,4,1,128]{3,2,1,0:T(1,128)S(1)}, u32[]{:S(2)}, u32[]{:S(2)}) collective-permute-start(f32[67,4,1,128]{3,2,1,0:T(1,128)S(1)} %get-tuple-element.502), channel_id=1, source_target_pairs={{2,0},{0,2},{3,1},{1,3},{6,4},{4,6},{7,5},{5,7},{10,8},{8,10},{11,... | collective-permute-start | bytes 411656 | tf_op jit(solution)/shard_map/ppermute | solution.py:25
  32.0 61.3 %copy-start.35 = (f32[8]{0:T(128)}, f32[8]{0:T(128)S(1)}, u32[]{:S(2)}) copy-start(f32[8]{0:T(128)S(1)} %iota_multiply_fusion.2) | copy-start | bytes 100 | tf_op jit(solution)/shard_map/while
  144.8 5.9 %copy-start.31 = (f32[48,128]{1,0:T(8,128)S(1)}, f32[48,128]{1,0:T(8,128)}, u32[]{:S(2)}) copy-start(f32[48,128]{1,0:T(8,128)} %copy-done.30) | copy-start | bytes 73732 | tf_op jit(solution)/shard_map/while
  158.4 5.4 %copy-start.12 = (f32[32,48,128]{2,0,1:T(8,128)}, f32[32,48,128]{2,0,1:T(8,128)S(1)}, u32[]{:S(2)}) copy-start(f32[32,48,128]{2,0,1:T(8,128)S(1)} %convolution_bitcast_fusion.15) | copy-start | bytes 2359300 | tf_op jit(solution)/shard_map/while
  169.3 4.4 copy-start.3
  173.7 4.1 copy-start.2
  230.4 36.0 %copy-start.24 = (f32[128,64]{0,1:T(8,128)S(1)}, f32[128,64]{0,1:T(8,128)}, u32[]{:S(2)}) copy-start(f32[128,64]{0,1:T(8,128)} %get-tuple-element.747) | copy-start | bytes 98308 | tf_op jit(solution)/shard_map/while
  230.4 36.0 %copy-start.28 = (f32[64,64]{1,0:T(8,128)S(1)}, f32[64,64]{1,0:T(8,128)}, u32[]{:S(2)}) copy-start(f32[64,64]{1,0:T(8,128)} %get-tuple-element.771) | copy-start | bytes 49156 | tf_op jit(solution)/shard_map/while
  230.4 36.0 %copy-start.38 = (s32[256]{0:T(256)S(1)}, s32[256]{0:T(256)}, u32[]{:S(2)}) copy-start(s32[256]{0:T(256)} %copy-done.37) | copy-start | bytes 3076 | tf_op jit(solution)/shard_map/while
  230.4 36.0 %copy-start.40 = (f32[64,64]{1,0:T(8,128)S(1)}, f32[64,64]{1,0:T(8,128)}, u32[]{:S(2)}) copy-start(f32[64,64]{1,0:T(8,128)} %get-tuple-element.840) | copy-start | bytes 49156 | tf_op jit(solution)/shard_map/while
  266.8 60.8 %copy-start.35 = (f32[8]{0:T(128)}, f32[8]{0:T(128)S(1)}, u32[]{:S(2)}) copy-start(f32[8]{0:T(128)S(1)} %iota_multiply_fusion.2) | copy-start | bytes 100 | tf_op jit(solution)/shard_map/while
  379.4 5.7 %copy-start.31 = (f32[48,128]{1,0:T(8,128)S(1)}, f32[48,128]{1,0:T(8,128)}, u32[]{:S(2)}) copy-start(f32[48,128]{1,0:T(8,128)} %copy-done.30) | copy-start | bytes 73732 | tf_op jit(solution)/shard_map/while
  392.7 5.4 %copy-start.12 = (f32[32,48,128]{2,0,1:T(8,128)}, f32[32,48,128]{2,0,1:T(8,128)S(1)}, u32[]{:S(2)}) copy-start(f32[32,48,128]{2,0,1:T(8,128)S(1)} %convolution_bitcast_fusion.15) | copy-start | bytes 2359300 | tf_op jit(solution)/shard_map/while
  403.7 4.4 copy-start.3
  408.0 4.1 copy-start.2
  464.9 37.8 %copy-start.24 = (f32[128,64]{0,1:T(8,128)S(1)}, f32[128,64]{0,1:T(8,128)}, u32[]{:S(2)}) copy-start(f32[128,64]{0,1:T(8,128)} %get-tuple-element.747) | copy-start | bytes 98308 | tf_op jit(solution)/shard_map/while
  464.9 37.9 %copy-start.28 = (f32[64,64]{1,0:T(8,128)S(1)}, f32[64,64]{1,0:T(8,128)}, u32[]{:S(2)}) copy-start(f32[64,64]{1,0:T(8,128)} %get-tuple-element.771) | copy-start | bytes 49156 | tf_op jit(solution)/shard_map/while
  464.9 37.9 %copy-start.38 = (s32[256]{0:T(256)S(1)}, s32[256]{0:T(256)}, u32[]{:S(2)}) copy-start(s32[256]{0:T(256)} %copy-done.37) | copy-start | bytes 3076 | tf_op jit(solution)/shard_map/while
  465.0 37.9 %copy-start.40 = (f32[64,64]{1,0:T(8,128)S(1)}, f32[64,64]{1,0:T(8,128)}, u32[]{:S(2)}) copy-start(f32[64,64]{1,0:T(8,128)} %get-tuple-element.840) | copy-start | bytes 49156 | tf_op jit(solution)/shard_map/while
  505.2 20.1 %copy-start.1 = (f32[64,64]{1,0:T(8,128)S(1)}, f32[64,64]{1,0:T(8,128)}, u32[]{:S(2)}) copy-start(f32[64,64]{1,0:T(8,128)} %param.21) | copy-start | bytes 49156
  505.3 7.7 %collective-permute-start.6 = (f32[4,1,4,128]{3,2,1,0:T(4,128)S(1)}, f32[4,1,4,128]{3,2,1,0:T(4,128)S(1)}, u32[]{:S(2)}, u32[]{:S(2)}) collective-permute-start(f32[4,1,4,128]{3,2,1,0:T(4,128)S(1)} %get-tuple-element.510), channel_id=1, source_target_pairs={{0,4},{4,8},{8,12},{12,0},{1,5},{5,9},{9,13},{13,1},{2,6},{6,10},{... | collective-permute-start | bytes 24584 | tf_op jit(solution)/shard_map/ppermute | solution.py:24
  511.6 3.7 collective-permute-start.7
  515.3 3.8 collective-permute-start.8
  517.4 3.7 collective-permute-start.9
  522.7 1.2 collective-permute-start.10
  522.7 1.3 collective-permute-start.11
  (58 other events, 128.6 us)
where the time goes:
time: 532 us; the launch traced here: 526 us
  local copies, waits for them, and re-layouts  211 us (40%)
  matrix products  173 us (33%)
  other arithmetic  102 us (19%)
  starting transfers between devices  16.9 us (3%)
  waiting for transfers between devices  16.6 us (3%)
    scatter-add x2, other arithmetic, one_block(): position_part = gradient[:3].at[:, nbr_flat].add(pulled.reshape(3, -1))  69.6 us
    gather x4, local copies, waits for them, and re-layouts, one_block(): jnp.take(ext_pos, nbr_flat, axis=1).reshape(3, nbr_slots, block_rows)  49.8 us
    gather x4, local copies, waits for them, and re-layouts, one_block(): jnp.take(pair_ext, nbr_flat, axis=1).reshape(-1, nbr_slots, block_rows)  46.5 us
    dot_general x6, matrix products, atom_energy(): jnp.einsum('cka,dka->cda', vec_weights, direction, precision=highest)  26.9 us
    dot_general x6, matrix products, atom_energy(): jnp.einsum('cka,xka->cxa', ten_weights, quadrupole, precision=highest)  25.9 us
    dot_general x6, matrix products, atom_energy(): jnp.einsum('cda,dka->cka', vec_sums, direction, precision=highest)  25.7 us
    dot_general x6, matrix products, atom_energy(): jnp.einsum('cxa,xka->cka', ten_sums, quadrupole, precision=highest)  24.1 us
    dot_general x4, matrix products, atom_energy(): jnp.einsum('fg,fka->gka', w_mix[:feat_width], latent, precision=highest)  18.9 us
  transfers between devices with their start and end apart: 12, of which 10 were waited for; matrix products, arithmetic and copies ran while one was open for 1% of the time, Pallas kernels for 0%

commit v1 on v0

v1 whole, which is shorter than its diff:
```python
import functools

import jax
import jax.numpy as jnp
from jax import lax
from jax.experimental import pallas as pl
from jax.experimental.pallas import tpu as pltpu
from jax.sharding import PartitionSpec as P

SLOTS = 32
cell_side = 6.0
cutoff = 6.0
soften = 0.25
env_norm = 0.25
root2 = 2.0**0.5
f32 = jnp.float32
bf16 = jnp.bfloat16
HALF = 24
WIDE = 256
FEAT = 64
ROWS = 72

U, Q, ENV, DIST, INV, VEC, DENV, GEO = 0, 3, 9, 10, 11, 12, 15, 16


def halves(x):
    hi = x.astype(bf16)
    return hi, (x - hi.astype(f32)).astype(bf16)


def stacked(x):
    hi, lo = halves(x)
    return jnp.concatenate([hi, lo, hi], axis=0)


def stacked_left(w):
    hi, lo = halves(w)
    return jnp.concatenate([hi, hi, lo], axis=1)


def dot(a, b):
    return jnp.dot(a, b, preferred_element_type=f32)


def small_stack(x):
    hi, lo = halves(x)
    hi, lo = hi.astype(f32), lo.astype(f32)
    return jnp.concatenate([hi, lo, hi, jnp.zeros_like(hi)], axis=0)


def sigmoid(x):
    return 0.5 + 0.5 * jnp.tanh(0.5 * x)


def prepare(
    w_self, w_pair, w_radial, w_tensor, w_mix, w_out, p_a, p_b, p_c, p_d, p_r, p_e, p_p, p_s, p_col
):
    tensor, mix, out_row = w_tensor[...], w_mix[...], w_out[...]
    first = jnp.concatenate(
        [tensor.T, mix[:FEAT].T, jnp.broadcast_to(out_row, (8, FEAT))], axis=0
    )
    p_a[...] = stacked_left(first)
    p_b[...] = stacked_left(mix[FEAT:].T)
    p_c[...] = stacked_left(mix * out_row)
    p_d[...] = stacked_left(tensor)
    radial = w_radial[...]
    hi, lo = halves(radial)
    hi, lo = hi.astype(f32), lo.astype(f32)
    p_r[...] = jnp.concatenate([hi, hi, lo, jnp.zeros_like(hi)], axis=0).T.astype(bf16)
    p_e[...] = stacked_left(jnp.concatenate([radial, jnp.zeros_like(radial)], axis=0))
    p_p[...] = stacked_left(w_pair[...].T)
    p_s[...] = stacked_left(w_self[...].T)
    p_col[...] = jnp.broadcast_to(out_row, (128, FEAT)).T


def layer(
    which,
    ghost,
    core,
    codes,
    limit,
    w_a,
    w_b,
    w_c,
    w_d,
    w_r,
    w_e,
    w_p,
    w_s,
    w_col,
    out,
    energy,
    pair,
    self_t,
    lane_i,
    col_i,
    geo,
    act,
    slope,
    tens,
    mix0,
    prod,
    back,
    resid,
    e_row,
    m_row,
    d_row,
    du_row,
    dr_row,
    v_acc,
    dv_acc,
    g_row,
    s_acc,
    own_sum,
):
    def source(dx, yc):
        if which == 0:
            return ghost.at[yc] if dx == 0 else core.at[dx - 1, yc]
        return ghost.at[yc] if dx == 2 else core.at[dx, yc]

    lanes = lax.broadcasted_iota(jnp.int32, (1, 128), 1)

    def both(x):
        return jnp.where(lanes < 64, pltpu.roll(x, 96, 1), pltpu.roll(x, 32, 1))

    for dx in range(3):
        rows = jnp.concatenate([source(dx, yc)[:FEAT, :] for yc in range(4)], axis=1)
        terms = dot(w_p[...], stacked(rows))
        for yc in range(4):
            pair[dx * 4 + yc] = terms[:, 128 * yc : 128 * yc + 128]
    rows = jnp.concatenate([source(1, 1 + y)[:FEAT, :] for y in range(2)], axis=1)
    terms = dot(w_s[...], stacked(rows))
    for y in range(2):
        self_t[:, 128 * y : 128 * y + 128] = both(terms[:, 128 * y : 128 * y + 128])

    code = codes[...]
    offset = code >> 5
    column = (offset * 43) >> 7
    dz = offset - 3 * column
    dx = (offset * 57) >> 9
    dy = column - 3 * dx
    lane256 = lax.broadcasted_iota(jnp.int32, (HALF, WIDE), 1)
    z_own = (lane256 >> 5) & 1
    lane_i[...] = ((z_own + dz) << 5) + (code & 31)
    col_i[...] = column
    rank = lax.broadcasted_iota(jnp.int32, (HALF, WIDE), 0) + HALF * ((lane256 >> 6) & 1)
    mask = (rank < limit[...]).astype(f32)

    steps = (dx, dy, dz)
    vec = []
    for d in range(3):
        found = []
        for y in range(2):
            own = both(source(1, 1 + y)[FEAT + d : FEAT + d + 1, :])
            parts = []
            for j in range(HALF // 8):
                where = (slice(8 * j, 8 * j + 8), slice(128 * y, 128 * y + 128))
                lane, col = lane_i[where], col_i[where]
                acc = None
                for c in range(9):
                    row = source(c // 3, y + c % 3)[FEAT + d : FEAT + d + 1, :]
                    value = jnp.take_along_axis(
                        jnp.broadcast_to(row, (8, 128)), lane, axis=1, mode="promise_in_bounds"
                    )
                    acc = value if c == 0 else jnp.where(col == c, value, acc)
                parts.append(acc)
            found.append(jnp.concatenate(parts, axis=0) - own)
        vec.append(
            jnp.concatenate(found, axis=1) + cell_side * (steps[d] - 1).astype(f32)
        )
    squared = vec[0] * vec[0] + vec[1] * vec[1] + vec[2] * vec[2] + soften
    dist = jnp.sqrt(squared)
    inv = 1.0 / dist
    u = [v * inv for v in vec]
    taper = jnp.maximum(1.0 - squared / (cutoff * cutoff), 0.0)
    for d in range(3):
        geo[U + d] = u[d]
        geo[VEC + d] = vec[d]
        geo[Q + d] = u[d] * u[d] - 1.0 / 3.0
    geo[Q + 3] = root2 * u[0] * u[1]
    geo[Q + 4] = root2 * u[0] * u[2]
    geo[Q + 5] = root2 * u[1] * u[2]
    geo[ENV] = taper * taper * mask
    geo[DENV] = taper * mask * (-2.0 / (cutoff * cutoff))
    geo[DIST] = dist
    geo[INV] = inv

    spacing = cutoff / (w_e.shape[0] // 2 - 1)
    level = lax.broadcasted_iota(jnp.int32, (8, 1), 0).astype(f32)

    def row(k, s):
        return geo[k, pl.ds(s, 1), :]

    def basis(s):
        x = row(DIST, s) / spacing - level
        return x, jnp.exp(-x * x)

    v_acc[...] = jnp.zeros_like(v_acc)
    dv_acc[...] = jnp.zeros_like(dv_acc)

    @pl.loop(0, HALF, unroll=2)
    def forward(s):
        lane_s = lane_i[pl.ds(s, 1), :]
        col_s = col_i[pl.ds(s, 1), :]
        sides = []
        for y in range(2):
            lane = jnp.broadcast_to(lane_s[:, 128 * y : 128 * y + 128], (8, 128))
            col = jnp.broadcast_to(col_s[:, 128 * y : 128 * y + 128], (8, 128))
            masks = [col == c for c in range(9)]
            groups = []
            for g in range(FEAT // 8):
                acc = None
                for c in range(9):
                    value = jnp.take_along_axis(
                        pair[(c // 3) * 4 + y + c % 3, 8 * g : 8 * g + 8, :],
                        lane,
                        axis=1,
                        mode="promise_in_bounds",
                    )
                    acc = value if c == 0 else jnp.where(masks[c], value, acc)
                groups.append(acc)
            sides.append(jnp.concatenate(groups, axis=0))
        terms = jnp.concatenate(sides, axis=1)
        _, waves = basis(s)
        z = dot(w_r[...], small_stack(waves).astype(bf16)) + (self_t[...] + terms)
        sg = sigmoid(z)
        silu = z * sg
        env = row(ENV, s)
        act[s] = silu
        slope[s] = (sg + silu * (1.0 - sg)) * env
        both_t = dot(w_a[...], stacked(silu * env))
        tens[s] = both_t[:FEAT]
        mix0[s] = both_t[FEAT : 2 * FEAT]
        e_row[pl.ds(s, 1), :] = both_t[2 * FEAT : 2 * FEAT + 1]
        for k in range(9):
            part = both_t[:32] if k < 3 else both_t[32:64]
            v_acc[k] += part * row(k, s)

    def folded(x):
        return jnp.concatenate(
            [
                env_norm * (x[:, c : c + 128] + pltpu.roll(x[:, c : c + 128], 64, 1))
                for c in (0, 128)
            ],
            axis=1,
        )

    for k in range(9):
        v_acc[k] = folded(v_acc[k])
    col_w = jnp.concatenate([w_col[...], w_col[...]], axis=1)

    @pl.loop(0, HALF, unroll=2)
    def middle(s):
        t = tens[s]
        vec_in = v_acc[0] * row(0, s)
        for k in range(1, 3):
            vec_in += v_acc[k] * row(k, s)
        ten_in = v_acc[3] * row(3, s)
        for k in range(4, 9):
            ten_in += v_acc[k] * row(k, s)
        inner = jnp.concatenate([vec_in, ten_in], axis=0)
        mixture = mix0[s] + dot(w_b[...], stacked(t * inner))
        sg = sigmoid(mixture)
        silu = mixture * sg
        m_row[pl.ds(s, 1), :] = jnp.sum(col_w * silu, axis=0, keepdims=True)
        grad = (sg + silu * (1.0 - sg)) * row(ENV, s)
        pulled = dot(w_c[...], stacked(grad))
        resid[s] = pulled[:FEAT] + col_w
        dvt = pulled[FEAT:]
        back[s] = dvt * inner
        p = dvt * t
        prod[s] = p
        for k in range(9):
            part = p[:32] if k < 3 else p[32:]
            dv_acc[k] += part * row(k, s)

    for k in range(9):
        dv_acc[k] = folded(dv_acc[k])

    @pl.loop(0, HALF, unroll=2)
    def backward(s):
        t = tens[s]
        p = prod[s]
        dt = back[s]
        vec_part, ten_part = dt[:32], dt[32:]
        for k in range(9):
            half = slice(0, 32) if k < 3 else slice(32, 64)
            moved = dv_acc[k]
            if k < 3:
                vec_part += moved * row(k, s)
            else:
                ten_part += moved * row(k, s)
            du_row[k, pl.ds(s, 1), :] = jnp.sum(
                p[half] * v_acc[k] + t[half] * moved, axis=0, keepdims=True
            )
        dl = resid[s] + dot(w_d[...], stacked(jnp.concatenate([vec_part, ten_part], axis=0)))
        d_row[pl.ds(s, 1), :] = jnp.sum(dl * act[s], axis=0, keepdims=True)
        dwaves = dot(w_e[...], stacked(dl * slope[s]))[:8]
        x, waves = basis(s)
        dr_row[pl.ds(s, 1), :] = jnp.sum(dwaves * waves * x, axis=0, keepdims=True)

    env, m_sum = geo[ENV], m_row[...]
    values = jnp.sum(e_row[...] + env * m_sum, axis=0, keepdims=True)
    energy[...] = jnp.broadcast_to(fold_sides(values), energy.shape)
    u = [geo[U + d] for d in range(3)]
    du = [du_row[d] for d in range(3)]
    dq = [du_row[3 + k] for k in range(6)]
    cross = ((0, 1, 3), (0, 2, 4), (1, 2, 5))
    du = [du[d] + 2.0 * u[d] * dq[d] for d in range(3)]
    for a, b, k in cross:
        du[a] = du[a] + root2 * u[b] * dq[k]
        du[b] = du[b] + root2 * u[a] * dq[k]
    inv = geo[INV]
    along = du[0] * u[0] + du[1] * u[1] + du[2] * u[2]
    dr = dr_row[...] * (-2.0 / spacing) - along * inv
    ds = 2.0 * geo[DENV] * (d_row[...] + m_sum) + dr * inv
    zero = jnp.zeros((HALF, WIDE), f32)
    for d in range(3):
        g = du[d] * inv + geo[VEC + d] * ds
        hi, lo = halves(g)
        g_row[:, d, :] = hi.astype(f32)
        g_row[:, 3 + d, :] = lo.astype(f32)
        own = fold_sides(jnp.sum(g, axis=0, keepdims=True))
        own_sum[d : d + 1, :] = own
    g_row[:, 6, :] = zero
    g_row[:, 7, :] = zero

    s_acc[...] = jnp.zeros_like(s_acc)
    places = lax.broadcasted_iota(jnp.int32, (128, 128), 0)

    @pl.loop(0, HALF // 4)
    def scatter(q):
        for y in range(2):
            side = slice(128 * y, 128 * y + 128)
            left, right = [], []
            for i in range(4):
                s = 4 * q + i
                lane = lane_i[pl.ds(s, 1), :][:, side]
                col = jnp.broadcast_to(col_i[pl.ds(s, 1), :][:, side], (8, 128))
                tile = g_row[s, :, side]
                left.append(
                    jnp.concatenate(
                        [jnp.where(col == c, tile, 0.0) for c in range(9)], axis=0
                    ).astype(bf16)
                )
                right.append((places == lane).astype(f32).astype(bf16))
            s_acc[y] += lax.dot_general(
                jnp.concatenate(left, axis=1),
                jnp.concatenate(right, axis=1),
                (((1,), (1,)), ((), ())),
                preferred_element_type=f32,
            )

    out[...] = jnp.zeros_like(out)
    for y in range(2):
        for c in range(9):
            tile = s_acc[y, 8 * c : 8 * c + 8, :]
            out[c // 3, y + c % 3, 0:3, :] += tile[0:3] + tile[3:6]
        own = pltpu.roll(own_sum[:, 128 * y : 128 * y + 128], 32, 1)
        kept = jnp.where((lanes >= 32) & (lanes < 96), own, 0.0)
        out[1, 1 + y, 0:3, :] -= kept[0:3]


def fold_sides(x):
    return jnp.concatenate(
        [x[:, c : c + 128] + pltpu.roll(x[:, c : c + 128], 64, 1) for c in (0, 128)], axis=1
    )


def run_prepare(*weights):
    shapes = ((136, 192), (64, 192), (128, 192), (64, 192), (64, 32), (16, 192), (64, 192), (64, 192))
    outs = [jax.ShapeDtypeStruct(shape, bf16) for shape in shapes]
    outs.append(jax.ShapeDtypeStruct((FEAT, 128), f32))
    return pl.pallas_call(prepare, out_shape=outs)(*weights)


def run_layer(which, ghost, core, codes, limit, weights):
    big = pltpu.VMEM((HALF, FEAT, WIDE), f32)
    flat = pltpu.VMEM((HALF, WIDE), f32)
    index = pltpu.VMEM((HALF, WIDE), jnp.int32)
    sums = pltpu.VMEM((9, 32, WIDE), f32)
    scratch = [
        pltpu.VMEM((12, FEAT, 128), f32),
        pltpu.VMEM((FEAT, WIDE), f32),
        index,
        index,
        pltpu.VMEM((GEO, HALF, WIDE), f32),
        big,
        big,
        big,
        big,
        big,
        big,
        big,
        flat,
        flat,
        flat,
        pltpu.VMEM((9, HALF, WIDE), f32),
        flat,
        sums,
        sums,
        pltpu.VMEM((HALF, 8, WIDE), f32),
        pltpu.VMEM((2, 72, 128), f32),
        pltpu.VMEM((8, WIDE), f32),
    ]
    return pl.pallas_call(
        functools.partial(layer, which),
        out_shape=[
            jax.ShapeDtypeStruct((3, 4, 8, 128), f32),
            jax.ShapeDtypeStruct((8, WIDE), f32),
        ],
        scratch_shapes=scratch,
        compiler_params=pltpu.CompilerParams(vmem_limit_bytes=40 * 2**20),
    )(ghost, core, codes, limit, *weights)


def shifts(axis):
    size = lax.axis_size(axis)
    up = [(i, (i + 1) % size) for i in range(size)]
    return up, [(j, i) for i, j in up]


def exchange(low, high, axis, joined):
    up, down = shifts(axis)
    if lax.axis_size(axis) == 2:
        got = lax.ppermute(joined((high, low)), axis, up)
        size = got.shape[-1] // 2 if joined is last_joined else got.shape[1] // 2
        if joined is last_joined:
            return got[..., :size], got[..., size:]
        return got[:, :size], got[:, size:]
    return lax.ppermute(high, axis, up), lax.ppermute(low, axis, down)


def last_joined(parts):
    return jnp.concatenate(parts, axis=-1)


def second_joined(parts):
    return jnp.concatenate(parts, axis=1)


def local(
    positions,
    features,
    nbr_index,
    nbr_count,
    bin_counts,
    w_self,
    w_pair,
    w_radial,
    w_tensor,
    w_mix,
    w_out,
):
    cells_x, cells_y = nbr_count.shape[:2]
    cells_z = nbr_count.shape[2] // SLOTS
    lanes = cells_z * SLOTS
    weights = run_prepare(w_self, w_pair, w_radial, w_tensor, w_mix, w_out[None])

    x_index = lax.axis_index("gx")
    y_index = lax.axis_index("gy")
    z_index = lax.axis_index("gz")
    own_counts = lax.dynamic_slice(
        bin_counts,
        (x_index * cells_x, y_index * cells_y, z_index * cells_z),
        (cells_x, cells_y, cells_z),
    )
    slot = jnp.arange(lanes, dtype=jnp.int32) % SLOTS
    limit = jnp.where(slot < jnp.repeat(own_counts, SLOTS, axis=2), nbr_count, 0)
    limit = jnp.broadcast_to(limit[:, :, None, :], (cells_x, cells_y, 2, lanes))
    limit = limit.reshape(cells_x, 1, WIDE)
    codes = nbr_index.reshape(2, HALF, cells_x, cells_y, lanes)
    codes = codes.transpose(2, 1, 3, 0, 4).reshape(cells_x, HALF, WIDE)

    fill = jnp.zeros((ROWS - FEAT - 3,) + positions.shape[1:], f32)
    state = jnp.concatenate([features, positions, fill], axis=0).transpose(1, 2, 0, 3)
    below, above = exchange(state[..., :SLOTS], state[..., -SLOTS:], "gz", last_joined)
    state = jnp.concatenate([below, state, above], axis=-1)
    below, above = exchange(state[:, :1], state[:, -1:], "gy", second_joined)
    core = jnp.concatenate([below, state, above], axis=1)
    up, down = shifts("gx")
    under = lax.ppermute(core[-1], "gx", up)
    over = lax.ppermute(core[0], "gx", down)

    grad0, energy0 = run_layer(0, under, core, codes[0], limit[0], weights)
    back0 = lax.ppermute(grad0[0, :, :4], "gx", down)
    grad1, energy1 = run_layer(1, over, core, codes[1], limit[1], weights)
    back1 = lax.ppermute(grad1[2, :, :4], "gx", up)

    grad = jnp.stack(
        [grad0[1, :, :4] + grad1[0, :, :4] + back1, grad0[2, :, :4] + grad1[1, :, :4] + back0]
    )
    below, above = exchange(grad[:, :1], grad[:, -1:], "gy", second_joined)
    grad = grad[:, 1:-1] + jnp.concatenate([below, above], axis=1)
    below, above = exchange(grad[..., :SLOTS], grad[..., -SLOTS:], "gz", last_joined)
    grad = grad[..., SLOTS:-SLOTS] + jnp.concatenate([below, above], axis=-1)
    forces = -grad[:, :, :3].transpose(2, 0, 1, 3)
    energies = jnp.stack([energy0[0], energy1[0]]).reshape(cells_x, cells_y, 2, lanes)[:, :, 0]
    return forces, energies


def solution(mesh):
    return jax.shard_map(
        local,
        mesh=mesh,
        in_specs=(
            P(None, ("rep", "gx"), "gy", "gz"),
            P(None, ("rep", "gx"), "gy", "gz"),
            P(None, ("rep", "gx"), "gy", "gz"),
            P(("rep", "gx"), "gy", "gz"),
            P("rep", None, None),
            P(),
            P(),
            P(),
            P(),
            P(),
            P(),
        ),
        out_specs=(P(None, ("rep", "gx"), "gy", "gz"), P(("rep", "gx"), "gy", "gz")),
        check_vma=False,
    )
```

time: 532 us -> 79.2 us (0.15); the launches traced: 526 us -> 78.4 us
  local copies, waits for them, and re-layouts: 211 us -> 12.3 us
  matrix products: 173 us -> 0 us
  other arithmetic: 102 us -> 0.62 us
  Pallas kernels: 0 us -> 43.3 us
  waiting for transfers between devices: 16.6 us -> 8.18 us
    dot_general x49 -> x0, matrix products: 173 us -> none  [the longest x6 26.9 us: atom_energy(): jnp.einsum('cka,dka->cda', vec_weights, direction, precision=highest)]
    gather x20 -> x0, local copies, waits for them, and re-layouts: 112 us -> none  [the longest x4 49.8 us: one_block(): jnp.take(ext_pos, nbr_flat, axis=1).reshape(3, nbr_slots, block_rows)]
    scatter-add x6 -> x0, other arithmetic: 76.1 us -> none  [the longest x2 69.6 us: one_block(): position_part = gradient[:3].at[:, nbr_flat].add(pulled.reshape(3, -1))]
    pallas_call x0 -> x3, Pallas kernels: none -> 43.3 us  [the longest x2 41.5 us: run_layer(): pl.pallas_call(functools.partial(layer, which), out_shape=[jax.ShapeDtype...]
    dot_general x12 -> x0, local copies, waits for them, and re-layouts: 35.3 us -> none  [the longest x4 10.9 us: atom_energy(): jnp.einsum('cka,dka->cda', vec_weights, direction, precision=highest)]
    slice x21 -> x11, local copies, waits for them, and re-layouts: 22.8 us -> 0.96 us  [the longest x1 0.58 us: local(): jnp.stack([energy0[0], energy1[0]]).reshape(cells_x, cells_y, 2, lanes)]
    transpose x4 -> x0, local copies, waits for them, and re-layouts: 15.9 us -> none  [the longest x2 8.01 us: atom_energy(): jnp.einsum('cda,dka->cka', vec_sums, direction, precision=highest)]
    while x150 -> x0, local copies, waits for them, and re-layouts: 9.39 us -> none
  transfers between devices with their start and end apart: 12 -> 8, of which waited for: 10 -> 5; matrix products, arithmetic and copies ran while one was open for 1% -> 4% of each run, Pallas kernels for 0% -> 55%
where the time goes in v1:
time: 79.2 us; the launch traced here: 78.4 us
  Pallas kernels  43.3 us (55%)
  starting transfers between devices  13.1 us (17%)
  local copies, waits for them, and re-layouts  12.3 us (16%)
  waiting for transfers between devices  8.18 us (10%)
  between operations  0.82 us (1%)
    pallas_call x2, Pallas kernels, run_layer(): pl.pallas_call(functools.partial(layer, which), out_shape=[jax.ShapeDtype...  41.5 us
    unnamed x28, local copies, waits for them, and re-layouts  9.69 us
    ppermute x4, waiting for transfers between devices, exchange(): got = lax.ppermute(joined((high, low)), axis, up)  6.41 us
    ppermute x4, starting transfers between devices, exchange(): got = lax.ppermute(joined((high, low)), axis, up)  5.08 us
    ppermute x1, starting transfers between devices, local(): back0 = lax.ppermute(grad0[0, :, :4], 'gx', down)  4.05 us
    ppermute x1, starting transfers between devices, local(): over = lax.ppermute(core[0], 'gx', down)  3.9 us
    pallas_call x1, Pallas kernels, run_prepare(): return pl.pallas_call(prepare, out_shape=outs)(*weights)  1.87 us
  transfers between devices with their start and end apart: 8, of which 5 were waited for; matrix products, arithmetic and copies ran while one was open for 4% of the time, Pallas kernels for 55%

profile of v1, /device:TPU:0, one launch (start us, length us, event | category | flops | bytes accessed | tf_op | source)
XLA Modules:
  0.0 78.4 jit_solution(8997612276886374115)
XLA Ops:
  0.6 0.7 copy.14
  1.3 0.9 %copy.13 = f32[64,2,2,64]{3,0,2,1:T(8,128)S(1)} copy(f32[64,2,2,64]{3,2,1,0:T(2,128)} %param.12) | data formatting | bytes 131072 | tf_op args[1]
  2.6 0.5 collective-permute-start
  3.2 0.3 copy-done.9
  3.5 0.1 squeeze.30.codes
  3.6 0.8 dynamic_slice.3
  4.8 0.1 pad_maximum_fusion.2
  5.0 3.0 %collective-permute-start.1 = (f32[2,2,72,128]{3,2,1,0:T(8,128)S(1)}, f32[2,2,72,128]{3,2,1,0:T(8,128)S(1)}, u32[]{:S(2)}, u32[]{:S(2)}) collective-permute-start(f32[2,2,72,128]{3,2,1,0:T(8,128)S(1)} %pad_maximum_fusion.3), channel_id=1, source_target_pairs={{0,2},{2,0},{1,3},{3,1},{4,6},{6,4},{5,7},{7,5},{8,10},{10,8},{9,1... | collective-permute-start | bytes 442376 | tf_op jit(solution)/shard_map/ppermute | solution.py:426
  8.0 3.8 %collective-permute-done.1 = f32[2,2,72,128]{3,2,1,0:T(8,128)S(1)} collective-permute-done((f32[2,2,72,128]{3,2,1,0:T(8,128)S(1)}, f32[2,2,72,128]{3,2,1,0:T(8,128)S(1)}, u32[]{:S(2)}, u32[]{:S(2)}) %collective-permute-start.1) | collective-permute-done | bytes 147488 | tf_op jit(solution)/shard_map/ppermute | solution.py:426
  11.8 0.1 pad_maximum_fusion.core
  12.0 3.9 %collective-permute-start.3 = (f32[4,72,128]{2,1,0:T(8,128)S(1)}, f32[4,72,128]{2,1,0:T(8,128)S(1)}, u32[]{:S(2)}, u32[]{:S(2)}) collective-permute-start(f32[4,72,128]{2,1,0:T(8,128)S(1)} %get-tuple-element.30), channel_id=1, source_target_pairs={{4,0},{8,4},{12,8},{0,12},{5,1},{9,5},{13,9},{1,13},{6,2},{10,6},{... | collective-permute-start | bytes 442376 | tf_op jit(solution)/shard_map/ppermute | solution.py:483
  16.0 0.7 copy.17.w_mix
  16.9 1.9 %shard_map.122 = (bf16[136,192]{1,0:T(8,128)(2,1)}, bf16[64,192]{1,0:T(8,128)(2,1)}, bf16[128,192]{1,0:T(8,128)(2,1)}, bf16[64,192]{1,0:T(8,128)(2,1)}, bf16[64,...) custom-call(f32[64,64]{1,0:T(8,128)} %w_self.1, ...), custom_call_target="tpu_custom_call" | custom-call | tf_op jit(solution)/shard_map/pallas_call | solution.py:374
  18.9 0.4 collective-permute-done.3.ghost
  19.3 0.3 copy-done.7
  19.5 0.9 %copy-done = bf16[136,192]{1,0:T(8,128)(2,1)S(1)} copy-done((bf16[136,192]{1,0:T(8,128)(2,1)S(1)}, bf16[136,192]{1,0:T(8,128)(2,1)}, u32[]{:S(2)}) %copy-start) | copy-done | bytes 52248
  20.4 0.8 %copy-done.1 = bf16[128,192]{1,0:T(8,128)(2,1)S(1)} copy-done((bf16[128,192]{1,0:T(8,128)(2,1)S(1)}, bf16[128,192]{1,0:T(8,128)(2,1)}, u32[]{:S(2)}) %copy-start.1) | copy-done | bytes 49176
  21.3 0.8 copy-done.2
  22.0 0.8 copy-done.3
  22.8 0.8 copy-done.4
  23.5 0.8 copy-done.5
  24.3 0.8 copy-done.6
  25.0 0.7 copy-done.8
  25.7 20.7 %shard_map.124 = (f32[3,4,8,128]{3,2,1,0:T(8,128)S(1)}, f32[8,256]{1,0:T(8,128)S(1)}) custom-call(f32[4,72,128]{2,1,0:T(8,128)S(1)} %collective-permute-done.3.ghost, f32[2,4,72,128]{3,2,1,0:T(8,128)S(1)} %pad_maximum_fusion.core, s32[24,256]{1,0:T(8,128)S(1)} %squeeze.30.codes, s32[1,256]{1,0:T(1,128)S(1)} %broadcast_in_dim.33.limit, ...), custom_call_target="tpu_custom_call" | custom-call | tf_op jit(solution)/shard_map/pallas_call | solution.py:406
  46.5 20.7 %shard_map.123 = (f32[3,4,8,128]{3,2,1,0:T(8,128)S(1)}, f32[8,256]{1,0:T(8,128)S(1)}) custom-call(f32[4,72,128]{2,1,0:T(8,128)S(1)} %collective-permute-done.2.ghost, f32[2,4,72,128]{3,2,1,0:T(8,128)S(1)} %pad_maximum_fusion.core, s32[24,256]{1,0:T(8,128)S(1)} %squeeze.28.codes, s32[1,256]{1,0:T(1,128)S(1)} %broadcast_in_dim.30.limit, ...), custom_call_target="tpu_custom_call" | custom-call | tf_op jit(solution)/shard_map/pallas_call | solution.py:406
  67.3 4.0 %collective-permute-start.5 = (f32[4,4,128]{2,1,0:T(4,128)S(1)}, f32[4,4,128]{2,1,0:T(4,128)S(1)}, u32[]{:S(2)}, u32[]{:S(2)}) collective-permute-start(f32[4,4,128]{2,1,0:T(4,128)S(1)} %slice_bitcast_fusion.2), channel_id=1, source_target_pairs={{4,0},{8,4},{12,8},{0,12},{5,1},{9,5},{13,9},{1,13},{6,2},{10,6},{... | collective-permute-start | bytes 24584 | tf_op jit(solution)/shard_map/ppermute | solution.py:486
  71.3 1.4 %collective-permute-done.5 = f32[4,4,128]{2,1,0:T(4,128)S(1)} collective-permute-done((f32[4,4,128]{2,1,0:T(4,128)S(1)}, f32[4,4,128]{2,1,0:T(4,128)S(1)}, u32[]{:S(2)}, u32[]{:S(2)}) %collective-permute-start.5) | collective-permute-done | bytes 8224 | tf_op jit(solution)/shard_map/ppermute | solution.py:486
  72.7 1.6 %collective-permute-start.6 = (f32[2,2,4,128]{3,2,1,0:T(4,128)S(1)}, f32[2,2,4,128]{3,2,1,0:T(4,128)S(1)}, u32[]{:S(2)}, u32[]{:S(2)}) collective-permute-start(f32[2,2,4,128]{3,2,1,0:T(4,128)S(1)} %fusion.4), channel_id=1, source_target_pairs={{0,2},{2,0},{1,3},{3,1},{4,6},{6,4},{5,7},{7,5},{8,10},{10,8},{9,1... | collective-permute-start | bytes 24584 | tf_op jit(solution)/shard_map/ppermute | solution.py:426
  74.3 2.2 %collective-permute-done.6 = f32[2,2,4,128]{3,2,1,0:T(4,128)S(1)} collective-permute-done((f32[2,2,4,128]{3,2,1,0:T(4,128)S(1)}, f32[2,2,4,128]{3,2,1,0:T(4,128)S(1)}, u32[]{:S(2)}, u32[]{:S(2)}) %collective-permute-start.6) | collective-permute-done | bytes 8224 | tf_op jit(solution)/shard_map/ppermute | solution.py:426
  76.7 0.6 slice.161
  77.4 0.4 collective-permute-done.7
  77.8 0.6 copy.19
  (57 shorter events, 1.6 us)
Async XLA Ops:
  2.5 0.9 %copy-start.9 = (s32[48,2,2,64]{3,2,1,0:T(2,128)S(1)}, s32[48,2,2,64]{3,2,1,0:T(2,128)}, u32[]{:S(2)}) copy-start(s32[48,2,2,64]{3,2,1,0:T(2,128)} %param.13) | copy-start | bytes 147460
  2.6 2.0 %collective-permute-start = (f32[2,2,72,64]{3,2,1,0:T(8,128)S(1)}, f32[2,2,72,64]{3,2,1,0:T(8,128)S(1)}, u32[]{:S(2)}, u32[]{:S(2)}) collective-permute-start(f32[2,2,72,64]{3,2,1,0:T(8,128)S(1)} %pad_maximum_fusion.1), channel_id=1, source_target_pairs={{0,1},{1,0},{2,3},{3,2},{4,5},{5,4},{6,7},{7,6},{8,9},{9,8},{10,11... | collective-permute-start | bytes 221192 | tf_op jit(solution)/shard_map/ppermute | solution.py:426
  4.9 3.0 %copy-start.11 = (s32[2,2,64]{2,1,0:T(2,128)S(1)}, s32[2,2,64]{2,1,0:T(2,128)}, u32[]{:S(2)}) copy-start(s32[2,2,64]{2,1,0:T(2,128)} %param.14) | copy-start | bytes 3076
  5.0 6.9 %collective-permute-start.1 = (f32[2,2,72,128]{3,2,1,0:T(8,128)S(1)}, f32[2,2,72,128]{3,2,1,0:T(8,128)S(1)}, u32[]{:S(2)}, u32[]{:S(2)}) collective-permute-start(f32[2,2,72,128]{3,2,1,0:T(8,128)S(1)} %pad_maximum_fusion.3), channel_id=1, source_target_pairs={{0,2},{2,0},{1,3},{3,1},{4,6},{6,4},{5,7},{7,5},{8,10},{10,8},{9,1... | collective-permute-start | bytes 442376 | tf_op jit(solution)/shard_map/ppermute | solution.py:426
  12.0 4.0 %copy-start.10 = (f32[128,64]{0,1:T(8,128)S(1)}, f32[128,64]{0,1:T(8,128)}, u32[]{:S(2)}) copy-start(f32[128,64]{0,1:T(8,128)} %param.20) | copy-start | bytes 98308
  12.0 7.2 %collective-permute-start.3 = (f32[4,72,128]{2,1,0:T(8,128)S(1)}, f32[4,72,128]{2,1,0:T(8,128)S(1)}, u32[]{:S(2)}, u32[]{:S(2)}) collective-permute-start(f32[4,72,128]{2,1,0:T(8,128)S(1)} %get-tuple-element.30), channel_id=1, source_target_pairs={{4,0},{8,4},{12,8},{0,12},{5,1},{9,5},{13,9},{1,13},{6,2},{10,6},{... | collective-permute-start | bytes 442376 | tf_op jit(solution)/shard_map/ppermute | solution.py:483
  18.8 0.7 copy-start.7
  18.8 27.7 %collective-permute-start.2 = (f32[4,72,128]{2,1,0:T(8,128)S(1)}, f32[4,72,128]{2,1,0:T(8,128)S(1)}, u32[]{:S(2)}, u32[]{:S(2)}) collective-permute-start(f32[4,72,128]{2,1,0:T(8,128)S(1)} %get-tuple-element.31), channel_id=1, source_target_pairs={{0,4},{4,8},{8,12},{12,0},{1,5},{5,9},{9,13},{13,1},{2,6},{6,10},{... | collective-permute-start | bytes 442376 | tf_op jit(solution)/shard_map/ppermute | solution.py:482
  19.5 0.9 %copy-start = (bf16[136,192]{1,0:T(8,128)(2,1)S(1)}, bf16[136,192]{1,0:T(8,128)(2,1)}, u32[]{:S(2)}) copy-start(bf16[136,192]{1,0:T(8,128)(2,1)} %get-tuple-element.15.w_a) | copy-start | bytes 156676
  20.4 0.8 %copy-start.1 = (bf16[128,192]{1,0:T(8,128)(2,1)S(1)}, bf16[128,192]{1,0:T(8,128)(2,1)}, u32[]{:S(2)}) copy-start(bf16[128,192]{1,0:T(8,128)(2,1)} %get-tuple-element.17.w_c) | copy-start | bytes 147460
  21.3 0.8 copy-start.2
  22.0 0.8 copy-start.3
  22.8 0.8 copy-start.4
  23.5 0.8 copy-start.5
  24.3 0.8 copy-start.6
  25.0 0.7 copy-start.8
  46.5 24.8 %collective-permute-start.4 = (f32[4,4,128]{2,1,0:T(4,128)S(1)}, f32[4,4,128]{2,1,0:T(4,128)S(1)}, u32[]{:S(2)}, u32[]{:S(2)}) collective-permute-start(f32[4,4,128]{2,1,0:T(4,128)S(1)} %slice_bitcast_fusion.3), channel_id=1, source_target_pairs={{0,4},{4,8},{8,12},{12,0},{1,5},{5,9},{9,13},{13,1},{2,6},{6,10},{... | collective-permute-start | bytes 24584 | tf_op jit(solution)/shard_map/ppermute | solution.py:488
  67.3 5.4 %collective-permute-start.5 = (f32[4,4,128]{2,1,0:T(4,128)S(1)}, f32[4,4,128]{2,1,0:T(4,128)S(1)}, u32[]{:S(2)}, u32[]{:S(2)}) collective-permute-start(f32[4,4,128]{2,1,0:T(4,128)S(1)} %slice_bitcast_fusion.2), channel_id=1, source_target_pairs={{4,0},{8,4},{12,8},{0,12},{5,1},{9,5},{13,9},{1,13},{6,2},{10,6},{... | collective-permute-start | bytes 24584 | tf_op jit(solution)/shard_map/ppermute | solution.py:486
  72.7 3.7 %collective-permute-start.6 = (f32[2,2,4,128]{3,2,1,0:T(4,128)S(1)}, f32[2,2,4,128]{3,2,1,0:T(4,128)S(1)}, u32[]{:S(2)}, u32[]{:S(2)}) collective-permute-start(f32[2,2,4,128]{3,2,1,0:T(4,128)S(1)} %fusion.4), channel_id=1, source_target_pairs={{0,2},{2,0},{1,3},{3,1},{4,6},{6,4},{5,7},{7,5},{8,10},{10,8},{9,1... | collective-permute-start | bytes 24584 | tf_op jit(solution)/shard_map/ppermute | solution.py:426
  76.6 1.2 %collective-permute-start.7 = (f32[2,2,4,64]{3,2,1,0:T(4,128)S(1)}, f32[2,2,4,64]{3,2,1,0:T(4,128)S(1)}, u32[]{:S(2)}, u32[]{:S(2)}) collective-permute-start(f32[2,2,4,64]{3,2,1,0:T(4,128)S(1)} %pad_maximum_fusion.5), channel_id=1, source_target_pairs={{0,1},{1,0},{2,3},{3,2},{4,5},{5,4},{6,7},{7,6},{8,9},{9,8},{10,11... | collective-permute-start | bytes 12296 | tf_op jit(solution)/shard_map/ppermute | solution.py:426

commit v2 on v1

v2 whole, which is shorter than its diff:
```python
import functools

import jax
import jax.numpy as jnp
from jax import lax
from jax.experimental import pallas as pl
from jax.experimental.pallas import tpu as pltpu
from jax.sharding import PartitionSpec as P

SLOTS = 32
cell_side = 6.0
cutoff = 6.0
soften = 0.25
env_norm = 0.25
root2 = 2.0**0.5
f32 = jnp.float32
bf16 = jnp.bfloat16
HALF = 24
WIDE = 256
FEAT = 64
ROWS = 72
BASIS = 8
MIRRORED = 64
SPACING = cutoff / (BASIS - 1)
GROUP = 4
UNROLL = 1

U, Q, ENV, DIST, INV, VEC, DENV, GEO = 0, 3, 9, 10, 11, 12, 15, 16


def halves(x):
    hi = x.astype(bf16)
    return hi, (x - hi.astype(f32)).astype(bf16)


def stacked(x):
    hi, lo = halves(x)
    return jnp.concatenate([hi, lo, hi], axis=0)


def stacked_left(w):
    hi, lo = halves(w)
    return jnp.concatenate([hi, hi, lo], axis=1)


def dot(a, b):
    return jnp.dot(a, b, preferred_element_type=f32)


def small_stack(x):
    hi, lo = halves(x)
    hi, lo = hi.astype(f32), lo.astype(f32)
    return jnp.concatenate([hi, lo, hi, jnp.zeros_like(hi)], axis=0)


def sigmoid(x):
    return 0.5 + 0.5 * jnp.tanh(0.5 * x)


W_A, W_B, W_C, W_D, W_E, W_P, W_S, W_R, W_END = 0, 144, 208, 336, 400, 416, 480, 544, 608


def pipeline(stages, last=None):
    groups, depth = HALF // GROUP, len(stages)

    def step(t, first, stop):
        for k in range(stop - 1, first - 1, -1):
            start = (t - k) * GROUP
            for i in range(GROUP):
                stages[k](start + i, i)
            if k == depth - 1 and last is not None:
                last(start)

    for t in range(depth - 1):
        step(t, 0, t + 1)
    pl.loop(depth - 1, groups, unroll=UNROLL)(lambda t: step(t, 0, depth))
    for t in range(groups, groups + depth - 1):
        step(t, t - groups + 1, depth)


def basis(dist):
    level = lax.broadcasted_iota(jnp.int32, (BASIS, 1), 0).astype(f32)
    x = dist / SPACING - level
    return x, jnp.exp(-x * x)


def lane_row():
    return lax.broadcasted_iota(jnp.int32, (1, 128), 1)


def fold_sides(x):
    return jnp.concatenate(
        [x[:, c : c + 128] + pltpu.roll(x[:, c : c + 128], 64, 1) for c in (0, 128)], axis=1
    )


def prepare(w_self, w_pair, w_radial, w_tensor, mix_t, w_out, merged):
    tensor, mix, out_row = w_tensor[...], mix_t[...].T, w_out[...]
    parts = (
        jnp.concatenate(
            [tensor.T, mix_t[:, :FEAT], jnp.broadcast_to(out_row, (16, FEAT))], axis=0
        ),
        mix_t[:, FEAT:],
        mix * out_row,
        tensor,
        jnp.concatenate([w_radial[...], jnp.zeros_like(w_radial)], axis=0),
        w_pair[...].T,
        w_self[...].T,
    )
    for first, part in zip((W_A, W_B, W_C, W_D, W_E, W_P, W_S), parts):
        merged[first : first + part.shape[0], :] = stacked_left(part)
    hi, lo = halves(w_radial[...])
    hi, lo = hi.astype(f32), lo.astype(f32)
    rows = jnp.concatenate([hi, hi, lo, jnp.zeros((168, FEAT), f32)], axis=0)
    merged[W_R:W_END, :] = rows.T.astype(bf16)


def front(
    which,
    ghost_own,
    ghost_sides,
    core_own,
    core_sides,
    codes,
    limit,
    merged,
    act,
    slope,
    tens,
    mix0,
    v_acc,
    e_row,
    geo,
    lane_i,
    col_i,
    pair,
    self_t,
    step_a,
    step_b,
):
    w_a = merged.at[W_A:W_B]
    w_p, w_s = merged.at[W_P:W_S], merged.at[W_S:W_R]
    w_r = merged.at[W_R:W_END, 0 : 4 * BASIS]

    def source(dx, yc):
        here = yc - 1 if yc in (1, 2) else yc // 3
        own, sides = (ghost_own, ghost_sides), (core_own, core_sides)
        if dx == (0 if which == 0 else 2):
            return own[yc in (0, 3)].at[here]
        return sides[yc in (0, 3)].at[dx - 1 + which, here]

    lanes = lane_row()

    def both(x):
        return jnp.where(lanes < 64, pltpu.roll(x, 96, 1), pltpu.roll(x, 32, 1))

    for dx in range(3):
        rows = jnp.concatenate([source(dx, yc)[:FEAT, :] for yc in range(4)], axis=1)
        terms = dot(w_p[...], stacked(rows))
        for yc in range(4):
            pair[dx * 4 + yc] = terms[:, 128 * yc : 128 * yc + 128]
    rows = jnp.concatenate([source(1, 1 + y)[:FEAT, :] for y in range(2)], axis=1)
    terms = dot(w_s[...], stacked(rows))
    for y in range(2):
        self_t[:, 128 * y : 128 * y + 128] = both(terms[:, 128 * y : 128 * y + 128])

    code = codes[...]
    offset = code >> 5
    plane = (offset * 43) >> 7
    dz = offset - 3 * plane
    dx = (offset * 57) >> 9
    dy = plane - 3 * dx
    limits = limit[...]
    mirrored = jnp.where(limits >= MIRRORED, 2 - dx, dx)
    lane256 = lax.broadcasted_iota(jnp.int32, (HALF, WIDE), 1)
    z_own = (lane256 >> 5) & 1
    lane_i[...] = ((z_own + dz) << 5) + (code & 31)
    col_i[...] = 3 * mirrored + dy
    rank = lax.broadcasted_iota(jnp.int32, (HALF, WIDE), 0) + HALF * ((lane256 >> 6) & 1)
    mask = (rank < (limits & (MIRRORED - 1))).astype(f32)

    steps = (dx, dy, dz)
    vec = []
    for d in range(3):
        found = []
        for y in range(2):
            own = both(source(1, 1 + y)[FEAT + d : FEAT + d + 1, :])
            parts = []
            for j in range(HALF // 8):
                where = (slice(8 * j, 8 * j + 8), slice(128 * y, 128 * y + 128))
                lane, col = lane_i[where], col_i[where]
                acc = None
                for c in range(9):
                    row = source(c // 3, y + c % 3)[FEAT + d : FEAT + d + 1, :]
                    value = jnp.take_along_axis(
                        jnp.broadcast_to(row, (8, 128)), lane, axis=1, mode="promise_in_bounds"
                    )
                    acc = value if c == 0 else jnp.where(col == c, value, acc)
                parts.append(acc)
            found.append(jnp.concatenate(parts, axis=0) - own)
        vec.append(
            jnp.concatenate(found, axis=1) + cell_side * (steps[d] - 1).astype(f32)
        )
    squared = vec[0] * vec[0] + vec[1] * vec[1] + vec[2] * vec[2] + soften
    dist = jnp.sqrt(squared)
    inv = 1.0 / dist
    u = [v * inv for v in vec]
    taper = jnp.maximum(1.0 - squared / (cutoff * cutoff), 0.0)
    for d in range(3):
        geo[U + d] = u[d]
        geo[VEC + d] = vec[d]
        geo[Q + d] = u[d] * u[d] - 1.0 / 3.0
    geo[Q + 3] = root2 * u[0] * u[1]
    geo[Q + 4] = root2 * u[0] * u[2]
    geo[Q + 5] = root2 * u[1] * u[2]
    geo[ENV] = taper * taper * mask
    geo[DENV] = taper * mask * (-2.0 / (cutoff * cutoff))
    geo[DIST] = dist
    geo[INV] = inv

    def row(k, s):
        return geo[k, pl.ds(s, 1), :]

    v_acc[...] = jnp.zeros_like(v_acc)

    def gathered(s):
        lane_s = lane_i[pl.ds(s, 1), :]
        col_s = col_i[pl.ds(s, 1), :]
        sides = []
        for y in range(2):
            lane = jnp.broadcast_to(lane_s[:, 128 * y : 128 * y + 128], (8, 128))
            col = jnp.broadcast_to(col_s[:, 128 * y : 128 * y + 128], (8, 128))
            masks = [col == c for c in range(9)]
            groups = []
            for g in range(FEAT // 8):
                acc = None
                for c in range(9):
                    value = jnp.take_along_axis(
                        pair[(c // 3) * 4 + y + c % 3, 8 * g : 8 * g + 8, :],
                        lane,
                        axis=1,
                        mode="promise_in_bounds",
                    )
                    acc = value if c == 0 else jnp.where(masks[c], value, acc)
                groups.append(acc)
            sides.append(jnp.concatenate(groups, axis=0))
        return jnp.concatenate(sides, axis=1)

    def forward_a(s, i):
        _, waves = basis(row(DIST, s))
        step_a[i] = dot(w_r[...], small_stack(waves).astype(bf16)) + (self_t[...] + gathered(s))

    def forward_b(s, i):
        z = step_a[i]
        sg = sigmoid(z)
        silu = z * sg
        env = row(ENV, s)
        act[s] = silu
        slope[s] = (sg + silu * (1.0 - sg)) * env
        step_b[i] = dot(w_a[...], stacked(silu * env))

    def forward_c(s, i):
        both_t = step_b[i]
        tens[s] = both_t[:FEAT]
        mix0[s] = both_t[FEAT : 2 * FEAT]
        e_row[pl.ds(s, 1), :] = both_t[2 * FEAT : 2 * FEAT + 1]

    def forward_sum(first):
        for k in range(9):
            part = slice(0, 32) if k < 3 else slice(32, 64)
            total = v_acc[k]
            for i in range(GROUP):
                total += step_b[i, part] * row(k, first + i)
            v_acc[k] = total

    pipeline((forward_a, forward_b, forward_c), forward_sum)

    for k in range(9):
        v_acc[k] = env_norm * fold_sides(v_acc[k])


def rear(
    merged,
    out_row,
    added,
    act,
    slope,
    tens,
    mix0,
    v_acc,
    e_row,
    geo,
    lane_i,
    col_i,
    out,
    energy,
    step_a,
    step_b,
    step_c,
    prod,
    back,
    resid,
    m_row,
    d_row,
    du_row,
    dr_row,
    dv_acc,
    g_row,
    s_acc,
    own_sum,
):
    w_b, w_c = merged.at[W_B:W_C], merged.at[W_C:W_D]
    w_d, w_e = merged.at[W_D:W_E], merged.at[W_E:W_P]
    lanes = lane_row()

    def row(k, s):
        return geo[k, pl.ds(s, 1), :]

    dv_acc[...] = jnp.zeros_like(dv_acc)
    col_w = jnp.broadcast_to(out_row[...], (128, FEAT)).T
    col_w = jnp.concatenate([col_w, col_w], axis=1)

    def middle_a(s, i):
        vec_in = v_acc[0] * row(0, s)
        for k in range(1, 3):
            vec_in += v_acc[k] * row(k, s)
        ten_in = v_acc[3] * row(3, s)
        for k in range(4, 9):
            ten_in += v_acc[k] * row(k, s)
        inner = jnp.concatenate([vec_in, ten_in], axis=0)
        back[s] = inner
        step_a[i] = mix0[s] + dot(w_b[...], stacked(tens[s] * inner))

    def middle_b(s, i):
        mixture = step_a[i]
        sg = sigmoid(mixture)
        silu = mixture * sg
        m_row[pl.ds(s, 1), :] = jnp.sum(col_w * silu, axis=0, keepdims=True)
        grad = (sg + silu * (1.0 - sg)) * row(ENV, s)
        step_b[i, : 2 * FEAT] = dot(w_c[...], stacked(grad))

    def middle_c(s, i):
        resid[s] = step_b[i, :FEAT] + col_w
        dvt = step_b[i, FEAT : 2 * FEAT]
        back[s] = dvt * back[s]
        p = dvt * tens[s]
        prod[s] = p
        step_c[i] = p

    def middle_sum(first):
        for k in range(9):
            part = slice(0, 32) if k < 3 else slice(32, 64)
            total = dv_acc[k]
            for i in range(GROUP):
                total += step_c[i, part] * row(k, first + i)
            dv_acc[k] = total

    pipeline((middle_a, middle_b, middle_c), middle_sum)

    for k in range(9):
        dv_acc[k] = env_norm * fold_sides(dv_acc[k])

    def backward_a(s, i):
        t = tens[s]
        p = prod[s]
        dt = back[s]
        vec_part, ten_part = dt[:32], dt[32:]
        for k in range(9):
            half = slice(0, 32) if k < 3 else slice(32, 64)
            moved = dv_acc[k]
            if k < 3:
                vec_part += moved * row(k, s)
            else:
                ten_part += moved * row(k, s)
            du_row[k, pl.ds(s, 1), :] = jnp.sum(
                p[half] * v_acc[k] + t[half] * moved, axis=0, keepdims=True
            )
        step_a[i] = resid[s] + dot(
            w_d[...], stacked(jnp.concatenate([vec_part, ten_part], axis=0))
        )

    def backward_b(s, i):
        dl = step_a[i]
        d_row[pl.ds(s, 1), :] = jnp.sum(dl * act[s], axis=0, keepdims=True)
        step_b[i, :16] = dot(w_e[...], stacked(dl * slope[s]))

    def backward_c(s, i):
        x, waves = basis(row(DIST, s))
        dr_row[pl.ds(s, 1), :] = jnp.sum(step_b[i, :8] * waves * x, axis=0, keepdims=True)

    pipeline((backward_a, backward_b, backward_c))

    env, m_sum = geo[ENV], m_row[...]
    values = jnp.sum(e_row[...] + env * m_sum, axis=0, keepdims=True)
    energy[...] = jnp.broadcast_to(fold_sides(values), energy.shape)
    u = [geo[U + d] for d in range(3)]
    du = [du_row[d] for d in range(3)]
    dq = [du_row[3 + k] for k in range(6)]
    cross = ((0, 1, 3), (0, 2, 4), (1, 2, 5))
    du = [du[d] + 2.0 * u[d] * dq[d] for d in range(3)]
    for a, b, k in cross:
        du[a] = du[a] + root2 * u[b] * dq[k]
        du[b] = du[b] + root2 * u[a] * dq[k]
    inv = geo[INV]
    along = du[0] * u[0] + du[1] * u[1] + du[2] * u[2]
    dr = dr_row[...] * (-2.0 / SPACING) - along * inv
    ds = 2.0 * geo[DENV] * (d_row[...] + m_sum) + dr * inv
    zero = jnp.zeros((HALF, WIDE), f32)
    for d in range(3):
        g = du[d] * inv + geo[VEC + d] * ds
        hi, lo = halves(g)
        g_row[:, d, :] = hi.astype(f32)
        g_row[:, 3 + d, :] = lo.astype(f32)
        own = fold_sides(jnp.sum(g, axis=0, keepdims=True))
        own_sum[d : d + 1, :] = own
    g_row[:, 6, :] = zero
    g_row[:, 7, :] = zero

    s_acc[...] = jnp.zeros_like(s_acc)
    places = lax.broadcasted_iota(jnp.int32, (128, 128), 0)

    @pl.loop(0, HALF // 4, unroll=3)
    def scatter(q):
        for y in range(2):
            side = slice(128 * y, 128 * y + 128)
            left, right = [], []
            for i in range(4):
                s = 4 * q + i
                lane = lane_i[pl.ds(s, 1), :][:, side]
                col = jnp.broadcast_to(col_i[pl.ds(s, 1), :][:, side], (8, 128))
                tile = g_row[s, :, side]
                left.append(
                    jnp.concatenate(
                        [jnp.where(col == c, tile, 0.0) for c in range(9)], axis=0
                    ).astype(bf16)
                )
                right.append((places == lane).astype(f32).astype(bf16))
            s_acc[y] += lax.dot_general(
                jnp.concatenate(left, axis=1),
                jnp.concatenate(right, axis=1),
                (((1,), (1,)), ((), ())),
                preferred_element_type=f32,
            )

    if added is None:
        out[...] = jnp.zeros_like(out)
    else:
        out[0:2] = added[1:3]
        out[2] = jnp.zeros_like(out[2])
    for y in range(2):
        for c in range(9):
            tile = s_acc[y, 8 * c : 8 * c + 8, :]
            out[c // 3, y + c % 3, 0:3, :] += tile[0:3] + tile[3:6]
        own = pltpu.roll(own_sum[:, 128 * y : 128 * y + 128], 32, 1)
        kept = jnp.where((lanes >= 32) & (lanes < 96), own, 0.0)
        out[1, 1 + y, 0:3, :] -= kept[0:3]


def whole(which, *refs):
    given, out, rest = refs[:7], refs[8:10], refs[10:]
    kept, rest = rest[:9], rest[9:]
    steps, rest = rest[:3], rest[3:]
    front(which, *given, *kept, *rest[:2], *steps[:2])
    rear(refs[6], refs[7], None, *kept, *out, *steps, *rest[2:])


def run_prepare(*weights):
    return pl.pallas_call(
        prepare, out_shape=jax.ShapeDtypeStruct((W_END, 3 * FEAT), bf16)
    )(*weights)


BIG = (HALF, FEAT, WIDE)
FLAT = (HALF, WIDE)
SUMS = (9, 32, WIDE)
KEPT = (
    (BIG, f32),
    (BIG, f32),
    (BIG, f32),
    (BIG, f32),
    (SUMS, f32),
    (FLAT, f32),
    ((GEO, HALF, WIDE), f32),
    (FLAT, jnp.int32),
    (FLAT, jnp.int32),
)
STEPS = ((GROUP, FEAT, WIDE), (GROUP, 2 * FEAT + 16, WIDE), (GROUP, FEAT, WIDE))
FRONT = ((12, FEAT, 128), (FEAT, WIDE))
REAR = (BIG, BIG, BIG, FLAT, FLAT, SUMS[:1] + FLAT, FLAT, SUMS)
REAR = REAR + ((HALF, 8, WIDE), (2, 72, 128), (8, WIDE))
RESULT = (
    jax.ShapeDtypeStruct((3, 4, 8, 128), f32),
    jax.ShapeDtypeStruct((8, WIDE), f32),
)


def in_vmem(shapes):
    return [pltpu.VMEM(shape, f32) for shape in shapes]


def call(kernel, out_shape, scratch, micros):
    return pl.pallas_call(
        kernel,
        out_shape=out_shape,
        scratch_shapes=scratch,
        compiler_params=pltpu.CompilerParams(vmem_limit_bytes=40 * 2**20),
        cost_estimate=pl.CostEstimate(
            flops=micros * 1_000_000_000, bytes_accessed=2_000_000, transcendentals=2_000_000
        ),
    )


def run_front(which, *given):
    shapes = [jax.ShapeDtypeStruct(shape, dtype) for shape, dtype in KEPT]
    scratch = in_vmem(FRONT + STEPS[:2])
    return call(functools.partial(front, which), shapes, scratch, 5)(*given)


def run_rear(merged, out_row, added, kept):
    return call(rear, RESULT, in_vmem(STEPS + REAR), 20)(merged, out_row, added, *kept)


def run_whole(which, *given):
    scratch = [pltpu.VMEM(shape, dtype) for shape, dtype in KEPT]
    scratch = scratch + in_vmem(STEPS + FRONT + REAR)
    return call(functools.partial(whole, which), RESULT, scratch, 12)(*given)


def shifts(axis):
    size = lax.axis_size(axis)
    up = [(i, (i + 1) % size) for i in range(size)]
    return up, [(j, i) for i, j in up]


def exchange(low, high, axis, dim):
    up, down = shifts(axis)
    if lax.axis_size(axis) == 2:
        return lax.ppermute(jnp.concatenate([high, low], axis=dim), axis, up)
    parts = [lax.ppermute(high, axis, up), lax.ppermute(low, axis, down)]
    return jnp.concatenate(parts, axis=dim)


def local(
    positions,
    features,
    nbr_index,
    nbr_count,
    bin_counts,
    w_self,
    w_pair,
    w_radial,
    w_tensor,
    w_mix,
    w_out,
):
    cells_x, cells_y = nbr_count.shape[:2]
    cells_z = nbr_count.shape[2] // SLOTS
    lanes = cells_z * SLOTS
    x_index = lax.axis_index("gx")
    y_index = lax.axis_index("gy")
    z_index = lax.axis_index("gz")
    odd = x_index % 2 == 1

    def mirrored(x):
        return jnp.where(odd, x[::-1], x)

    fill = jnp.zeros((ROWS - FEAT - 3,) + positions.shape[1:], f32)
    state = jnp.concatenate([features, positions, fill], axis=0).transpose(1, 2, 0, 3)
    state = mirrored(state)
    ends = exchange(state[..., :SLOTS], state[..., -SLOTS:], "gz", 3)
    own_counts = lax.dynamic_slice(
        bin_counts,
        (x_index * cells_x, y_index * cells_y, z_index * cells_z),
        (cells_x, cells_y, cells_z),
    )
    slot = jnp.arange(lanes, dtype=jnp.int32) % SLOTS
    limit = jnp.where(slot < jnp.repeat(own_counts, SLOTS, axis=2), nbr_count, 0)
    limit = mirrored(limit) + MIRRORED * odd.astype(jnp.int32)
    limit = jnp.broadcast_to(limit[:, :, None, :], (cells_x, cells_y, 2, lanes))
    limit = limit.reshape(cells_x, 1, WIDE)
    ends, nbr_index, w_self = lax.optimization_barrier((ends, nbr_index, w_self))
    state = jnp.concatenate([ends[..., :SLOTS], state, ends[..., SLOTS:]], axis=-1)

    size = lax.axis_size("gx")
    first = [(i, i + 1 - 2 * (i % 2)) for i in range(size)]
    second = [(i, (i - 1 + 2 * (i % 2)) % size) for i in range(size)]
    sides = exchange(state[:, :1], state[:, -1:], "gy", 1)
    out_row = w_out[None]
    merged = run_prepare(w_self, w_pair, w_radial, w_tensor, w_mix.T, out_row)
    codes = nbr_index.reshape(2, HALF, cells_x, cells_y, lanes)
    codes = mirrored(codes.transpose(2, 1, 3, 0, 4).reshape(cells_x, HALF, WIDE))
    inner_own, outer_own, codes = lax.optimization_barrier((state[1], state[:1], codes))
    inner_own = lax.ppermute(inner_own, "gx", first)
    outer_own = lax.ppermute(outer_own, "gx", second)
    sides, merged, codes, limit = lax.optimization_barrier((sides, merged, codes, limit))
    inner_sides = lax.ppermute(sides[1], "gx", first)
    outer_own, late_sides = lax.optimization_barrier((outer_own, sides))
    outer_sides = exchange(outer_own[:, :1], outer_own[:, -1:], "gy", 1)[0]

    kept = run_front(1, inner_own, inner_sides, state, sides, codes[1], limit[1], merged)
    late_sides, kept = lax.optimization_barrier((late_sides, kept))
    grad0, energy0 = run_whole(
        0, outer_own[0], outer_sides, state, late_sides, codes[0], limit[0], merged, out_row
    )
    back0 = lax.ppermute(grad0[0, :, :4], "gx", second)
    grad1, energy1 = run_rear(merged, out_row, grad0, kept)
    grad1, back0 = lax.optimization_barrier((grad1, back0))
    back1 = lax.ppermute(grad1[2, :, :4], "gx", first)

    grad = grad1[:2, :, :4] + jnp.stack([back0, back1])
    grad = grad[:, 1:-1] + exchange(grad[:, :1], grad[:, -1:], "gy", 1)
    grad = grad[..., SLOTS:-SLOTS] + exchange(grad[..., :SLOTS], grad[..., -SLOTS:], "gz", 3)
    forces = -mirrored(grad)[:, :, :3].transpose(2, 0, 1, 3)
    energies = mirrored(jnp.stack([energy0[0], energy1[0]]))
    energies = energies.reshape(cells_x, cells_y, 2, lanes)[:, :, 0]
    return forces, energies


def solution(mesh):
    return jax.shard_map(
        local,
        mesh=mesh,
        in_specs=(
            P(None, ("rep", "gx"), "gy", "gz"),
            P(None, ("rep", "gx"), "gy", "gz"),
            P(None, ("rep", "gx"), "gy", "gz"),
            P(("rep", "gx"), "gy", "gz"),
            P("rep", None, None),
            P(),
            P(),
            P(),
            P(),
            P(),
            P(),
        ),
        out_specs=(P(None, ("rep", "gx"), "gy", "gz"), P(("rep", "gx"), "gy", "gz")),
        check_vma=False,
    )
```

time: 79.2 us -> 57.3 us (0.72)
  Pallas kernels: 43.3 us -> 28 us
  local copies, waits for them, and re-layouts: 12.3 us -> 5.67 us
  waiting for transfers between devices: 8.18 us -> 9.22 us
    pallas_call x3 -> x4, Pallas kernels: 43.3 us -> 28 us  [the longest x1 12.9 us: run_whole(): return call(functools.partial(whole, which), RESULT, scratch, 12)(*given)]
    unnamed x28 -> x13, local copies, waits for them, and re-layouts: 9.69 us -> 3.2 us
    ppermute x8 -> x10, waiting for transfers between devices: 8.18 us -> 9.22 us  [the longest x1 3.62 us: local(): back1 = lax.ppermute(grad1[2, :, :4], 'gx', first)]
    ppermute x8 -> x10, starting transfers between devices: 13.1 us -> 12.6 us  [the longest x5 5.46 us: exchange(): return lax.ppermute(jnp.concatenate([high, low], axis=dim), axis, up)]
  transfers between devices with their start and end apart: 8 -> 10, of which waited for: 5 -> 5; matrix products, arithmetic and copies ran while one was open for 4% -> 3% of each run, Pallas kernels for 55% -> 26%
where the time goes in v2:
time: 57.3 us; the launch traced here: 57 us
  Pallas kernels  28 us (49%)
  starting transfers between devices  12.6 us (22%)
  waiting for transfers between devices  9.22 us (16%)
  local copies, waits for them, and re-layouts  5.67 us (10%)
  between operations  0.87 us (2%)
  other arithmetic  0.59 us (1%)
    pallas_call x1, Pallas kernels, run_whole(): return call(functools.partial(whole, which), RESULT, scratch, 12)(*given)  12.9 us
    pallas_call x1, Pallas kernels, run_rear(): call(rear, RESULT, in_vmem(STEPS + REAR), 20)(merged, out_row, added, *kept)  7.78 us
    pallas_call x1, Pallas kernels, run_front(): return call(functools.partial(front, which), shapes, scratch, 5)(*given)  5.52 us
    ppermute x5, starting transfers between devices, exchange(): return lax.ppermute(jnp.concatenate([high, low], axis=dim), axis, up)  5.46 us
    ppermute x1, waiting for transfers between devices, local(): back1 = lax.ppermute(grad1[2, :, :4], 'gx', first)  3.62 us
    unnamed x13, local copies, waits for them, and re-layouts  3.2 us
    ppermute x5, waiting for transfers between devices, exchange(): return lax.ppermute(jnp.concatenate([high, low], axis=dim), axis, up)  2.56 us
    ppermute x1, starting transfers between devices, local(): outer_own = lax.ppermute(outer_own, 'gx', second)  2.47 us
  transfers between devices with their start and end apart: 10, of which 5 were waited for; matrix products, arithmetic and copies ran while one was open for 3% of the time, Pallas kernels for 26%

profile of v2, /device:TPU:0, one launch (start us, length us, event | category | flops | bytes accessed | tf_op | source)
XLA Modules:
  0.0 57.0 jit_solution(16635156695074769726)
XLA Ops:
  0.7 0.9 %copy.13 = f32[64,2,2,64]{3,0,2,1:T(8,128)S(1)} copy(f32[64,2,2,64]{3,2,1,0:T(2,128)} %param.12) | data formatting | bytes 131072 | tf_op args[1]
  1.6 0.7 %copy.14 = f32[3,2,2,64]{3,0,2,1:T(4,128)S(1)} copy(f32[3,2,2,64]{3,2,1,0:T(2,128)} %param.11) | data formatting | bytes 6144 | tf_op args[0]
  2.3 0.1 maximum_bitcast_fusion
  2.5 0.1 fusion.6
  2.6 0.1 pad_maximum_fusion
  2.7 0.5 collective-permute-start
  3.2 0.8 %dynamic_slice.3 = s32[2,2,2]{0,2,1:T(2,128)S(1)} dynamic-slice(s32[8,4,4]{0,2,1:T(4,128)} %param.15, s32[]{:T(128)S(6)} %select_n.78, s32[]{:T(128)S(6)} %select_n.79, s32[]{:T(128)S(6)} %select_n.80), dynamic_slice_sizes={2,2,2} | dynamic-slice | bytes 68 | tf_op jit(solution)/shard_map/dynamic_slice | solution.py:571
  4.0 0.1 copy.16
  4.1 0.1 reshape.31
  4.3 0.1 reshape.32
  4.3 0.1 fusion.5
  4.4 0.1 pad_maximum_fusion.1.core_own.refs_2_
  4.7 0.1 reshape.30
  4.9 2.8 %collective-permute-start.1 = (f32[2,2,72,128]{3,2,1,0:T(8,128)S(1)}, f32[2,2,72,128]{3,2,1,0:T(8,128)S(1)}, u32[]{:S(2)}, u32[]{:S(2)}) collective-permute-start(f32[2,2,72,128]{3,2,1,0:T(8,128)S(1)} %pad_maximum_fusion.2), channel_id=1, source_target_pairs={{0,2},{2,0},{1,3},{3,1},{4,6},{6,4},{5,7},{7,5},{8,10},{10,8},{9,1... | collective-permute-start | bytes 442376 | tf_op jit(solution)/shard_map/ppermute | solution.py:538
  7.7 1.6 %collective-permute-start.4 = (f32[2,72,128]{2,1,0:T(8,128)S(1)}, f32[2,72,128]{2,1,0:T(8,128)S(1)}, u32[]{:S(2)}, u32[]{:S(2)}) collective-permute-start(f32[2,72,128]{2,1,0:T(8,128)S(1)} %get-tuple-element.48), channel_id=1, source_target_pairs={{0,4},{4,0},{8,12},{12,8},{1,5},{5,1},{9,13},{13,9},{2,6},{6,2},{1... | collective-permute-start | bytes 221192 | tf_op jit(solution)/shard_map/ppermute | solution.py:593
  9.3 2.5 %collective-permute-start.2 = (f32[1,2,72,128]{3,2,1,0:T(8,128)S(1)}, f32[1,2,72,128]{3,2,1,0:T(8,128)S(1)}, u32[]{:S(2)}, u32[]{:S(2)}) collective-permute-start(f32[1,2,72,128]{3,2,1,0:T(8,128)S(1)} %get-tuple-element.44), channel_id=1, source_target_pairs={{0,12},{4,8},{8,4},{12,0},{1,13},{5,9},{9,5},{13,1},{2,14},{6,10},... | collective-permute-start | bytes 221192 | tf_op jit(solution)/shard_map/ppermute | solution.py:594
  11.7 1.8 %shard_map.122.merged.refs_6_ = bf16[608,192]{1,0:T(8,128)(2,1)} custom-call(f32[64,64]{1,0:T(8,128)} %w_self, f32[64,64]{1,0:T(8,128)} %w_pair.1, f32[8,64]{1,0:T(8,128)} %w_radial.1, f32[64,64]{1,0:T(8,128)} %w_tensor.1, f32[64,128]{1,0:T(8,128)} %bitcast.40, f32[1,64]{1,0:T(1,128)} %bitcast.34), custom_call_target="tpu_custom_call" | custom-call | tf_op jit(solution)/shard_map/pallas_call | solution.py:468
  13.5 0.7 %collective-permute-start.5 = (f32[2,72,128]{2,1,0:T(8,128)S(1)}, f32[2,72,128]{2,1,0:T(8,128)S(1)}, u32[]{:S(2)}, u32[]{:S(2)}) collective-permute-start(f32[2,72,128]{2,1,0:T(8,128)S(1)} %slice_bitcast_fusion.1), channel_id=1, source_target_pairs={{0,4},{4,0},{8,12},{12,8},{1,5},{5,1},{9,13},{13,9},{2,6},{6,2},{1... | collective-permute-start | bytes 221192 | tf_op jit(solution)/shard_map/ppermute | solution.py:596
  14.3 1.5 %collective-permute-done.2 = f32[1,2,72,128]{3,2,1,0:T(8,128)S(1)} collective-permute-done((f32[1,2,72,128]{3,2,1,0:T(8,128)S(1)}, f32[1,2,72,128]{3,2,1,0:T(8,128)S(1)}, u32[]{:S(2)}, u32[]{:S(2)}) %collective-permute-start.2) | collective-permute-done | bytes 73760 | tf_op jit(solution)/shard_map/ppermute | solution.py:594
  15.8 0.6 %collective-permute-start.3 = (f32[1,2,72,128]{3,2,1,0:T(8,128)S(1)}, f32[1,2,72,128]{3,2,1,0:T(8,128)S(1)}, u32[]{:S(2)}, u32[]{:S(2)}) collective-permute-start(f32[1,2,72,128]{3,2,1,0:T(8,128)S(1)} %pad_maximum_fusion.3), channel_id=1, source_target_pairs={{0,2},{2,0},{1,3},{3,1},{4,6},{6,4},{5,7},{7,5},{8,10},{10,8},{9,1... | collective-permute-start | bytes 221192 | tf_op jit(solution)/shard_map/ppermute | solution.py:538
  16.4 1.6 %collective-permute-done.5.ghost_sides = f32[2,72,128]{2,1,0:T(8,128)S(1)} collective-permute-done((f32[2,72,128]{2,1,0:T(8,128)S(1)}, f32[2,72,128]{2,1,0:T(8,128)S(1)}, u32[]{:S(2)}, u32[]{:S(2)}) %collective-permute-start.5) | collective-permute-done | bytes 73760 | tf_op jit(solution)/shard_map/ppermute | solution.py:596
  17.9 1.0 %copy-done = bf16[608,192]{1,0:T(8,128)(2,1)S(1)} copy-done((bf16[608,192]{1,0:T(8,128)(2,1)S(1)}, bf16[608,192]{1,0:T(8,128)(2,1)}, u32[]{:S(2)}) %copy-start) | copy-done | bytes 233496
  18.9 5.5 %shard_map.123 = (f32[24,64,256]{2,1,0:T(8,128)S(1)}, f32[24,64,256]{2,1,0:T(8,128)S(1)}, f32[24,64,256]{2,1,0:T(8,128)S(1)}, f32[24,64,256]{2,1,0:T(8,128)S(1)}...) custom-call(f32[2,72,128]{2,1,0:T(8,128)S(1)} %collective-permute-do, ...), custom_call_target="tpu_custom_call" | custom-call | flops 5000000000 | bytes 2000000 | tf_op jit(solution)/shard_map/pallas_call | solution.py:516
  24.5 12.9 %shard_map.124 = (f32[3,4,8,128]{3,2,1,0:T(8,128)S(1)}, f32[8,256]{1,0:T(8,128)S(1)}) custom-call(f32[2,72,128]{2,1,0:T(8,128)S(1)} %bitcast.33, f32[2,72,128]{2,1,0:T(8,128)S(1)} %bitcast.37, f32[2,2,72,128]{3,2,1,0:T(8,128)S(1)} %pad_maximum_fusion.1.core_own.refs_2_, f32[2,2,72,128]{3,2,1,0:T(8,128)S(1)} %collective-permute-done.1.core_sides.refs_3_, ...), custom_call_target="tpu_custom_call" | custom-call | flops 12000000000 | bytes 2000000 | tf_op jit(solution)/shard_map/pallas_call | solution.py:526
  37.4 2.3 %collective-permute-start.6 = (f32[4,4,128]{2,1,0:T(4,128)S(1)}, f32[4,4,128]{2,1,0:T(4,128)S(1)}, u32[]{:S(2)}, u32[]{:S(2)}) collective-permute-start(f32[4,4,128]{2,1,0:T(4,128)S(1)} %slice_bitcast_fusion.5), channel_id=1, source_target_pairs={{0,12},{4,8},{8,4},{12,0},{1,13},{5,9},{9,5},{13,1},{2,14},{6,10},... | collective-permute-start | bytes 24584 | tf_op jit(solution)/shard_map/ppermute | solution.py:605
  39.7 7.8 %shard_map.125 = (f32[3,4,8,128]{3,2,1,0:T(8,128)S(1)}, f32[8,256]{1,0:T(8,128)S(1)}) custom-call(bf16[608,192]{1,0:T(8,128)(2,1)S(1)} %copy-done.1, f32[1,64]{1,0:T(1,128)S(1)} %bitcast.36, f32[3,4,8,128]{3,2,1,0:T(8,128)S(1)} %get-tuple-element.61.added, f32[24,64,256]{2,1,0:T(8,128)S(1)} %get-tuple-element.62.act, ...), custom_call_target="tpu_custom_call" | custom-call | flops 20000000000 | bytes 2000000 | tf_op jit(solution)/shard_map/pallas_call | solution.py:520
  47.6 3.6 %collective-permute-done.7 = f32[4,4,128]{2,1,0:T(4,128)S(1)} collective-permute-done((f32[4,4,128]{2,1,0:T(4,128)S(1)}, f32[4,4,128]{2,1,0:T(4,128)S(1)}, u32[]{:S(2)}, u32[]{:S(2)}) %collective-permute-start.7) | collective-permute-done | bytes 8224 | tf_op jit(solution)/shard_map/ppermute | solution.py:608
  51.2 1.6 %collective-permute-start.8 = (f32[2,2,4,128]{3,2,1,0:T(4,128)S(1)}, f32[2,2,4,128]{3,2,1,0:T(4,128)S(1)}, u32[]{:S(2)}, u32[]{:S(2)}) collective-permute-start(f32[2,2,4,128]{3,2,1,0:T(4,128)S(1)} %pad_maximum_fusion.4), channel_id=1, source_target_pairs={{0,2},{2,0},{1,3},{3,1},{4,6},{6,4},{5,7},{7,5},{8,10},{10,8},{9,1... | collective-permute-start | bytes 24584 | tf_op jit(solution)/shard_map/ppermute | solution.py:538
  52.9 2.1 %collective-permute-done.8 = f32[2,2,4,128]{3,2,1,0:T(4,128)S(1)} collective-permute-done((f32[2,2,4,128]{3,2,1,0:T(4,128)S(1)}, f32[2,2,4,128]{3,2,1,0:T(4,128)S(1)}, u32[]{:S(2)}, u32[]{:S(2)}) %collective-permute-start.8) | collective-permute-done | bytes 8224 | tf_op jit(solution)/shard_map/ppermute | solution.py:538
  55.2 0.6 %slice.126 = f32[2,2,1,64]{3,2,1,0:T(1,128)} slice(f32[2,2,2,64]{3,2,1,0:T(2,128)S(1)} %reshape.33), slice={[0:2], [0:2], [0:1], [0:64]} | slice | bytes 2048 | tf_op jit(solution)/shard_map/slice | solution.py:615
  55.8 0.5 collective-permute-done.9
  56.4 0.6 %copy.18 = f32[3,2,2,64]{3,2,1,0:T(2,128)} copy(f32[3,2,2,64]{3,0,2,1:T(4,128)S(1)} %fusion.1) | data formatting | bytes 6144
  (51 shorter events, 0.9 us)
Async XLA Ops:
  0.6 3.6 %copy-start.4 = (s32[2,2,64]{2,1,0:T(2,128)S(1)}, s32[2,2,64]{2,1,0:T(2,128)}, u32[]{:S(2)}) copy-start(s32[2,2,64]{2,1,0:T(2,128)} %param.14) | copy-start | bytes 3076
  2.4 2.2 %copy-start.3 = (s32[48,2,2,64]{3,2,1,0:T(2,128)S(1)}, s32[48,2,2,64]{3,2,1,0:T(2,128)}, u32[]{:S(2)}) copy-start(s32[48,2,2,64]{3,2,1,0:T(2,128)} %param.13) | copy-start | bytes 147460
  2.7 1.7 %collective-permute-start = (f32[2,2,72,64]{3,2,1,0:T(8,128)S(1)}, f32[2,2,72,64]{3,2,1,0:T(8,128)S(1)}, u32[]{:S(2)}, u32[]{:S(2)}) collective-permute-start(f32[2,2,72,64]{3,2,1,0:T(8,128)S(1)} %pad_maximum_fusion), channel_id=1, source_target_pairs={{0,1},{1,0},{2,3},{3,2},{4,5},{5,4},{6,7},{7,6},{8,9},{9,8},{10,11... | collective-permute-start | bytes 221192 | tf_op jit(solution)/shard_map/ppermute | solution.py:538
  4.9 8.6 %collective-permute-start.1 = (f32[2,2,72,128]{3,2,1,0:T(8,128)S(1)}, f32[2,2,72,128]{3,2,1,0:T(8,128)S(1)}, u32[]{:S(2)}, u32[]{:S(2)}) collective-permute-start(f32[2,2,72,128]{3,2,1,0:T(8,128)S(1)} %pad_maximum_fusion.2), channel_id=1, source_target_pairs={{0,2},{2,0},{1,3},{3,1},{4,6},{6,4},{5,7},{7,5},{8,10},{10,8},{9,1... | collective-permute-start | bytes 442376 | tf_op jit(solution)/shard_map/ppermute | solution.py:538
  7.7 8.7 %collective-permute-start.4 = (f32[2,72,128]{2,1,0:T(8,128)S(1)}, f32[2,72,128]{2,1,0:T(8,128)S(1)}, u32[]{:S(2)}, u32[]{:S(2)}) collective-permute-start(f32[2,72,128]{2,1,0:T(8,128)S(1)} %get-tuple-element.48), channel_id=1, source_target_pairs={{0,4},{4,0},{8,12},{12,8},{1,5},{5,1},{9,13},{13,9},{2,6},{6,2},{1... | collective-permute-start | bytes 221192 | tf_op jit(solution)/shard_map/ppermute | solution.py:593
  9.3 6.5 %collective-permute-start.2 = (f32[1,2,72,128]{3,2,1,0:T(8,128)S(1)}, f32[1,2,72,128]{3,2,1,0:T(8,128)S(1)}, u32[]{:S(2)}, u32[]{:S(2)}) collective-permute-start(f32[1,2,72,128]{3,2,1,0:T(8,128)S(1)} %get-tuple-element.44), channel_id=1, source_target_pairs={{0,12},{4,8},{8,4},{12,0},{1,13},{5,9},{9,5},{13,1},{2,14},{6,10},... | collective-permute-start | bytes 221192 | tf_op jit(solution)/shard_map/ppermute | solution.py:594
  13.5 4.4 %collective-permute-start.5 = (f32[2,72,128]{2,1,0:T(8,128)S(1)}, f32[2,72,128]{2,1,0:T(8,128)S(1)}, u32[]{:S(2)}, u32[]{:S(2)}) collective-permute-start(f32[2,72,128]{2,1,0:T(8,128)S(1)} %slice_bitcast_fusion.1), channel_id=1, source_target_pairs={{0,4},{4,0},{8,12},{12,8},{1,5},{5,1},{9,13},{13,9},{2,6},{6,2},{1... | collective-permute-start | bytes 221192 | tf_op jit(solution)/shard_map/ppermute | solution.py:596
  15.8 8.7 %collective-permute-start.3 = (f32[1,2,72,128]{3,2,1,0:T(8,128)S(1)}, f32[1,2,72,128]{3,2,1,0:T(8,128)S(1)}, u32[]{:S(2)}, u32[]{:S(2)}) collective-permute-start(f32[1,2,72,128]{3,2,1,0:T(8,128)S(1)} %pad_maximum_fusion.3), channel_id=1, source_target_pairs={{0,2},{2,0},{1,3},{3,1},{4,6},{6,4},{5,7},{7,5},{8,10},{10,8},{9,1... | collective-permute-start | bytes 221192 | tf_op jit(solution)/shard_map/ppermute | solution.py:538
  17.9 1.0 %copy-start = (bf16[608,192]{1,0:T(8,128)(2,1)S(1)}, bf16[608,192]{1,0:T(8,128)(2,1)}, u32[]{:S(2)}) copy-start(bf16[608,192]{1,0:T(8,128)(2,1)} %shard_map.122.merged.refs_6_) | copy-start | bytes 700420
  18.9 5.5 %copy-start.1 = (bf16[608,192]{1,0:T(8,128)(2,1)S(1)}, bf16[608,192]{1,0:T(8,128)(2,1)}, u32[]{:S(2)}) copy-start(bf16[608,192]{1,0:T(8,128)(2,1)} %shard_map.122.merged.refs_6_) | copy-start | bytes 700420
  18.9 5.6 %copy-start.2 = (f32[64]{0:T(128)S(1)}, f32[64]{0:T(128)}, u32[]{:S(2)}) copy-start(f32[64]{0:T(128)} %param.21) | copy-start | bytes 772
  37.4 10.1 %collective-permute-start.6 = (f32[4,4,128]{2,1,0:T(4,128)S(1)}, f32[4,4,128]{2,1,0:T(4,128)S(1)}, u32[]{:S(2)}, u32[]{:S(2)}) collective-permute-start(f32[4,4,128]{2,1,0:T(4,128)S(1)} %slice_bitcast_fusion.5), channel_id=1, source_target_pairs={{0,12},{4,8},{8,4},{12,0},{1,13},{5,9},{9,5},{13,1},{2,14},{6,10},... | collective-permute-start | bytes 24584 | tf_op jit(solution)/shard_map/ppermute | solution.py:605
  47.5 3.7 %collective-permute-start.7 = (f32[4,4,128]{2,1,0:T(4,128)S(1)}, f32[4,4,128]{2,1,0:T(4,128)S(1)}, u32[]{:S(2)}, u32[]{:S(2)}) collective-permute-start(f32[4,4,128]{2,1,0:T(4,128)S(1)} %slice_bitcast_fusion.4), channel_id=1, source_target_pairs={{0,4},{4,0},{8,12},{12,8},{1,5},{5,1},{9,13},{13,9},{2,6},{6,2},{1... | collective-permute-start | bytes 24584 | tf_op jit(solution)/shard_map/ppermute | solution.py:608
  51.2 3.7 %collective-permute-start.8 = (f32[2,2,4,128]{3,2,1,0:T(4,128)S(1)}, f32[2,2,4,128]{3,2,1,0:T(4,128)S(1)}, u32[]{:S(2)}, u32[]{:S(2)}) collective-permute-start(f32[2,2,4,128]{3,2,1,0:T(4,128)S(1)} %pad_maximum_fusion.4), channel_id=1, source_target_pairs={{0,2},{2,0},{1,3},{3,1},{4,6},{6,4},{5,7},{7,5},{8,10},{10,8},{9,1... | collective-permute-start | bytes 24584 | tf_op jit(solution)/shard_map/ppermute | solution.py:538
  55.1 1.2 %collective-permute-start.9 = (f32[2,2,4,64]{3,2,1,0:T(4,128)S(1)}, f32[2,2,4,64]{3,2,1,0:T(4,128)S(1)}, u32[]{:S(2)}, u32[]{:S(2)}) collective-permute-start(f32[2,2,4,64]{3,2,1,0:T(4,128)S(1)} %pad_maximum_fusion.5), channel_id=1, source_target_pairs={{0,1},{1,0},{2,3},{3,2},{4,5},{5,4},{6,7},{7,6},{8,9},{9,8},{10,11... | collective-permute-start | bytes 12296 | tf_op jit(solution)/shard_map/ppermute | solution.py:538

commit v3 on v2

--- a/solution.py
+++ b/solution.py
@@ -22,8 +22,9 @@
 BASIS = 8
 MIRRORED = 64
 SPACING = cutoff / (BASIS - 1)
-GROUP = 4
-UNROLL = 1
+STEP = 8
+ALONE = ((8, 1), (8, 1), (8, 1))
+TOGETHER = ((3, 3), (3, 3), (8, 1))
 
 U, Q, ENV, DIST, INV, VEC, DENV, GEO = 0, 3, 9, 10, 11, 12, 15, 16
 
@@ -60,22 +61,28 @@
 W_A, W_B, W_C, W_D, W_E, W_P, W_S, W_R, W_END = 0, 144, 208, 336, 400, 416, 480, 544, 608
 
 
-def pipeline(stages, last=None):
-    groups, depth = HALF // GROUP, len(stages)
+def pipeline(stages, plan, last=None):
+    group, unroll = plan
+    groups, depth = HALF // group, len(stages)
 
     def step(t, first, stop):
         for k in range(stop - 1, first - 1, -1):
-            start = (t - k) * GROUP
-            for i in range(GROUP):
+            start = (t - k) * group
+            for i in range(group):
                 stages[k](start + i, i)
             if k == depth - 1 and last is not None:
-                last(start)
+                last(start, group)
 
     for t in range(depth - 1):
         step(t, 0, t + 1)
-    pl.loop(depth - 1, groups, unroll=UNROLL)(lambda t: step(t, 0, depth))
+    pl.loop(depth - 1, groups, unroll=unroll)(lambda t: step(t, 0, depth))
     for t in range(groups, groups + depth - 1):
         step(t, t - groups + 1, depth)
+
+
+def one_hot(index, size):
+    rows = lax.broadcasted_iota(jnp.int16, (size, index.shape[1]), 0)
+    return jnp.where(rows == index.astype(jnp.int16), jnp.ones((), bf16), jnp.zeros((), bf16))
 
 
 def basis(dist):
@@ -115,15 +122,64 @@
     merged[W_R:W_END, :] = rows.T.astype(bf16)
 
 
+def column_of(own, sides, yc):
+    return sides.at[yc // 3] if yc in (0, 3) else own.at[yc - 1]
+
+
+def both(x):
+    return jnp.where(lane_row() < 64, pltpu.roll(x, 96, 1), pltpu.roll(x, 32, 1))
+
+
+def early(
+    core_own,
+    core_sides,
+    codes,
+    limits,
+    w_self,
+    w_pair,
+    w_radial,
+    w_tensor,
+    mix_t,
+    w_out,
+    merged,
+    pair,
+    self_t,
+    lane_i,
+    col_i,
+):
+    prepare(w_self, w_pair, w_radial, w_tensor, mix_t, w_out, merged)
+    for x in range(2):
+        columns = [column_of(core_own.at[x], core_sides.at[x], yc) for yc in range(4)]
+        rows = jnp.concatenate([column[:FEAT, :] for column in columns], axis=1)
+        terms = dot(merged[W_P:W_S, :], stacked(rows))
+        own = dot(merged[W_S:W_R, :], stacked(rows[:, 128:384]))
+        for yc in range(4):
+            pair[4 * x + yc] = terms[:, 128 * yc : 128 * yc + 128]
+        for y in range(2):
+            self_t[x, :, 128 * y : 128 * y + 128] = both(own[:, 128 * y : 128 * y + 128])
+        code = codes[x]
+        offset = code >> 5
+        plane = (offset * 43) >> 7
+        dz = offset - 3 * plane
+        dx = (offset * 57) >> 9
+        lane256 = lax.broadcasted_iota(jnp.int32, (HALF, WIDE), 1)
+        lane_i[x] = ((((lane256 >> 5) & 1) + dz) << 5) + (code & 31)
+        col_i[x] = plane + jnp.where(limits[x] >= MIRRORED, 6 - 6 * dx, 0)
+
+
 def front(
+    plan,
     which,
     ghost_own,
     ghost_sides,
     core_own,
     core_sides,
-    codes,
     limit,
     merged,
+    pair,
+    self_t,
+    lane_i,
+    col_i,
     act,
     slope,
     tens,
@@ -131,51 +187,34 @@
     v_acc,
     e_row,
     geo,
-    lane_i,
-    col_i,
-    pair,
-    self_t,
+    table,
     step_a,
     step_b,
 ):
-    w_a = merged.at[W_A:W_B]
-    w_p, w_s = merged.at[W_P:W_S], merged.at[W_S:W_R]
+    w_a, w_p = merged.at[W_A:W_B], merged.at[W_P:W_S]
     w_r = merged.at[W_R:W_END, 0 : 4 * BASIS]
+    self_t, lane_i, col_i = self_t.at[which], lane_i.at[which], col_i.at[which]
+    far_layer = 0 if which == 0 else 2
+    near_first = 3 if which == 0 else 0
 
     def source(dx, yc):
-        here = yc - 1 if yc in (1, 2) else yc // 3
-        own, sides = (ghost_own, ghost_sides), (core_own, core_sides)
-        if dx == (0 if which == 0 else 2):
-            return own[yc in (0, 3)].at[here]
-        return sides[yc in (0, 3)].at[dx - 1 + which, here]
-
-    lanes = lane_row()
-
-    def both(x):
-        return jnp.where(lanes < 64, pltpu.roll(x, 96, 1), pltpu.roll(x, 32, 1))
-
-    for dx in range(3):
-        rows = jnp.concatenate([source(dx, yc)[:FEAT, :] for yc in range(4)], axis=1)
-        terms = dot(w_p[...], stacked(rows))
-        for yc in range(4):
-            pair[dx * 4 + yc] = terms[:, 128 * yc : 128 * yc + 128]
-    rows = jnp.concatenate([source(1, 1 + y)[:FEAT, :] for y in range(2)], axis=1)
-    terms = dot(w_s[...], stacked(rows))
-    for y in range(2):
-        self_t[:, 128 * y : 128 * y + 128] = both(terms[:, 128 * y : 128 * y + 128])
-
-    code = codes[...]
-    offset = code >> 5
-    plane = (offset * 43) >> 7
-    dz = offset - 3 * plane
-    dx = (offset * 57) >> 9
-    dy = plane - 3 * dx
-    limits = limit[...]
-    mirrored = jnp.where(limits >= MIRRORED, 2 - dx, dx)
+        if dx == far_layer:
+            return column_of(ghost_own, ghost_sides, yc)
+        x = dx - 1 + which
+        return column_of(core_own.at[x], core_sides.at[x], yc)
+
+    rows = jnp.concatenate([source(far_layer, yc)[:FEAT, :] for yc in range(4)], axis=1)
+    hi, lo = halves(dot(w_p[...], stacked(rows)))
+    table[:FEAT] = hi
+    table[FEAT:] = lo
+
     lane256 = lax.broadcasted_iota(jnp.int32, (HALF, WIDE), 1)
-    z_own = (lane256 >> 5) & 1
-    lane_i[...] = ((z_own + dz) << 5) + (code & 31)
-    col_i[...] = 3 * mirrored + dy
+    column = col_i[...]
+    mirrored = (column * 11) >> 5
+    limits = limit[which]
+    dx = jnp.where(limits >= MIRRORED, 2 - mirrored, mirrored)
+    dy = column - 3 * mirrored
+    dz = (lane_i[...] >> 5) - ((lane256 >> 5) & 1)
     rank = lax.broadcasted_iota(jnp.int32, (HALF, WIDE), 0) + HALF * ((lane256 >> 6) & 1)
     mask = (rank < (limits & (MIRRORED - 1))).astype(f32)
 
@@ -226,15 +265,19 @@
     def gathered(s):
         lane_s = lane_i[pl.ds(s, 1), :]
         col_s = col_i[pl.ds(s, 1), :]
+        far_col = col_s - 3 * far_layer + (lax.broadcasted_iota(jnp.int32, (1, WIDE), 1) >> 7)
+        is_far = (col_s < 3) if which == 0 else (col_s >= 6)
+        spots = jnp.where(is_far, (far_col << 7) + lane_s, -1)
         sides = []
         for y in range(2):
             lane = jnp.broadcast_to(lane_s[:, 128 * y : 128 * y + 128], (8, 128))
             col = jnp.broadcast_to(col_s[:, 128 * y : 128 * y + 128], (8, 128))
-            masks = [col == c for c in range(9)]
+            masks = [col == c + near_first for c in range(6)]
+            near = (col >= 3) if which == 0 else (col < 6)
             groups = []
             for g in range(FEAT // 8):
                 acc = None
-                for c in range(9):
+                for c in range(6):
                     value = jnp.take_along_axis(
                         pair[(c // 3) * 4 + y + c % 3, 8 * g : 8 * g + 8, :],
                         lane,
@@ -242,9 +285,10 @@
                         mode="promise_in_bounds",
                     )
                     acc = value if c == 0 else jnp.where(masks[c], value, acc)
-                groups.append(acc)
+                groups.append(jnp.where(near, acc, 0.0))
             sides.append(jnp.concatenate(groups, axis=0))
-        return jnp.concatenate(sides, axis=1)
+        far = dot(table[...], one_hot(spots, 512))
+        return jnp.concatenate(sides, axis=1) + (far[:FEAT] + far[FEAT:])
 
     def forward_a(s, i):
         _, waves = basis(row(DIST, s))
@@ -265,23 +309,27 @@
         mix0[s] = both_t[FEAT : 2 * FEAT]
         e_row[pl.ds(s, 1), :] = both_t[2 * FEAT : 2 * FEAT + 1]
 
-    def forward_sum(first):
+    def forward_sum(first, group):
         for k in range(9):
             part = slice(0, 32) if k < 3 else slice(32, 64)
             total = v_acc[k]
-            for i in range(GROUP):
+            for i in range(group):
                 total += step_b[i, part] * row(k, first + i)
             v_acc[k] = total
 
-    pipeline((forward_a, forward_b, forward_c), forward_sum)
+    pipeline((forward_a, forward_b, forward_c), plan[0], forward_sum)
 
     for k in range(9):
         v_acc[k] = env_norm * fold_sides(v_acc[k])
 
 
 def rear(
+    plan,
+    which,
     merged,
     out_row,
+    lane_i,
+    col_i,
     added,
     act,
     slope,
@@ -290,8 +338,6 @@
     v_acc,
     e_row,
     geo,
-    lane_i,
-    col_i,
     out,
     energy,
     step_a,
@@ -309,6 +355,7 @@
     s_acc,
     own_sum,
 ):
+    lane_i, col_i = lane_i.at[which], col_i.at[which]
     w_b, w_c = merged.at[W_B:W_C], merged.at[W_C:W_D]
     w_d, w_e = merged.at[W_D:W_E], merged.at[W_E:W_P]
     lanes = lane_row()
@@ -347,15 +394,15 @@
         prod[s] = p
         step_c[i] = p
 
-    def middle_sum(first):
+    def middle_sum(first, group):
         for k in range(9):
             part = slice(0, 32) if k < 3 else slice(32, 64)
             total = dv_acc[k]
-            for i in range(GROUP):
+            for i in range(group):
                 total += step_c[i, part] * row(k, first + i)
             dv_acc[k] = total
 
-    pipeline((middle_a, middle_b, middle_c), middle_sum)
+    pipeline((middle_a, middle_b, middle_c), plan[1], middle_sum)
 
     for k in range(9):
         dv_acc[k] = env_norm * fold_sides(dv_acc[k])
@@ -388,7 +435,7 @@
         x, waves = basis(row(DIST, s))
         dr_row[pl.ds(s, 1), :] = jnp.sum(step_b[i, :8] * waves * x, axis=0, keepdims=True)
 
-    pipeline((backward_a, backward_b, backward_c))
+    pipeline((backward_a, backward_b, backward_c), plan[2])
 
     env, m_sum = geo[ENV], m_row[...]
     values = jnp.sum(e_row[...] + env * m_sum, axis=0, keepdims=True)
@@ -446,28 +493,27 @@
         out[...] = jnp.zeros_like(out)
     else:
         out[0:2] = added[1:3]
-        out[2] = jnp.zeros_like(out[2])
+        out[2:3] = jnp.zeros_like(out[2:3])
     for y in range(2):
         for c in range(9):
             tile = s_acc[y, 8 * c : 8 * c + 8, :]
-            out[c // 3, y + c % 3, 0:3, :] += tile[0:3] + tile[3:6]
+            for d in range(3):
+                out[c // 3, d, y + c % 3 : y + c % 3 + 1, :] += tile[d : d + 1] + tile[3 + d : 4 + d]
         own = pltpu.roll(own_sum[:, 128 * y : 128 * y + 128], 32, 1)
         kept = jnp.where((lanes >= 32) & (lanes < 96), own, 0.0)
-        out[1, 1 + y, 0:3, :] -= kept[0:3]
+        for d in range(3):
+            out[1, d, 1 + y : 2 + y, :] -= kept[d : d + 1]
 
 
 def whole(which, *refs):
-    given, out, rest = refs[:7], refs[8:10], refs[10:]
-    kept, rest = rest[:9], rest[9:]
-    steps, rest = rest[:3], rest[3:]
-    front(which, *given, *kept, *rest[:2], *steps[:2])
-    rear(refs[6], refs[7], None, *kept, *out, *steps, *rest[2:])
-
-
-def run_prepare(*weights):
-    return pl.pallas_call(
-        prepare, out_shape=jax.ShapeDtypeStruct((W_END, 3 * FEAT), bf16)
-    )(*weights)
+    given, out_row, out, rest = refs[:10], refs[10], refs[11:13], refs[13:]
+    kept, table, steps, rest = rest[:7], rest[7], rest[8:11], rest[11:]
+    front(TOGETHER, which, *given, *kept, table, *steps[:2])
+    rear(TOGETHER, which, given[5], out_row, *given[8:10], None, *kept, *out, *steps, *rest)
+
+
+def opening(which, ghost, *refs):
+    front(ALONE, which, ghost.at[0:2], ghost.at[2:4], *refs)
 
 
 BIG = (HALF, FEAT, WIDE)
@@ -481,60 +527,68 @@
     (SUMS, f32),
     (FLAT, f32),
     ((GEO, HALF, WIDE), f32),
-    (FLAT, jnp.int32),
-    (FLAT, jnp.int32),
 )
-STEPS = ((GROUP, FEAT, WIDE), (GROUP, 2 * FEAT + 16, WIDE), (GROUP, FEAT, WIDE))
-FRONT = ((12, FEAT, 128), (FEAT, WIDE))
+STEPS = tuple(((STEP, rows, WIDE), f32) for rows in (FEAT, 2 * FEAT + 16, FEAT))
+TABLE = (((2 * FEAT, 4 * 128), bf16),)
+EARLY = (
+    ((W_END, 3 * FEAT), bf16),
+    ((8, FEAT, 128), f32),
+    ((2, FEAT, WIDE), f32),
+    ((2,) + FLAT, jnp.int32),
+    ((2,) + FLAT, jnp.int32),
+)
 REAR = (BIG, BIG, BIG, FLAT, FLAT, SUMS[:1] + FLAT, FLAT, SUMS)
 REAR = REAR + ((HALF, 8, WIDE), (2, 72, 128), (8, WIDE))
+REAR = tuple((shape, f32) for shape in REAR)
 RESULT = (
-    jax.ShapeDtypeStruct((3, 4, 8, 128), f32),
+    jax.ShapeDtypeStruct((3, 3, 4, 128), f32),
     jax.ShapeDtypeStruct((8, WIDE), f32),
 )
 
 
 def in_vmem(shapes):
-    return [pltpu.VMEM(shape, f32) for shape in shapes]
-
-
-def call(kernel, out_shape, scratch, micros):
+    return [pltpu.VMEM(shape, dtype) for shape, dtype in shapes]
+
+
+def call(kernel, out_shape, scratch, micros, mib):
     return pl.pallas_call(
         kernel,
         out_shape=out_shape,
         scratch_shapes=scratch,
-        compiler_params=pltpu.CompilerParams(vmem_limit_bytes=40 * 2**20),
+        compiler_params=pltpu.CompilerParams(vmem_limit_bytes=mib * 2**20),
         cost_estimate=pl.CostEstimate(
             flops=micros * 1_000_000_000, bytes_accessed=2_000_000, transcendentals=2_000_000
         ),
     )
 
 
+def shaped(shapes):
+    return [jax.ShapeDtypeStruct(shape, dtype) for shape, dtype in shapes]
+
+
+def run_early(*given):
+    return call(early, shaped(EARLY), [], 2, 16)(*given)
+
+
 def run_front(which, *given):
-    shapes = [jax.ShapeDtypeStruct(shape, dtype) for shape, dtype in KEPT]
-    scratch = in_vmem(FRONT + STEPS[:2])
-    return call(functools.partial(front, which), shapes, scratch, 5)(*given)
-
-
-def run_rear(merged, out_row, added, kept):
-    return call(rear, RESULT, in_vmem(STEPS + REAR), 20)(merged, out_row, added, *kept)
+    scratch = in_vmem(TABLE + STEPS[:2])
+    return call(functools.partial(opening, which), shaped(KEPT), scratch, 5, 16)(*given)
+
+
+def run_rear(which, *given):
+    return call(functools.partial(rear, ALONE, which), RESULT, in_vmem(STEPS + REAR), 20, 24)(*given)
 
 
 def run_whole(which, *given):
-    scratch = [pltpu.VMEM(shape, dtype) for shape, dtype in KEPT]
-    scratch = scratch + in_vmem(STEPS + FRONT + REAR)
-    return call(functools.partial(whole, which), RESULT, scratch, 12)(*given)
-
-
-def shifts(axis):
+    scratch = in_vmem(KEPT + TABLE + STEPS + REAR)
+    return call(functools.partial(whole, which), RESULT, scratch, 12, 28)(*given)
+
+
+def exchange(low, high, axis, dim):
     size = lax.axis_size(axis)
     up = [(i, (i + 1) % size) for i in range(size)]
-    return up, [(j, i) for i, j in up]
-
-
-def exchange(low, high, axis, dim):
-    up, down = shifts(axis)
-    if lax.axis_size(axis) == 2:
+    down = [(j, i) for i, j in up]
+    if size == 2:
         return lax.ppermute(jnp.concatenate([high, low], axis=dim), axis, up)
     parts = [lax.ppermute(high, axis, up), lax.ppermute(low, axis, down)]
     return jnp.concatenate(parts, axis=dim)
@@ -578,39 +632,37 @@
     limit = mirrored(limit) + MIRRORED * odd.astype(jnp.int32)
     limit = jnp.broadcast_to(limit[:, :, None, :], (cells_x, cells_y, 2, lanes))
     limit = limit.reshape(cells_x, 1, WIDE)
-    ends, nbr_index, w_self = lax.optimization_barrier((ends, nbr_index, w_self))
+    ends, nbr_index = lax.optimization_barrier((ends, nbr_index))
     state = jnp.concatenate([ends[..., :SLOTS], state, ends[..., SLOTS:]], axis=-1)
 
     size = lax.axis_size("gx")
     first = [(i, i + 1 - 2 * (i % 2)) for i in range(size)]
     second = [(i, (i - 1 + 2 * (i % 2)) % size) for i in range(size)]
     sides = exchange(state[:, :1], state[:, -1:], "gy", 1)
-    out_row = w_out[None]
-    merged = run_prepare(w_self, w_pair, w_radial, w_tensor, w_mix.T, out_row)
     codes = nbr_index.reshape(2, HALF, cells_x, cells_y, lanes)
     codes = mirrored(codes.transpose(2, 1, 3, 0, 4).reshape(cells_x, HALF, WIDE))
-    inner_own, outer_own, codes = lax.optimization_barrier((state[1], state[:1], codes))
-    inner_own = lax.ppermute(inner_own, "gx", first)
+    outer_own, codes = lax.optimization_barrier((state[:1], codes))
     outer_own = lax.ppermute(outer_own, "gx", second)
-    sides, merged, codes, limit = lax.optimization_barrier((sides, merged, codes, limit))
-    inner_sides = lax.ppermute(sides[1], "gx", first)
+    inner = lax.ppermute(jnp.concatenate([state[1], sides[1]]), "gx", first)
+    out_row = w_out[None]
+    weights = (w_self, w_pair, w_radial, w_tensor, w_mix.T, out_row)
+    merged, *decoded = run_early(state, sides, codes, limit, *weights)
     outer_own, late_sides = lax.optimization_barrier((outer_own, sides))
     outer_sides = exchange(outer_own[:, :1], outer_own[:, -1:], "gy", 1)[0]
 
-    kept = run_front(1, inner_own, inner_sides, state, sides, codes[1], limit[1], merged)
+    kept = run_front(1, inner, state, sides, limit, merged, *decoded)
     late_sides, kept = lax.optimization_barrier((late_sides, kept))
     grad0, energy0 = run_whole(
-        0, outer_own[0], outer_sides, state, late_sides, codes[0], limit[0], merged, out_row
+        0, outer_own[0], outer_sides, state, late_sides, limit, merged, *decoded, out_row
     )
-    back0 = lax.ppermute(grad0[0, :, :4], "gx", second)
-    grad1, energy1 = run_rear(merged, out_row, grad0, kept)
+    back0 = lax.ppermute(grad0[0], "gx", second)
+    grad1, energy1 = run_rear(1, merged, out_row, *decoded[2:], grad0, *kept)
     grad1, back0 = lax.optimization_barrier((grad1, back0))
-    back1 = lax.ppermute(grad1[2, :, :4], "gx", first)
-
-    grad = grad1[:2, :, :4] + jnp.stack([back0, back1])
-    grad = grad[:, 1:-1] + exchange(grad[:, :1], grad[:, -1:], "gy", 1)
+    back1 = lax.ppermute(grad1[2], "gx", first)
+    grad = grad1[:2] + jnp.stack([back0, back1])
+    grad = grad[:, :, 1:-1] + exchange(grad[:, :, :1], grad[:, :, -1:], "gy", 2)
     grad = grad[..., SLOTS:-SLOTS] + exchange(grad[..., :SLOTS], grad[..., -SLOTS:], "gz", 3)
-    forces = -mirrored(grad)[:, :, :3].transpose(2, 0, 1, 3)
+    forces = -mirrored(grad).transpose(1, 0, 2, 3)
     energies = mirrored(jnp.stack([energy0[0], energy1[0]]))
     energies = energies.reshape(cells_x, cells_y, 2, lanes)[:, :, 0]
     return forces, energies

time: 57.3 us -> 53.8 us (0.939)
  Pallas kernels: 28 us -> 23.6 us
  starting transfers between devices: 12.6 us -> 15.4 us
  local copies, waits for them, and re-layouts: 5.67 us -> 4.71 us
  waiting for transfers between devices: 9.22 us -> 8.42 us
    pallas_call x4, Pallas kernels: 28 us -> 23.6 us  [the longest x1 11.6 us: run_whole(): call(functools.partial(whole, which), RESULT, scratch, 12, 28)(*given)]
    ppermute x1, waiting for transfers between devices: 1.49 us -> 0.26 us  [local(): outer_own = lax.ppermute(outer_own, 'gx', second)]
    ppermute x1, starting transfers between devices: 2.47 us -> 3.67 us  [local(): outer_own = lax.ppermute(outer_own, 'gx', second)]
    unnamed x13 -> x19, local copies, waits for them, and re-layouts: 3.2 us -> 2.25 us
    ppermute x4 -> x3, starting transfers between devices: 4.69 us -> 5.56 us  [the longest x1 3.59 us: local(): back0 = lax.ppermute(grad0[0], 'gx', second)]
    ppermute x5, starting transfers between devices: 5.46 us -> 6.13 us  [exchange(): return lax.ppermute(jnp.concatenate([high, low], axis=dim), axis, up)]
    ppermute x4 -> x3, waiting for transfers between devices: 5.18 us -> 5.19 us  [the longest x1 3.59 us: local(): back1 = lax.ppermute(grad1[2], 'gx', first)]
  transfers between devices with their start and end apart: 10 -> 9, of which waited for: 5 -> 6; matrix products, arithmetic and copies ran while one was open for 3% -> 4% of each run, Pallas kernels for 26% -> 22%
where the time goes in v3:
time: 53.8 us; the launch traced here: 53.6 us
  Pallas kernels  23.6 us (44%)
  starting transfers between devices  15.4 us (29%)
  waiting for transfers between devices  8.42 us (16%)
  local copies, waits for them, and re-layouts  4.71 us (9%)
  between operations  0.91 us (2%)
  other arithmetic  0.62 us (1%)
    pallas_call x1, Pallas kernels, run_whole(): call(functools.partial(whole, which), RESULT, scratch, 12, 28)(*given)  11.6 us
    pallas_call x1, Pallas kernels, run_rear(): call(functools.partial(rear, ALONE, which), RESULT, in_vmem(STEPS + REAR)...  7.34 us
    ppermute x5, starting transfers between devices, exchange(): return lax.ppermute(jnp.concatenate([high, low], axis=dim), axis, up)  6.13 us
    pallas_call x1, Pallas kernels, run_front(): call(functools.partial(opening, which), shaped(KEPT), scratch, 5, 16)  4.05 us
    ppermute x1, starting transfers between devices, local(): outer_own = lax.ppermute(outer_own, 'gx', second)  3.67 us
    ppermute x1, waiting for transfers between devices, local(): back1 = lax.ppermute(grad1[2], 'gx', first)  3.59 us
    ppermute x1, starting transfers between devices, local(): back0 = lax.ppermute(grad0[0], 'gx', second)  3.59 us
    ppermute x5, waiting for transfers between devices, exchange(): return lax.ppermute(jnp.concatenate([high, low], axis=dim), axis, up)  2.96 us
  transfers between devices with their start and end apart: 9, of which 6 were waited for; matrix products, arithmetic and copies ran while one was open for 4% of the time, Pallas kernels for 22%

profile of v3, /device:TPU:0, one launch (start us, length us, event | category | flops | bytes accessed | tf_op | source)
XLA Modules:
  0.0 53.6 jit_solution(1335694842328172053)
XLA Ops:
  0.7 0.9 %copy.13 = f32[64,2,2,64]{3,0,2,1:T(8,128)S(1)} copy(f32[64,2,2,64]{3,2,1,0:T(2,128)} %param.12) | data formatting | bytes 131072 | tf_op args[1]
  1.6 0.7 %copy.14 = f32[3,2,2,64]{3,0,2,1:T(4,128)S(1)} copy(f32[3,2,2,64]{3,2,1,0:T(2,128)} %param.11) | data formatting | bytes 6144 | tf_op args[0]
  2.3 0.1 maximum_bitcast_fusion
  2.5 0.1 fusion.5
  2.6 0.1 pad_maximum_fusion
  2.7 0.5 collective-permute-start
  3.2 0.8 %dynamic_slice.3 = s32[2,2,2]{0,2,1:T(2,128)S(1)} dynamic-slice(s32[8,4,4]{0,2,1:T(4,128)} %param.15, s32[]{:T(128)S(6)} %select_n.78, s32[]{:T(128)S(6)} %select_n.79, s32[]{:T(128)S(6)} %select_n.80), dynamic_slice_sizes={2,2,2} | dynamic-slice | bytes 68 | tf_op jit(solution)/shard_map/dynamic_slice | solution.py:625
  4.0 0.1 copy.16
  4.1 0.1 reshape.31
  4.3 0.1 reshape.32.limits.refs_2_.refs_4_
  4.4 0.1 fusion.4
  4.5 0.1 pad_maximum_fusion.1.core_own.refs_0_.refs_2_
  4.7 2.7 %collective-permute-start.1 = (f32[2,2,72,128]{3,2,1,0:T(8,128)S(1)}, f32[2,2,72,128]{3,2,1,0:T(8,128)S(1)}, u32[]{:S(2)}, u32[]{:S(2)}) collective-permute-start(f32[2,2,72,128]{3,2,1,0:T(8,128)S(1)} %pad_maximum_fusion.2), channel_id=1, source_target_pairs={{0,2},{2,0},{1,3},{3,1},{4,6},{6,4},{5,7},{7,5},{8,10},{10,8},{9,1... | collective-permute-start | bytes 442376 | tf_op jit(solution)/shard_map/ppermute | solution.py:592
  7.5 0.1 reshape.30
  7.7 3.7 %collective-permute-start.2 = (f32[1,2,72,128]{3,2,1,0:T(8,128)S(1)}, f32[1,2,72,128]{3,2,1,0:T(8,128)S(1)}, u32[]{:S(2)}, u32[]{:S(2)}) collective-permute-start(f32[1,2,72,128]{3,2,1,0:T(8,128)S(1)} %get-tuple-element.40), channel_id=1, source_target_pairs={{0,12},{4,8},{8,4},{12,0},{1,13},{5,9},{9,5},{13,1},{2,14},{6,10},... | collective-permute-start | bytes 221192 | tf_op jit(solution)/shard_map/ppermute | solution.py:645
  11.4 0.4 collective-permute-done.1.core_sides.refs_1_.refs_3_
  11.8 1.9 %collective-permute-start.4 = (f32[4,72,128]{2,1,0:T(8,128)S(1)}, f32[4,72,128]{2,1,0:T(8,128)S(1)}, u32[]{:S(2)}, u32[]{:S(2)}) collective-permute-start(f32[4,72,128]{2,1,0:T(8,128)S(1)} %pad_maximum_fusion.3), channel_id=1, source_target_pairs={{0,4},{4,0},{8,12},{12,8},{1,5},{5,1},{9,13},{13,9},{2,6},{6,2},{1... | collective-permute-start | bytes 442376 | tf_op jit(solution)/shard_map/ppermute | solution.py:646
  13.7 0.3 collective-permute-done.2
  14.0 1.3 %collective-permute-start.3 = (f32[1,2,72,128]{3,2,1,0:T(8,128)S(1)}, f32[1,2,72,128]{3,2,1,0:T(8,128)S(1)}, u32[]{:S(2)}, u32[]{:S(2)}) collective-permute-start(f32[1,2,72,128]{3,2,1,0:T(8,128)S(1)} %pad_maximum_fusion.4), channel_id=1, source_target_pairs={{0,2},{2,0},{1,3},{3,1},{4,6},{6,4},{5,7},{7,5},{8,10},{10,8},{9,1... | collective-permute-start | bytes 221192 | tf_op jit(solution)/shard_map/ppermute | solution.py:592
  15.3 0.5 %shard_map.122 = (bf16[608,192]{1,0:T(8,128)(2,1)S(1)}, f32[8,64,128]{2,1,0:T(8,128)S(1)}, f32[2,64,256]{2,1,0:T(8,128)S(1)}, s32[2,24,256]{2,1,0:T(8,128)S(1)}, s32[2,24,256]{2,1,0:T(8,128)S(1)}) custom-call(f32[2,2,72,128]{3,2,1,0:T(8,128)S(1)} %pad_maximum_fusion.1.core_own.refs_0_.refs_2_, ...), custom_call_target="tpu_custom_call" | custom-call | flops 2000000000 | bytes 2000000 | tf_op jit(solution)/shard_map/pallas_call | solution.py:570
  15.9 1.6 %collective-permute-done.4.ghost = f32[4,72,128]{2,1,0:T(8,128)S(1)} collective-permute-done((f32[4,72,128]{2,1,0:T(8,128)S(1)}, f32[4,72,128]{2,1,0:T(8,128)S(1)}, u32[]{:S(2)}, u32[]{:S(2)}) %collective-permute-start.4) | collective-permute-done | bytes 147488 | tf_op jit(solution)/shard_map/ppermute | solution.py:646
  17.5 4.0 %shard_map.123 = (f32[24,64,256]{2,1,0:T(8,128)S(1)}, f32[24,64,256]{2,1,0:T(8,128)S(1)}, f32[24,64,256]{2,1,0:T(8,128)S(1)}, f32[24,64,256]{2,1,0:T(8,128)S(1)}...) custom-call(f32[4,72,128]{2,1,0:T(8,128)S(1)} %collective-permute-done.4.ghost, ...), custom_call_target="tpu_custom_call" | custom-call | flops 5000000000 | bytes 2000000 | tf_op jit(solution)/shard_map/pallas_call | solution.py:575
  21.5 11.6 %shard_map.124 = (f32[3,3,4,128]{3,2,1,0:T(4,128)S(1)}, f32[8,256]{1,0:T(8,128)S(1)}) custom-call(f32[2,72,128]{2,1,0:T(8,128)S(1)} %bitcast.25, f32[2,72,128]{2,1,0:T(8,128)S(1)} %bitcast.26, f32[2,2,72,128]{3,2,1,0:T(8,128)S(1)} %pad_maximum_fusion.1.core_own.refs_0_.refs_2_, f32[2,2,72,128]{3,2,1,0:T(8,128)S(1)} %collective-permute-done.1.core_sides.refs_1_.refs_3_, ...), custom_call_target="tpu_custom_call" | custom-call | flops 12000000000 | bytes 2000000 | tf_op jit(solution)/shard_map/pallas_call | solution.py:584
  33.2 3.6 %collective-permute-start.5 = (f32[3,4,128]{2,1,0:T(4,128)S(1)}, f32[3,4,128]{2,1,0:T(4,128)S(1)}, u32[]{:S(2)}, u32[]{:S(2)}) collective-permute-start(f32[3,4,128]{2,1,0:T(4,128)S(1)} %slice_bitcast_fusion.3), channel_id=1, source_target_pairs={{0,12},{4,8},{8,4},{12,0},{1,13},{5,9},{9,5},{13,1},{2,14},{6,10},... | collective-permute-start | bytes 18440 | tf_op jit(solution)/shard_map/ppermute | solution.py:658
  36.8 7.3 %shard_map.125 = (f32[3,3,4,128]{3,2,1,0:T(4,128)S(1)}, f32[8,256]{1,0:T(8,128)S(1)}) custom-call(bf16[608,192]{1,0:T(8,128)(2,1)S(1)} %get-tuple-element.37.refs_3_.refs_5_.merged, f32[1,64]{1,0:T(1,128)S(1)} %bitcast.30, s32[2,24,256]{2,1,0:T(8,128)S(1)} %get-tuple-element.38.refs_6_.refs_8_.lane_i, ...), custom_call_target="tpu_custom_call" | custom-call | flops 20000000000 | bytes 2000000 | tf_op jit(solution)/shard_map/pallas_call | solution.py:579
  44.2 3.6 %collective-permute-done.6 = f32[3,4,128]{2,1,0:T(4,128)S(1)} collective-permute-done((f32[3,4,128]{2,1,0:T(4,128)S(1)}, f32[3,4,128]{2,1,0:T(4,128)S(1)}, u32[]{:S(2)}, u32[]{:S(2)}) %collective-permute-start.6) | collective-permute-done | bytes 6176 | tf_op jit(solution)/shard_map/ppermute | solution.py:661
  47.9 1.6 %collective-permute-start.7 = (f32[2,3,2,128]{3,2,1,0:T(2,128)S(1)}, f32[2,3,2,128]{3,2,1,0:T(2,128)S(1)}, u32[]{:S(2)}, u32[]{:S(2)}) collective-permute-start(f32[2,3,2,128]{3,2,1,0:T(2,128)S(1)} %pad_maximum_fusion.5), channel_id=1, source_target_pairs={{0,2},{2,0},{1,3},{3,1},{4,6},{6,4},{5,7},{7,5},{8,10},{10,8},{9,1... | collective-permute-start | bytes 18440 | tf_op jit(solution)/shard_map/ppermute | solution.py:592
  49.5 2.1 %collective-permute-done.7 = f32[2,3,2,128]{3,2,1,0:T(2,128)S(1)} collective-permute-done((f32[2,3,2,128]{3,2,1,0:T(2,128)S(1)}, f32[2,3,2,128]{3,2,1,0:T(2,128)S(1)}, u32[]{:S(2)}, u32[]{:S(2)}) %collective-permute-start.7) | collective-permute-done | bytes 6176 | tf_op jit(solution)/shard_map/ppermute | solution.py:592
  51.7 0.1 reshape.33
  51.8 0.6 %slice.105 = f32[2,2,1,64]{3,2,1,0:T(1,128)} slice(f32[2,2,2,64]{3,2,1,0:T(2,128)S(1)} %reshape.33), slice={[0:2], [0:2], [0:1], [0:64]} | slice | bytes 2048 | tf_op jit(solution)/shard_map/slice | solution.py:667
  52.4 0.5 collective-permute-done.8
  53.0 0.6 %copy.18 = f32[3,2,2,64]{3,2,1,0:T(2,128)} copy(f32[3,2,2,64]{3,2,0,1:T(2,128)S(1)} %fusion.1) | data formatting | bytes 6144
  (53 shorter events, 0.8 us)
Async XLA Ops:
  0.6 3.6 %copy-start.7 = (s32[2,2,64]{2,1,0:T(2,128)S(1)}, s32[2,2,64]{2,1,0:T(2,128)}, u32[]{:S(2)}) copy-start(s32[2,2,64]{2,1,0:T(2,128)} %param.14) | copy-start | bytes 3076
  2.5 5.0 %copy-start.6 = (s32[48,2,2,64]{3,2,1,0:T(2,128)S(1)}, s32[48,2,2,64]{3,2,1,0:T(2,128)}, u32[]{:S(2)}) copy-start(s32[48,2,2,64]{3,2,1,0:T(2,128)} %param.13) | copy-start | bytes 147460
  2.7 1.7 %collective-permute-start = (f32[2,2,72,64]{3,2,1,0:T(8,128)S(1)}, f32[2,2,72,64]{3,2,1,0:T(8,128)S(1)}, u32[]{:S(2)}, u32[]{:S(2)}) collective-permute-start(f32[2,2,72,64]{3,2,1,0:T(8,128)S(1)} %pad_maximum_fusion), channel_id=1, source_target_pairs={{0,1},{1,0},{2,3},{3,2},{4,5},{5,4},{6,7},{7,6},{8,9},{9,8},{10,11... | collective-permute-start | bytes 221192 | tf_op jit(solution)/shard_map/ppermute | solution.py:592
  4.3 10.9 %copy-start = (f32[64,64]{1,0:T(8,128)S(1)}, f32[64,64]{1,0:T(8,128)}, u32[]{:S(2)}) copy-start(f32[64,64]{1,0:T(8,128)} %w_self.1) | copy-start | bytes 49156
  4.3 10.9 %copy-start.1 = (f32[64,64]{1,0:T(8,128)S(1)}, f32[64,64]{1,0:T(8,128)}, u32[]{:S(2)}) copy-start(f32[64,64]{1,0:T(8,128)} %w_pair.1) | copy-start | bytes 49156
  4.3 10.9 %copy-start.2 = (f32[64,64]{1,0:T(8,128)S(1)}, f32[64,64]{1,0:T(8,128)}, u32[]{:S(2)}) copy-start(f32[64,64]{1,0:T(8,128)} %w_tensor.1) | copy-start | bytes 49156
  4.3 10.9 %copy-start.3 = (f32[128,64]{0,1:T(8,128)S(1)}, f32[128,64]{0,1:T(8,128)}, u32[]{:S(2)}) copy-start(f32[128,64]{0,1:T(8,128)} %param.20) | copy-start | bytes 98308
  4.4 10.9 %copy-start.4 = (f32[8,64]{1,0:T(8,128)S(1)}, f32[8,64]{1,0:T(8,128)}, u32[]{:S(2)}) copy-start(f32[8,64]{1,0:T(8,128)} %w_radial.1) | copy-start | bytes 6148
  4.4 10.9 %copy-start.5 = (f32[64]{0:T(128)S(1)}, f32[64]{0:T(128)}, u32[]{:S(2)}) copy-start(f32[64]{0:T(128)} %param.21) | copy-start | bytes 772
  4.7 7.1 %collective-permute-start.1 = (f32[2,2,72,128]{3,2,1,0:T(8,128)S(1)}, f32[2,2,72,128]{3,2,1,0:T(8,128)S(1)}, u32[]{:S(2)}, u32[]{:S(2)}) collective-permute-start(f32[2,2,72,128]{3,2,1,0:T(8,128)S(1)} %pad_maximum_fusion.2), channel_id=1, source_target_pairs={{0,2},{2,0},{1,3},{3,1},{4,6},{6,4},{5,7},{7,5},{8,10},{10,8},{9,1... | collective-permute-start | bytes 442376 | tf_op jit(solution)/shard_map/ppermute | solution.py:592
  7.7 6.3 %collective-permute-start.2 = (f32[1,2,72,128]{3,2,1,0:T(8,128)S(1)}, f32[1,2,72,128]{3,2,1,0:T(8,128)S(1)}, u32[]{:S(2)}, u32[]{:S(2)}) collective-permute-start(f32[1,2,72,128]{3,2,1,0:T(8,128)S(1)} %get-tuple-element.40), channel_id=1, source_target_pairs={{0,12},{4,8},{8,4},{12,0},{1,13},{5,9},{9,5},{13,1},{2,14},{6,10},... | collective-permute-start | bytes 221192 | tf_op jit(solution)/shard_map/ppermute | solution.py:645
  11.8 5.7 %collective-permute-start.4 = (f32[4,72,128]{2,1,0:T(8,128)S(1)}, f32[4,72,128]{2,1,0:T(8,128)S(1)}, u32[]{:S(2)}, u32[]{:S(2)}) collective-permute-start(f32[4,72,128]{2,1,0:T(8,128)S(1)} %pad_maximum_fusion.3), channel_id=1, source_target_pairs={{0,4},{4,0},{8,12},{12,8},{1,5},{5,1},{9,13},{13,9},{2,6},{6,2},{1... | collective-permute-start | bytes 442376 | tf_op jit(solution)/shard_map/ppermute | solution.py:646
  14.0 7.5 %collective-permute-start.3 = (f32[1,2,72,128]{3,2,1,0:T(8,128)S(1)}, f32[1,2,72,128]{3,2,1,0:T(8,128)S(1)}, u32[]{:S(2)}, u32[]{:S(2)}) collective-permute-start(f32[1,2,72,128]{3,2,1,0:T(8,128)S(1)} %pad_maximum_fusion.4), channel_id=1, source_target_pairs={{0,2},{2,0},{1,3},{3,1},{4,6},{6,4},{5,7},{7,5},{8,10},{10,8},{9,1... | collective-permute-start | bytes 221192 | tf_op jit(solution)/shard_map/ppermute | solution.py:592
  33.2 10.9 %collective-permute-start.5 = (f32[3,4,128]{2,1,0:T(4,128)S(1)}, f32[3,4,128]{2,1,0:T(4,128)S(1)}, u32[]{:S(2)}, u32[]{:S(2)}) collective-permute-start(f32[3,4,128]{2,1,0:T(4,128)S(1)} %slice_bitcast_fusion.3), channel_id=1, source_target_pairs={{0,12},{4,8},{8,4},{12,0},{1,13},{5,9},{9,5},{13,1},{2,14},{6,10},... | collective-permute-start | bytes 18440 | tf_op jit(solution)/shard_map/ppermute | solution.py:658
  44.1 3.7 %collective-permute-start.6 = (f32[3,4,128]{2,1,0:T(4,128)S(1)}, f32[3,4,128]{2,1,0:T(4,128)S(1)}, u32[]{:S(2)}, u32[]{:S(2)}) collective-permute-start(f32[3,4,128]{2,1,0:T(4,128)S(1)} %slice_bitcast_fusion.2), channel_id=1, source_target_pairs={{0,4},{4,0},{8,12},{12,8},{1,5},{5,1},{9,13},{13,9},{2,6},{6,2},{1... | collective-permute-start | bytes 18440 | tf_op jit(solution)/shard_map/ppermute | solution.py:661
  47.9 3.7 %collective-permute-start.7 = (f32[2,3,2,128]{3,2,1,0:T(2,128)S(1)}, f32[2,3,2,128]{3,2,1,0:T(2,128)S(1)}, u32[]{:S(2)}, u32[]{:S(2)}) collective-permute-start(f32[2,3,2,128]{3,2,1,0:T(2,128)S(1)} %pad_maximum_fusion.5), channel_id=1, source_target_pairs={{0,2},{2,0},{1,3},{3,1},{4,6},{6,4},{5,7},{7,5},{8,10},{10,8},{9,1... | collective-permute-start | bytes 18440 | tf_op jit(solution)/shard_map/ppermute | solution.py:592
  51.7 1.2 %collective-permute-start.8 = (f32[2,3,2,64]{3,2,1,0:T(2,128)S(1)}, f32[2,3,2,64]{3,2,1,0:T(2,128)S(1)}, u32[]{:S(2)}, u32[]{:S(2)}) collective-permute-start(f32[2,3,2,64]{3,2,1,0:T(2,128)S(1)} %pad_maximum_fusion.6), channel_id=1, source_target_pairs={{0,1},{1,0},{2,3},{3,2},{4,5},{5,4},{6,7},{7,6},{8,9},{9,8},{10,11... | collective-permute-start | bytes 9224 | tf_op jit(solution)/shard_map/ppermute | solution.py:592

commit v4 on v3

--- a/solution.py
+++ b/solution.py
@@ -122,8 +122,12 @@
     merged[W_R:W_END, :] = rows.T.astype(bf16)
 
 
-def column_of(own, sides, yc):
-    return sides.at[yc // 3] if yc in (0, 3) else own.at[yc - 1]
+def joined_column(yc, own, sides, own_z, sides_z):
+    mine, theirs = (sides, sides_z) if yc in (0, 3) else (own, own_z)
+    first, second = (96, 32) if yc in (0, 2) else (32, 96)
+    lanes = lane_row()
+    inside = (lanes >= 32) & (lanes < 96)
+    return jnp.where(inside, pltpu.roll(mine[...], first, 1), pltpu.roll(theirs[...], second, 1))
 
 
 def both(x):
@@ -131,8 +135,10 @@
 
 
 def early(
-    core_own,
-    core_sides,
+    own,
+    sides,
+    own_z,
+    sides_z,
     codes,
     limits,
     w_self,
@@ -142,6 +148,7 @@
     mix_t,
     w_out,
     merged,
+    columns,
     pair,
     self_t,
     lane_i,
@@ -149,14 +156,16 @@
 ):
     prepare(w_self, w_pair, w_radial, w_tensor, mix_t, w_out, merged)
     for x in range(2):
-        columns = [column_of(core_own.at[x], core_sides.at[x], yc) for yc in range(4)]
-        rows = jnp.concatenate([column[:FEAT, :] for column in columns], axis=1)
+        blocks = [block.at[x] for block in (own, sides, own_z, sides_z)]
+        for yc in range(4):
+            columns[4 * x + yc] = joined_column(yc, *blocks)
+        rows = jnp.concatenate([columns[4 * x + yc, :FEAT, :] for yc in range(4)], axis=1)
         terms = dot(merged[W_P:W_S, :], stacked(rows))
-        own = dot(merged[W_S:W_R, :], stacked(rows[:, 128:384]))
+        self_terms = dot(merged[W_S:W_R, :], stacked(rows[:, 128:384]))
         for yc in range(4):
             pair[4 * x + yc] = terms[:, 128 * yc : 128 * yc + 128]
         for y in range(2):
-            self_t[x, :, 128 * y : 128 * y + 128] = both(own[:, 128 * y : 128 * y + 128])
+            self_t[x, :, 128 * y : 128 * y + 128] = both(self_terms[:, 128 * y : 128 * y + 128])
         code = codes[x]
         offset = code >> 5
         plane = (offset * 43) >> 7
@@ -172,10 +181,11 @@
     which,
     ghost_own,
     ghost_sides,
-    core_own,
-    core_sides,
+    ghost_own_z,
+    ghost_sides_z,
     limit,
     merged,
+    columns,
     pair,
     self_t,
     lane_i,
@@ -188,6 +198,7 @@
     e_row,
     geo,
     table,
+    ghost,
     step_a,
     step_b,
 ):
@@ -198,10 +209,10 @@
     near_first = 3 if which == 0 else 0
 
     def source(dx, yc):
-        if dx == far_layer:
-            return column_of(ghost_own, ghost_sides, yc)
-        x = dx - 1 + which
-        return column_of(core_own.at[x], core_sides.at[x], yc)
+        return ghost.at[yc] if dx == far_layer else columns.at[4 * (dx - 1 + which) + yc]
+
+    for yc in range(4):
+        ghost[yc] = joined_column(yc, ghost_own, ghost_sides, ghost_own_z, ghost_sides_z)
 
     rows = jnp.concatenate([source(far_layer, yc)[:FEAT, :] for yc in range(4)], axis=1)
     hi, lo = halves(dot(w_p[...], stacked(rows)))
@@ -506,14 +517,16 @@
 
 
 def whole(which, *refs):
-    given, out_row, out, rest = refs[:10], refs[10], refs[11:13], refs[13:]
-    kept, table, steps, rest = rest[:7], rest[7], rest[8:11], rest[11:]
-    front(TOGETHER, which, *given, *kept, table, *steps[:2])
-    rear(TOGETHER, which, given[5], out_row, *given[8:10], None, *kept, *out, *steps, *rest)
-
-
-def opening(which, ghost, *refs):
-    front(ALONE, which, ghost.at[0:2], ghost.at[2:4], *refs)
+    (own, sides), given, out_row, out, rest = refs[:2], refs[2:9], refs[9], refs[10:12], refs[12:]
+    kept, tables, steps, rest = rest[:7], rest[7:9], rest[9:12], rest[12:]
+    ghost = (own.at[0], sides.at[0], own.at[1], sides.at[1])
+    front(TOGETHER, which, *ghost, *given[:1], *given[1:], *kept, *tables, *steps[:2])
+    rear(TOGETHER, which, given[1], out_row, *given[5:7], None, *kept, *out, *steps, *rest)
+
+
+def opening(which, ghost, ghost_z, *refs):
+    blocks = (ghost.at[0], ghost.at[1], ghost_z.at[0], ghost_z.at[1])
+    front(ALONE, which, *blocks, *refs)
 
 
 BIG = (HALF, FEAT, WIDE)
@@ -529,9 +542,10 @@
     ((GEO, HALF, WIDE), f32),
 )
 STEPS = tuple(((STEP, rows, WIDE), f32) for rows in (FEAT, 2 * FEAT + 16, FEAT))
-TABLE = (((2 * FEAT, 4 * 128), bf16),)
+TABLE = (((2 * FEAT, 4 * 128), bf16), ((4, ROWS, 128), f32))
 EARLY = (
     ((W_END, 3 * FEAT), bf16),
+    ((8, ROWS, 128), f32),
     ((8, FEAT, 128), f32),
     ((2, FEAT, WIDE), f32),
     ((2,) + FLAT, jnp.int32),
@@ -592,6 +606,17 @@
         return lax.ppermute(jnp.concatenate([high, low], axis=dim), axis, up)
     parts = [lax.ppermute(high, axis, up), lax.ppermute(low, axis, down)]
     return jnp.concatenate(parts, axis=dim)
+
+
+def neighbours(x, axis, width):
+    size = lax.axis_size(axis)
+    up = [(i, (i + 1) % size) for i in range(size)]
+    if size == 2:
+        return lax.ppermute(x, axis, up)
+    below = lax.ppermute(x, axis, up)
+    above = lax.ppermute(x, axis, [(j, i) for i, j in up])
+    lane = jnp.arange(x.shape[-1], dtype=jnp.int32)
+    return jnp.where(lane % (2 * width) < width, above, below)
 
 
 def local(
@@ -619,9 +644,19 @@
         return jnp.where(odd, x[::-1], x)
 
     fill = jnp.zeros((ROWS - FEAT - 3,) + positions.shape[1:], f32)
-    state = jnp.concatenate([features, positions, fill], axis=0).transpose(1, 2, 0, 3)
-    state = mirrored(state)
-    ends = exchange(state[..., :SLOTS], state[..., -SLOTS:], "gz", 3)
+    state = jnp.concatenate([features, positions, fill], axis=0).transpose(1, 0, 2, 3)
+    state = mirrored(state.reshape(cells_x, ROWS, cells_y * lanes))
+    state_z = neighbours(state, "gz", SLOTS)
+    size = lax.axis_size("gx")
+    first = [(i, i + 1 - 2 * (i % 2)) for i in range(size)]
+    second = [(i, (i - 1 + 2 * (i % 2)) % size) for i in range(size)]
+    sides = neighbours(state, "gy", lanes)
+    outer = lax.ppermute(state[0], "gx", second)
+    inner = lax.ppermute(jnp.stack([state[1], sides[1]]), "gx", first)
+    sides_z = neighbours(sides, "gz", SLOTS)
+    sides_z, nbr_index, nbr_count, bin_counts = lax.optimization_barrier(
+        (sides_z, nbr_index, nbr_count, bin_counts)
+    )
     own_counts = lax.dynamic_slice(
         bin_counts,
         (x_index * cells_x, y_index * cells_y, z_index * cells_z),
@@ -632,31 +667,21 @@
     limit = mirrored(limit) + MIRRORED * odd.astype(jnp.int32)
     limit = jnp.broadcast_to(limit[:, :, None, :], (cells_x, cells_y, 2, lanes))
     limit = limit.reshape(cells_x, 1, WIDE)
-    ends, nbr_index = lax.optimization_barrier((ends, nbr_index))
-    state = jnp.concatenate([ends[..., :SLOTS], state, ends[..., SLOTS:]], axis=-1)
-
-    size = lax.axis_size("gx")
-    first = [(i, i + 1 - 2 * (i % 2)) for i in range(size)]
-    second = [(i, (i - 1 + 2 * (i % 2)) % size) for i in range(size)]
-    sides = exchange(state[:, :1], state[:, -1:], "gy", 1)
     codes = nbr_index.reshape(2, HALF, cells_x, cells_y, lanes)
     codes = mirrored(codes.transpose(2, 1, 3, 0, 4).reshape(cells_x, HALF, WIDE))
-    outer_own, codes = lax.optimization_barrier((state[:1], codes))
-    outer_own = lax.ppermute(outer_own, "gx", second)
-    inner = lax.ppermute(jnp.concatenate([state[1], sides[1]]), "gx", first)
+    inner_z = neighbours(inner, "gz", SLOTS)
     out_row = w_out[None]
     weights = (w_self, w_pair, w_radial, w_tensor, w_mix.T, out_row)
-    merged, *decoded = run_early(state, sides, codes, limit, *weights)
-    outer_own, late_sides = lax.optimization_barrier((outer_own, sides))
-    outer_sides = exchange(outer_own[:, :1], outer_own[:, -1:], "gy", 1)[0]
-
-    kept = run_front(1, inner, state, sides, limit, merged, *decoded)
-    late_sides, kept = lax.optimization_barrier((late_sides, kept))
-    grad0, energy0 = run_whole(
-        0, outer_own[0], outer_sides, state, late_sides, limit, merged, *decoded, out_row
-    )
+    merged, *decoded = run_early(state, sides, state_z, sides_z, codes, limit, *weights)
+    outer, codes, limit = lax.optimization_barrier((outer, codes, limit))
+    outer_own = jnp.stack([outer, neighbours(outer, "gz", SLOTS)])
+    outer_sides = neighbours(outer_own, "gy", lanes)
+
+    kept = run_front(1, inner, inner_z, limit, merged, *decoded)
+    late_limit, kept = lax.optimization_barrier((limit, kept))
+    grad0, energy0 = run_whole(0, outer_own, outer_sides, late_limit, merged, *decoded, out_row)
     back0 = lax.ppermute(grad0[0], "gx", second)
-    grad1, energy1 = run_rear(1, merged, out_row, *decoded[2:], grad0, *kept)
+    grad1, energy1 = run_rear(1, merged, out_row, *decoded[3:], grad0, *kept)
     grad1, back0 = lax.optimization_barrier((grad1, back0))
     back1 = lax.ppermute(grad1[2], "gx", first)
     grad = grad1[:2] + jnp.stack([back0, back1])

time: 53.8 us -> 51.1 us (0.950)
  starting transfers between devices: 15.4 us -> 12.8 us
  local copies, waits for them, and re-layouts: 4.71 us -> 3.93 us
  other arithmetic: 0.62 us -> 1.31 us
    ppermute x5 -> x2, starting transfers between devices: 6.13 us -> 0.69 us  [exchange(): return lax.ppermute(jnp.concatenate([high, low], axis=dim), axis, up)]
    ppermute x2 -> x8, starting transfers between devices: 5.56 us -> 8.39 us  [the longest x6 4.06 us: neighbours(): return lax.ppermute(x, axis, up)]
    unnamed x19 -> x15, local copies, waits for them, and re-layouts: 2.25 us -> 0.63 us
    transpose x1, other arithmetic: 0.08 us -> 1.06 us  [local(): jnp.concatenate([features, positions, fill], axis=0).transpose(1, 0, 2, 3)]
    reshape x1, local copies, waits for them, and re-layouts: 0.08 us -> 0.97 us  [local(): codes = nbr_index.reshape(2, HALF, cells_x, cells_y, lanes)]
    ppermute x5 -> x2, waiting for transfers between devices: 2.96 us -> 3.4 us  [exchange(): return lax.ppermute(jnp.concatenate([high, low], axis=dim), axis, up)]
    ppermute x2 -> x8, waiting for transfers between devices: 1.86 us -> 1.49 us  [the longest x1 1.05 us: local(): inner = lax.ppermute(jnp.stack([state[1], sides[1]]), 'gx', first)]
  transfers between devices with their start and end apart: 9 -> 12, of which waited for: 6 -> 5; matrix products, arithmetic and copies ran while one was open for 4% -> 6% of each run, Pallas kernels for 22% -> 23%
where the time goes in v4:
time: 51.1 us; the launch traced here: 50.9 us
  Pallas kernels  23.4 us (46%)
  starting transfers between devices  12.8 us (25%)
  waiting for transfers between devices  8.49 us (17%)
  local copies, waits for them, and re-layouts  3.93 us (8%)
  other arithmetic  1.31 us (3%)
  between operations  0.95 us (2%)
    pallas_call x1, Pallas kernels, run_whole(): call(functools.partial(whole, which), RESULT, scratch, 12, 28)(*given)  11.6 us
    pallas_call x1, Pallas kernels, run_rear(): call(functools.partial(rear, ALONE, which), RESULT, in_vmem(STEPS + REAR)...  7.25 us
    ppermute x6, starting transfers between devices, neighbours(): return lax.ppermute(x, axis, up)  4.06 us
    pallas_call x1, Pallas kernels, run_front(): call(functools.partial(opening, which), shaped(KEPT), scratch, 5, 16)  4.03 us
    ppermute x1, starting transfers between devices, local(): back0 = lax.ppermute(grad0[0], 'gx', second)  3.67 us
    ppermute x1, starting transfers between devices, local(): outer = lax.ppermute(state[0], 'gx', second)  3.67 us
    ppermute x1, waiting for transfers between devices, local(): back1 = lax.ppermute(grad1[2], 'gx', first)  3.59 us
    ppermute x2, waiting for transfers between devices, exchange(): return lax.ppermute(jnp.concatenate([high, low], axis=dim), axis, up)  3.4 us
  transfers between devices with their start and end apart: 12, of which 5 were waited for; matrix products, arithmetic and copies ran while one was open for 6% of the time, Pallas kernels for 23%

profile of v4, /device:TPU:0, one launch (start us, length us, event | category | flops | bytes accessed | tf_op | source)
XLA Modules:
  0.0 50.9 jit_solution(12797031441263267853)
XLA Ops:
  0.7 0.1 pad.14.clone
  0.8 1.1 %maximum_bitcast_fusion = f32[2,72,2,64]{3,2,0,1:T(2,128)S(1)} fusion(f32[3,2,2,64]{3,2,1,0:T(2,128)} %param.11, f32[64,2,2,64]{3,2,1,0:T(2,128)} %param.12, f32[72]{0:T(128)S(1)} %pad.14.clone), kind=kLoop, calls=%fused_computation | loop fusion | flops 36864 | bytes 142624 | tf_op jit(solution)/shard_map/transpose | solution.py:647
  1.9 0.2 reshape.38
  2.1 3.0 %collective-permute-start = (f32[2,72,128]{2,1,0:T(8,128)S(1)}, f32[2,72,128]{2,1,0:T(8,128)S(1)}, u32[]{:S(2)}, u32[]{:S(2)}) collective-permute-start(f32[2,72,128]{2,1,0:T(8,128)S(1)} %reverse_select_fusion.own), channel_id=1, source_target_pairs={{0,2},{2,0},{1,3},{3,1},{4,6},{6,4},{5,7},{7,5},{8,10},{10,8},{9,1... | collective-permute-start | bytes 221192 | tf_op jit(solution)/shard_map/ppermute | solution.py:615
  5.1 3.7 %collective-permute-start.3 = (f32[72,128]{1,0:T(8,128)S(1)}, f32[72,128]{1,0:T(8,128)S(1)}, u32[]{:S(2)}, u32[]{:S(2)}) collective-permute-start(f32[72,128]{1,0:T(8,128)S(1)} %get-tuple-element.73), channel_id=1, source_target_pairs={{0,12},{4,8},{8,4},{12,0},{1,13},{5,9},{9,5},{13,1},{2,14},{6,10},... | collective-permute-start | bytes 110600 | tf_op jit(solution)/shard_map/ppermute | solution.py:654
  8.7 0.2 collective-permute-start.2
  8.9 0.7 %collective-permute-start.6 = (f32[2,72,128]{2,1,0:T(8,128)S(1)}, f32[2,72,128]{2,1,0:T(8,128)S(1)}, u32[]{:S(2)}, u32[]{:S(2)}) collective-permute-start(f32[2,72,128]{2,1,0:T(8,128)S(1)} %pad_maximum_fusion.1), channel_id=1, source_target_pairs={{0,4},{4,0},{8,12},{12,8},{1,5},{5,1},{9,13},{13,9},{2,6},{6,2},{1... | collective-permute-start | bytes 221192 | tf_op jit(solution)/shard_map/ppermute | solution.py:655
  9.6 0.4 collective-permute-done.2.sides_z
  10.0 0.8 %dynamic_slice.3 = s32[2,2,2]{0,2,1:T(2,128)S(1)} dynamic-slice(s32[8,4,4]{0,2,1:T(4,128)} %param.15, s32[]{:T(128)S(6)} %select_n.78, s32[]{:T(128)S(6)} %select_n.79, s32[]{:T(128)S(6)} %select_n.80), dynamic_slice_sizes={2,2,2} | dynamic-slice | bytes 68 | tf_op jit(solution)/shard_map/dynamic_slice | solution.py:660
  10.8 0.1 copy.20
  11.0 0.1 reshape.35
  11.0 1.0 %copy.26 = s32[2,24,2,2,64]{4,0,3,1,2:T(2,128)S(1)} copy(s32[2,24,2,2,64]{4,3,2,1,0:T(2,128)} %bitcast.30) | data formatting | bytes 98304 | tf_op jit(solution)/shard_map/reshape | solution.py:670
  12.0 0.1 reshape.34
  12.2 0.1 reshape.36.limits.refs_0_.refs_2_
  12.3 0.2 collective-permute-start.4
  12.5 1.0 %collective-permute-done.6.ghost = f32[2,72,128]{2,1,0:T(8,128)S(1)} collective-permute-done((f32[2,72,128]{2,1,0:T(8,128)S(1)}, f32[2,72,128]{2,1,0:T(8,128)S(1)}, u32[]{:S(2)}, u32[]{:S(2)}) %collective-permute-start.6) | collective-permute-done | bytes 73760 | tf_op jit(solution)/shard_map/ppermute | solution.py:655
  13.6 0.6 %shard_map.122 = (bf16[608,192]{1,0:T(8,128)(2,1)S(1)}, f32[8,72,128]{2,1,0:T(8,128)S(1)}, f32[8,64,128]{2,1,0:T(8,128)S(1)}, f32[2,64,256]{2,1,0:T(8,128)S(1)},...) custom-call(f32[2,72,128]{2,1,0:T(8,128)S(1)} %reverse_select_fusion.own, ...), custom_call_target="tpu_custom_call" | custom-call | flops 2000000000 | bytes 2000000 | tf_op jit(solution)/shard_map/pallas_call | solution.py:584
  14.2 0.7 %collective-permute-start.5 = (f32[2,72,128]{2,1,0:T(8,128)S(1)}, f32[2,72,128]{2,1,0:T(8,128)S(1)}, u32[]{:S(2)}, u32[]{:S(2)}) collective-permute-start(f32[2,72,128]{2,1,0:T(8,128)S(1)} %pad_maximum_fusion.refs_0_), channel_id=1, source_target_pairs={{0,2},{2,0},{1,3},{3,1},{4,6},{6,4},{5,7},{7,5},{8,10},{10,8},{9,1... | collective-permute-start | bytes 221192 | tf_op jit(solution)/shard_map/ppermute | solution.py:615
  14.9 4.0 %shard_map.123 = (f32[24,64,256]{2,1,0:T(8,128)S(1)}, f32[24,64,256]{2,1,0:T(8,128)S(1)}, f32[24,64,256]{2,1,0:T(8,128)S(1)}, f32[24,64,256]{2,1,0:T(8,128)S(1)}...) custom-call(f32[2,72,128]{2,1,0:T(8,128)S(1)} %collective-permute-done.6.ghost, ...), custom_call_target="tpu_custom_call" | custom-call | flops 5000000000 | bytes 2000000 | tf_op jit(solution)/shard_map/pallas_call | solution.py:589
  19.0 11.6 %shard_map.124 = (f32[3,3,4,128]{3,2,1,0:T(4,128)S(1)}, f32[8,256]{1,0:T(8,128)S(1)}) custom-call(f32[2,72,128]{2,1,0:T(8,128)S(1)} %pad_maximum_fusion.refs_0_, f32[2,72,128]{2,1,0:T(8,128)S(1)} %collective-permute-done.5.refs_1_, s32[2,1,256]{2,1,0:T(1,128)S(1)} %reshape.36.limits.refs_0_.refs_2_, ...), custom_call_target="tpu_custom_call" | custom-call | flops 12000000000 | bytes 2000000 | tf_op jit(solution)/shard_map/pallas_call | solution.py:598
  30.6 3.7 %collective-permute-start.8 = (f32[3,4,128]{2,1,0:T(4,128)S(1)}, f32[3,4,128]{2,1,0:T(4,128)S(1)}, u32[]{:S(2)}, u32[]{:S(2)}) collective-permute-start(f32[3,4,128]{2,1,0:T(4,128)S(1)} %slice_bitcast_fusion.2), channel_id=1, source_target_pairs={{0,12},{4,8},{8,4},{12,0},{1,13},{5,9},{9,5},{13,1},{2,14},{6,10},... | collective-permute-start | bytes 18440 | tf_op jit(solution)/shard_map/ppermute | solution.py:683
  34.2 7.2 %shard_map.125 = (f32[3,3,4,128]{3,2,1,0:T(4,128)S(1)}, f32[8,256]{1,0:T(8,128)S(1)}) custom-call(bf16[608,192]{1,0:T(8,128)(2,1)S(1)} %get-tuple-element.39.refs_1_.refs_3_.merged, f32[1,64]{1,0:T(1,128)S(1)} %bitcast.28, s32[2,24,256]{2,1,0:T(8,128)S(1)} %get-tuple-element.40.refs_5_.refs_7_.lane_i, ...), custom_call_target="tpu_custom_call" | custom-call | flops 20000000000 | bytes 2000000 | tf_op jit(solution)/shard_map/pallas_call | solution.py:593
  41.6 3.6 %collective-permute-done.9 = f32[3,4,128]{2,1,0:T(4,128)S(1)} collective-permute-done((f32[3,4,128]{2,1,0:T(4,128)S(1)}, f32[3,4,128]{2,1,0:T(4,128)S(1)}, u32[]{:S(2)}, u32[]{:S(2)}) %collective-permute-start.9) | collective-permute-done | bytes 6176 | tf_op jit(solution)/shard_map/ppermute | solution.py:686
  45.2 0.7 %collective-permute-start.10 = (f32[2,3,2,128]{3,2,1,0:T(2,128)S(1)}, f32[2,3,2,128]{3,2,1,0:T(2,128)S(1)}, u32[]{:S(2)}, u32[]{:S(2)}) collective-permute-start(f32[2,3,2,128]{3,2,1,0:T(2,128)S(1)} %pad_maximum_fusion.2), channel_id=1, source_target_pairs={{0,2},{2,0},{1,3},{3,1},{4,6},{6,4},{5,7},{7,5},{8,10},{10,8},{9,1... | collective-permute-start | bytes 18440 | tf_op jit(solution)/shard_map/ppermute | solution.py:606
  46.0 2.9 %collective-permute-done.10 = f32[2,3,2,128]{3,2,1,0:T(2,128)S(1)} collective-permute-done((f32[2,3,2,128]{3,2,1,0:T(2,128)S(1)}, f32[2,3,2,128]{3,2,1,0:T(2,128)S(1)}, u32[]{:S(2)}, u32[]{:S(2)}) %collective-permute-start.10) | collective-permute-done | bytes 6176 | tf_op jit(solution)/shard_map/ppermute | solution.py:606
  48.9 0.1 fusion.5
  49.0 0.1 pad_maximum_fusion.3
  49.1 0.1 reshape.37
  49.2 0.6 %slice.69 = f32[2,2,1,64]{3,2,1,0:T(1,128)} slice(f32[2,2,2,64]{3,2,1,0:T(2,128)S(1)} %reshape.37), slice={[0:2], [0:2], [0:1], [0:64]} | slice | bytes 2048 | tf_op jit(solution)/shard_map/slice | solution.py:692
  49.8 0.5 collective-permute-done.11
  50.3 0.1 slice_add_fusion
  50.3 0.6 %copy.22 = f32[3,2,2,64]{3,2,1,0:T(2,128)} copy(f32[3,2,2,64]{3,2,0,1:T(2,128)S(1)} %fusion.1) | data formatting | bytes 6144
  (50 shorter events, 0.4 us)
Async XLA Ops:
  0.6 11.5 %copy-start.6 = (s32[2,2,64]{2,1,0:T(2,128)S(1)}, s32[2,2,64]{2,1,0:T(2,128)}, u32[]{:S(2)}) copy-start(s32[2,2,64]{2,1,0:T(2,128)} %param.14) | copy-start | bytes 3076
  0.6 12.9 %copy-start.5 = (f32[64]{0:T(128)S(1)}, f32[64]{0:T(128)}, u32[]{:S(2)}) copy-start(f32[64]{0:T(128)} %param.21) | copy-start | bytes 772
  0.7 12.9 %copy-start.3 = (f32[128,64]{0,1:T(8,128)S(1)}, f32[128,64]{0,1:T(8,128)}, u32[]{:S(2)}) copy-start(f32[128,64]{0,1:T(8,128)} %param.20) | copy-start | bytes 98308
  0.7 12.9 %copy-start = (f32[64,64]{1,0:T(8,128)S(1)}, f32[64,64]{1,0:T(8,128)}, u32[]{:S(2)}) copy-start(f32[64,64]{1,0:T(8,128)} %w_self.1) | copy-start | bytes 49156
  0.7 12.9 %copy-start.1 = (f32[64,64]{1,0:T(8,128)S(1)}, f32[64,64]{1,0:T(8,128)}, u32[]{:S(2)}) copy-start(f32[64,64]{1,0:T(8,128)} %w_pair.1) | copy-start | bytes 49156
  0.7 12.9 %copy-start.4 = (f32[8,64]{1,0:T(8,128)S(1)}, f32[8,64]{1,0:T(8,128)}, u32[]{:S(2)}) copy-start(f32[8,64]{1,0:T(8,128)} %w_radial.1) | copy-start | bytes 6148
  0.7 12.9 %copy-start.2 = (f32[64,64]{1,0:T(8,128)S(1)}, f32[64,64]{1,0:T(8,128)}, u32[]{:S(2)}) copy-start(f32[64,64]{1,0:T(8,128)} %w_tensor.1) | copy-start | bytes 49156
  2.1 6.7 %collective-permute-start = (f32[2,72,128]{2,1,0:T(8,128)S(1)}, f32[2,72,128]{2,1,0:T(8,128)S(1)}, u32[]{:S(2)}, u32[]{:S(2)}) collective-permute-start(f32[2,72,128]{2,1,0:T(8,128)S(1)} %reverse_select_fusion.own), channel_id=1, source_target_pairs={{0,2},{2,0},{1,3},{3,1},{4,6},{6,4},{5,7},{7,5},{8,10},{10,8},{9,1... | collective-permute-start | bytes 221192 | tf_op jit(solution)/shard_map/ppermute | solution.py:615
  5.1 8.5 %collective-permute-start.1 = (f32[2,72,128]{2,1,0:T(8,128)S(1)}, f32[2,72,128]{2,1,0:T(8,128)S(1)}, u32[]{:S(2)}, u32[]{:S(2)}) collective-permute-start(f32[2,72,128]{2,1,0:T(8,128)S(1)} %reverse_select_fusion.own), channel_id=1, source_target_pairs={{0,1},{1,0},{2,3},{3,2},{4,5},{5,4},{6,7},{7,6},{8,9},{9,8},{10,11... | collective-permute-start | bytes 221192 | tf_op jit(solution)/shard_map/ppermute | solution.py:615
  5.1 7.2 %collective-permute-start.3 = (f32[72,128]{1,0:T(8,128)S(1)}, f32[72,128]{1,0:T(8,128)S(1)}, u32[]{:S(2)}, u32[]{:S(2)}) collective-permute-start(f32[72,128]{1,0:T(8,128)S(1)} %get-tuple-element.73), channel_id=1, source_target_pairs={{0,12},{4,8},{8,4},{12,0},{1,13},{5,9},{9,5},{13,1},{2,14},{6,10},... | collective-permute-start | bytes 110600 | tf_op jit(solution)/shard_map/ppermute | solution.py:654
  8.7 1.3 %collective-permute-start.2 = (f32[2,72,128]{2,1,0:T(8,128)S(1)}, f32[2,72,128]{2,1,0:T(8,128)S(1)}, u32[]{:S(2)}, u32[]{:S(2)}) collective-permute-start(f32[2,72,128]{2,1,0:T(8,128)S(1)} %collective-permute-done.sides), channel_id=1, source_target_pairs={{0,1},{1,0},{2,3},{3,2},{4,5},{5,4},{6,7},{7,6},{8,9},{9,8},{10,11... | collective-permute-start | bytes 221192 | tf_op jit(solution)/shard_map/ppermute | solution.py:615
  8.9 4.6 %collective-permute-start.6 = (f32[2,72,128]{2,1,0:T(8,128)S(1)}, f32[2,72,128]{2,1,0:T(8,128)S(1)}, u32[]{:S(2)}, u32[]{:S(2)}) collective-permute-start(f32[2,72,128]{2,1,0:T(8,128)S(1)} %pad_maximum_fusion.1), channel_id=1, source_target_pairs={{0,4},{4,0},{8,12},{12,8},{1,5},{5,1},{9,13},{13,9},{2,6},{6,2},{1... | collective-permute-start | bytes 221192 | tf_op jit(solution)/shard_map/ppermute | solution.py:655
  12.3 1.9 %collective-permute-start.4 = (f32[72,128]{1,0:T(8,128)S(1)}, f32[72,128]{1,0:T(8,128)S(1)}, u32[]{:S(2)}, u32[]{:S(2)}) collective-permute-start(f32[72,128]{1,0:T(8,128)S(1)} %collective-permute-done.3), channel_id=1, source_target_pairs={{0,1},{1,0},{2,3},{3,2},{4,5},{5,4},{6,7},{7,6},{8,9},{9,8},{10,11... | collective-permute-start | bytes 110600 | tf_op jit(solution)/shard_map/ppermute | solution.py:615
  13.5 1.4 %collective-permute-start.7 = (f32[2,72,128]{2,1,0:T(8,128)S(1)}, f32[2,72,128]{2,1,0:T(8,128)S(1)}, u32[]{:S(2)}, u32[]{:S(2)}) collective-permute-start(f32[2,72,128]{2,1,0:T(8,128)S(1)} %collective-permute-done.6.ghost), channel_id=1, source_target_pairs={{0,1},{1,0},{2,3},{3,2},{4,5},{5,4},{6,7},{7,6},{8,9},{9,8},{10,11... | collective-permute-start | bytes 221192 | tf_op jit(solution)/shard_map/ppermute | solution.py:615
  14.2 4.8 %collective-permute-start.5 = (f32[2,72,128]{2,1,0:T(8,128)S(1)}, f32[2,72,128]{2,1,0:T(8,128)S(1)}, u32[]{:S(2)}, u32[]{:S(2)}) collective-permute-start(f32[2,72,128]{2,1,0:T(8,128)S(1)} %pad_maximum_fusion.refs_0_), channel_id=1, source_target_pairs={{0,2},{2,0},{1,3},{3,1},{4,6},{6,4},{5,7},{7,5},{8,10},{10,8},{9,1... | collective-permute-start | bytes 221192 | tf_op jit(solution)/shard_map/ppermute | solution.py:615
  30.6 10.9 %collective-permute-start.8 = (f32[3,4,128]{2,1,0:T(4,128)S(1)}, f32[3,4,128]{2,1,0:T(4,128)S(1)}, u32[]{:S(2)}, u32[]{:S(2)}) collective-permute-start(f32[3,4,128]{2,1,0:T(4,128)S(1)} %slice_bitcast_fusion.2), channel_id=1, source_target_pairs={{0,12},{4,8},{8,4},{12,0},{1,13},{5,9},{9,5},{13,1},{2,14},{6,10},... | collective-permute-start | bytes 18440 | tf_op jit(solution)/shard_map/ppermute | solution.py:683
  41.5 3.7 %collective-permute-start.9 = (f32[3,4,128]{2,1,0:T(4,128)S(1)}, f32[3,4,128]{2,1,0:T(4,128)S(1)}, u32[]{:S(2)}, u32[]{:S(2)}) collective-permute-start(f32[3,4,128]{2,1,0:T(4,128)S(1)} %slice_bitcast_fusion.1), channel_id=1, source_target_pairs={{0,4},{4,0},{8,12},{12,8},{1,5},{5,1},{9,13},{13,9},{2,6},{6,2},{1... | collective-permute-start | bytes 18440 | tf_op jit(solution)/shard_map/ppermute | solution.py:686
  45.2 3.7 %collective-permute-start.10 = (f32[2,3,2,128]{3,2,1,0:T(2,128)S(1)}, f32[2,3,2,128]{3,2,1,0:T(2,128)S(1)}, u32[]{:S(2)}, u32[]{:S(2)}) collective-permute-start(f32[2,3,2,128]{3,2,1,0:T(2,128)S(1)} %pad_maximum_fusion.2), channel_id=1, source_target_pairs={{0,2},{2,0},{1,3},{3,1},{4,6},{6,4},{5,7},{7,5},{8,10},{10,8},{9,1... | collective-permute-start | bytes 18440 | tf_op jit(solution)/shard_map/ppermute | solution.py:606
  49.1 1.2 %collective-permute-start.11 = (f32[2,3,2,64]{3,2,1,0:T(2,128)S(1)}, f32[2,3,2,64]{3,2,1,0:T(2,128)S(1)}, u32[]{:S(2)}, u32[]{:S(2)}) collective-permute-start(f32[2,3,2,64]{3,2,1,0:T(2,128)S(1)} %pad_maximum_fusion.3), channel_id=1, source_target_pairs={{0,1},{1,0},{2,3},{3,2},{4,5},{5,4},{6,7},{7,6},{8,9},{9,8},{10,11... | collective-permute-start | bytes 9224 | tf_op jit(solution)/shard_map/ppermute | solution.py:606

commit v5 on v4

--- a/solution.py
+++ b/solution.py
@@ -475,9 +475,8 @@
     g_row[:, 7, :] = zero
 
     s_acc[...] = jnp.zeros_like(s_acc)
-    places = lax.broadcasted_iota(jnp.int32, (128, 128), 0)
-
-    @pl.loop(0, HALF // 4, unroll=3)
+
+    @pl.loop(0, HALF // 4, unroll=6)
     def scatter(q):
         for y in range(2):
             side = slice(128 * y, 128 * y + 128)
@@ -492,7 +491,7 @@
                         [jnp.where(col == c, tile, 0.0) for c in range(9)], axis=0
                     ).astype(bf16)
                 )
-                right.append((places == lane).astype(f32).astype(bf16))
+                right.append(one_hot(lane, 128))
             s_acc[y] += lax.dot_general(
                 jnp.concatenate(left, axis=1),
                 jnp.concatenate(right, axis=1),
@@ -669,11 +668,12 @@
     limit = limit.reshape(cells_x, 1, WIDE)
     codes = nbr_index.reshape(2, HALF, cells_x, cells_y, lanes)
     codes = mirrored(codes.transpose(2, 1, 3, 0, 4).reshape(cells_x, HALF, WIDE))
-    inner_z = neighbours(inner, "gz", SLOTS)
+    outer, codes, limit = lax.optimization_barrier((outer, codes, limit))
     out_row = w_out[None]
     weights = (w_self, w_pair, w_radial, w_tensor, w_mix.T, out_row)
     merged, *decoded = run_early(state, sides, state_z, sides_z, codes, limit, *weights)
-    outer, codes, limit = lax.optimization_barrier((outer, codes, limit))
+    inner, merged = lax.optimization_barrier((inner, merged))
+    inner_z = neighbours(inner, "gz", SLOTS)
     outer_own = jnp.stack([outer, neighbours(outer, "gz", SLOTS)])
     outer_sides = neighbours(outer_own, "gy", lanes)
 

time: 51.1 us -> 49.7 us (0.973)
  waiting for transfers between devices: 8.49 us -> 7.39 us
  Pallas kernels: 23.4 us -> 22.7 us
    ppermute x1, waiting for transfers between devices: 1.05 us -> 0.41 us  [local(): inner = lax.ppermute(jnp.stack([state[1], sides[1]]), 'gx', first)]
    pallas_call x1, Pallas kernels: 11.6 us -> 11 us  [run_whole(): call(functools.partial(whole, which), RESULT, scratch, 12, 28)(*given)]
    ppermute x2, waiting for transfers between devices: 3.4 us -> 2.84 us  [exchange(): return lax.ppermute(jnp.concatenate([high, low], axis=dim), axis, up)]
    ppermute x2, starting transfers between devices: 0.69 us -> 1.26 us  [exchange(): return lax.ppermute(jnp.concatenate([high, low], axis=dim), axis, up)]
    ppermute x1, starting transfers between devices: 3.67 us -> 3.16 us  [local(): back0 = lax.ppermute(grad0[0], 'gx', second)]
  transfers between devices with their start and end apart: 12 -> 12, of which waited for: 5 -> 6; matrix products, arithmetic and copies ran while one was open for 6% -> 6% of each run, Pallas kernels for 23% -> 24%
where the time goes in v5:
time: 49.7 us; the launch traced here: 49.5 us
  Pallas kernels  22.7 us (46%)
  starting transfers between devices  13.3 us (27%)
  waiting for transfers between devices  7.39 us (15%)
  local copies, waits for them, and re-layouts  3.93 us (8%)
  other arithmetic  1.31 us (3%)
  between operations  0.95 us (2%)
    pallas_call x1, Pallas kernels, run_whole(): call(functools.partial(whole, which), RESULT, scratch, 12, 28)(*given)  11 us
    pallas_call x1, Pallas kernels, run_rear(): call(functools.partial(rear, ALONE, which), RESULT, in_vmem(STEPS + REAR)...  7.05 us
    ppermute x6, starting transfers between devices, neighbours(): return lax.ppermute(x, axis, up)  4.48 us
    pallas_call x1, Pallas kernels, run_front(): call(functools.partial(opening, which), shaped(KEPT), scratch, 5, 16)  4.03 us
    ppermute x1, starting transfers between devices, local(): outer = lax.ppermute(state[0], 'gx', second)  3.67 us
    ppermute x1, waiting for transfers between devices, local(): back1 = lax.ppermute(grad1[2], 'gx', first)  3.59 us
    ppermute x1, starting transfers between devices, local(): back0 = lax.ppermute(grad0[0], 'gx', second)  3.16 us
    ppermute x2, waiting for transfers between devices, exchange(): return lax.ppermute(jnp.concatenate([high, low], axis=dim), axis, up)  2.84 us
  transfers between devices with their start and end apart: 12, of which 6 were waited for; matrix products, arithmetic and copies ran while one was open for 6% of the time, Pallas kernels for 24%

profile of v5, /device:TPU:0, one launch (start us, length us, event | category | flops | bytes accessed | tf_op | source)
XLA Modules:
  0.0 49.5 jit_solution(2088542781320405300)
XLA Ops:
  0.7 0.1 pad.14.clone
  0.8 1.1 %maximum_bitcast_fusion = f32[2,72,2,64]{3,2,0,1:T(2,128)S(1)} fusion(f32[3,2,2,64]{3,2,1,0:T(2,128)} %param.11, f32[64,2,2,64]{3,2,1,0:T(2,128)} %param.12, f32[72]{0:T(128)S(1)} %pad.14.clone), kind=kLoop, calls=%fused_computation | loop fusion | flops 36864 | bytes 142624 | tf_op jit(solution)/shard_map/transpose | solution.py:646
  1.9 0.2 reshape.38
  2.1 3.0 %collective-permute-start = (f32[2,72,128]{2,1,0:T(8,128)S(1)}, f32[2,72,128]{2,1,0:T(8,128)S(1)}, u32[]{:S(2)}, u32[]{:S(2)}) collective-permute-start(f32[2,72,128]{2,1,0:T(8,128)S(1)} %reverse_select_fusion.own), channel_id=1, source_target_pairs={{0,2},{2,0},{1,3},{3,1},{4,6},{6,4},{5,7},{7,5},{8,10},{10,8},{9,1... | collective-permute-start | bytes 221192 | tf_op jit(solution)/shard_map/ppermute | solution.py:614
  5.1 3.7 %collective-permute-start.4 = (f32[72,128]{1,0:T(8,128)S(1)}, f32[72,128]{1,0:T(8,128)S(1)}, u32[]{:S(2)}, u32[]{:S(2)}) collective-permute-start(f32[72,128]{1,0:T(8,128)S(1)} %get-tuple-element.78), channel_id=1, source_target_pairs={{0,12},{4,8},{8,4},{12,0},{1,13},{5,9},{9,5},{13,1},{2,14},{6,10},... | collective-permute-start | bytes 110600 | tf_op jit(solution)/shard_map/ppermute | solution.py:653
  8.7 0.2 collective-permute-start.3
  8.9 0.7 %collective-permute-start.1 = (f32[2,72,128]{2,1,0:T(8,128)S(1)}, f32[2,72,128]{2,1,0:T(8,128)S(1)}, u32[]{:S(2)}, u32[]{:S(2)}) collective-permute-start(f32[2,72,128]{2,1,0:T(8,128)S(1)} %pad_maximum_fusion), channel_id=1, source_target_pairs={{0,4},{4,0},{8,12},{12,8},{1,5},{5,1},{9,13},{13,9},{2,6},{6,2},{1... | collective-permute-start | bytes 221192 | tf_op jit(solution)/shard_map/ppermute | solution.py:654
  9.6 0.4 collective-permute-done.3.sides_z
  10.0 0.8 %dynamic_slice.3 = s32[2,2,2]{0,2,1:T(2,128)S(1)} dynamic-slice(s32[8,4,4]{0,2,1:T(4,128)} %param.15, s32[]{:T(128)S(6)} %select_n.78, s32[]{:T(128)S(6)} %select_n.79, s32[]{:T(128)S(6)} %select_n.80), dynamic_slice_sizes={2,2,2} | dynamic-slice | bytes 68 | tf_op jit(solution)/shard_map/dynamic_slice | solution.py:659
  10.8 0.1 copy.20
  11.0 0.1 reshape.35
  11.0 1.0 %copy.26 = s32[2,24,2,2,64]{4,0,3,1,2:T(2,128)S(1)} copy(s32[2,24,2,2,64]{4,3,2,1,0:T(2,128)} %bitcast.30) | data formatting | bytes 98304 | tf_op jit(solution)/shard_map/reshape | solution.py:669
  12.0 0.1 reshape.34
  12.2 0.1 reshape.36.limits.refs_0_.refs_2_
  12.3 0.2 collective-permute-start.5
  12.5 0.6 %shard_map.122 = (bf16[608,192]{1,0:T(8,128)(2,1)S(1)}, f32[8,72,128]{2,1,0:T(8,128)S(1)}, f32[8,64,128]{2,1,0:T(8,128)S(1)}, f32[2,64,256]{2,1,0:T(8,128)S(1)},...) custom-call(f32[2,72,128]{2,1,0:T(8,128)S(1)} %reverse_select_fusion.own, ...), custom_call_target="tpu_custom_call" | custom-call | flops 2000000000 | bytes 2000000 | tf_op jit(solution)/shard_map/pallas_call | solution.py:583
  13.1 0.4 collective-permute-done.1.ghost
  13.5 1.1 %collective-permute-start.6 = (f32[2,72,128]{2,1,0:T(8,128)S(1)}, f32[2,72,128]{2,1,0:T(8,128)S(1)}, u32[]{:S(2)}, u32[]{:S(2)}) collective-permute-start(f32[2,72,128]{2,1,0:T(8,128)S(1)} %pad_maximum_fusion.1.refs_0_), channel_id=1, source_target_pairs={{0,2},{2,0},{1,3},{3,1},{4,6},{6,4},{5,7},{7,5},{8,10},{10,8},{9,1... | collective-permute-start | bytes 221192 | tf_op jit(solution)/shard_map/ppermute | solution.py:614
  14.7 0.1 collective-permute-done.7.ghost_z
  14.8 4.0 %shard_map.123 = (f32[24,64,256]{2,1,0:T(8,128)S(1)}, f32[24,64,256]{2,1,0:T(8,128)S(1)}, f32[24,64,256]{2,1,0:T(8,128)S(1)}, f32[24,64,256]{2,1,0:T(8,128)S(1)}...) custom-call(f32[2,72,128]{2,1,0:T(8,128)S(1)} %collective-permute-done.1.ghost, ...), custom_call_target="tpu_custom_call" | custom-call | flops 5000000000 | bytes 2000000 | tf_op jit(solution)/shard_map/pallas_call | solution.py:588
  18.8 11.0 %shard_map.124 = (f32[3,3,4,128]{3,2,1,0:T(4,128)S(1)}, f32[8,256]{1,0:T(8,128)S(1)}) custom-call(f32[2,72,128]{2,1,0:T(8,128)S(1)} %pad_maximum_fusion.1.refs_0_, f32[2,72,128]{2,1,0:T(8,128)S(1)} %collective-permute-done.6.refs_1_, s32[2,1,256]{2,1,0:T(1,128)S(1)} %reshape.36.limits.refs_0_.refs_2_, ...), custom_call_target="tpu_custom_call" | custom-call | flops 12000000000 | bytes 2000000 | tf_op jit(solution)/shard_map/pallas_call | solution.py:597
  29.8 3.2 %collective-permute-start.8 = (f32[3,4,128]{2,1,0:T(4,128)S(1)}, f32[3,4,128]{2,1,0:T(4,128)S(1)}, u32[]{:S(2)}, u32[]{:S(2)}) collective-permute-start(f32[3,4,128]{2,1,0:T(4,128)S(1)} %slice_bitcast_fusion.2), channel_id=1, source_target_pairs={{0,12},{4,8},{8,4},{12,0},{1,13},{5,9},{9,5},{13,1},{2,14},{6,10},... | collective-permute-start | bytes 18440 | tf_op jit(solution)/shard_map/ppermute | solution.py:683
  33.0 7.1 %shard_map.125 = (f32[3,3,4,128]{3,2,1,0:T(4,128)S(1)}, f32[8,256]{1,0:T(8,128)S(1)}) custom-call(bf16[608,192]{1,0:T(8,128)(2,1)S(1)} %get-tuple-element.45.refs_1_.refs_3_.merged, f32[1,64]{1,0:T(1,128)S(1)} %bitcast.28, s32[2,24,256]{2,1,0:T(8,128)S(1)} %get-tuple-element.46.refs_5_.refs_7_.lane_i, ...), custom_call_target="tpu_custom_call" | custom-call | flops 20000000000 | bytes 2000000 | tf_op jit(solution)/shard_map/pallas_call | solution.py:592
  40.2 3.6 %collective-permute-done.9 = f32[3,4,128]{2,1,0:T(4,128)S(1)} collective-permute-done((f32[3,4,128]{2,1,0:T(4,128)S(1)}, f32[3,4,128]{2,1,0:T(4,128)S(1)}, u32[]{:S(2)}, u32[]{:S(2)}) %collective-permute-start.9) | collective-permute-done | bytes 6176 | tf_op jit(solution)/shard_map/ppermute | solution.py:686
  43.8 1.2 %collective-permute-start.10 = (f32[2,3,2,128]{3,2,1,0:T(2,128)S(1)}, f32[2,3,2,128]{3,2,1,0:T(2,128)S(1)}, u32[]{:S(2)}, u32[]{:S(2)}) collective-permute-start(f32[2,3,2,128]{3,2,1,0:T(2,128)S(1)} %pad_maximum_fusion.2), channel_id=1, source_target_pairs={{0,2},{2,0},{1,3},{3,1},{4,6},{6,4},{5,7},{7,5},{8,10},{10,8},{9,1... | collective-permute-start | bytes 18440 | tf_op jit(solution)/shard_map/ppermute | solution.py:605
  45.1 2.4 %collective-permute-done.10 = f32[2,3,2,128]{3,2,1,0:T(2,128)S(1)} collective-permute-done((f32[2,3,2,128]{3,2,1,0:T(2,128)S(1)}, f32[2,3,2,128]{3,2,1,0:T(2,128)S(1)}, u32[]{:S(2)}, u32[]{:S(2)}) %collective-permute-start.10) | collective-permute-done | bytes 6176 | tf_op jit(solution)/shard_map/ppermute | solution.py:605
  47.5 0.1 fusion.4
  47.6 0.1 pad_maximum_fusion.3
  47.7 0.1 reshape.37
  47.8 0.6 %slice.69 = f32[2,2,1,64]{3,2,1,0:T(1,128)} slice(f32[2,2,2,64]{3,2,1,0:T(2,128)S(1)} %reshape.37), slice={[0:2], [0:2], [0:1], [0:64]} | slice | bytes 2048 | tf_op jit(solution)/shard_map/slice | solution.py:692
  48.4 0.5 collective-permute-done.11
  48.9 0.6 %copy.22 = f32[3,2,2,64]{3,2,1,0:T(2,128)} copy(f32[3,2,2,64]{3,2,0,1:T(2,128)S(1)} %fusion.1) | data formatting | bytes 6144
  (50 shorter events, 0.5 us)
Async XLA Ops:
  0.6 11.5 %copy-start.6 = (s32[2,2,64]{2,1,0:T(2,128)S(1)}, s32[2,2,64]{2,1,0:T(2,128)}, u32[]{:S(2)}) copy-start(s32[2,2,64]{2,1,0:T(2,128)} %param.14) | copy-start | bytes 3076
  0.6 11.8 %copy-start.5 = (f32[64]{0:T(128)S(1)}, f32[64]{0:T(128)}, u32[]{:S(2)}) copy-start(f32[64]{0:T(128)} %param.21) | copy-start | bytes 772
  0.7 11.8 %copy-start.3 = (f32[128,64]{0,1:T(8,128)S(1)}, f32[128,64]{0,1:T(8,128)}, u32[]{:S(2)}) copy-start(f32[128,64]{0,1:T(8,128)} %param.20) | copy-start | bytes 98308
  0.7 11.8 %copy-start = (f32[64,64]{1,0:T(8,128)S(1)}, f32[64,64]{1,0:T(8,128)}, u32[]{:S(2)}) copy-start(f32[64,64]{1,0:T(8,128)} %w_self.1) | copy-start | bytes 49156
  0.7 11.8 %copy-start.1 = (f32[64,64]{1,0:T(8,128)S(1)}, f32[64,64]{1,0:T(8,128)}, u32[]{:S(2)}) copy-start(f32[64,64]{1,0:T(8,128)} %w_pair.1) | copy-start | bytes 49156
  0.7 11.8 %copy-start.4 = (f32[8,64]{1,0:T(8,128)S(1)}, f32[8,64]{1,0:T(8,128)}, u32[]{:S(2)}) copy-start(f32[8,64]{1,0:T(8,128)} %w_radial.1) | copy-start | bytes 6148
  0.7 11.8 %copy-start.2 = (f32[64,64]{1,0:T(8,128)S(1)}, f32[64,64]{1,0:T(8,128)}, u32[]{:S(2)}) copy-start(f32[64,64]{1,0:T(8,128)} %w_tensor.1) | copy-start | bytes 49156
  2.1 6.7 %collective-permute-start = (f32[2,72,128]{2,1,0:T(8,128)S(1)}, f32[2,72,128]{2,1,0:T(8,128)S(1)}, u32[]{:S(2)}, u32[]{:S(2)}) collective-permute-start(f32[2,72,128]{2,1,0:T(8,128)S(1)} %reverse_select_fusion.own), channel_id=1, source_target_pairs={{0,2},{2,0},{1,3},{3,1},{4,6},{6,4},{5,7},{7,5},{8,10},{10,8},{9,1... | collective-permute-start | bytes 221192 | tf_op jit(solution)/shard_map/ppermute | solution.py:614
  5.1 7.4 %collective-permute-start.2 = (f32[2,72,128]{2,1,0:T(8,128)S(1)}, f32[2,72,128]{2,1,0:T(8,128)S(1)}, u32[]{:S(2)}, u32[]{:S(2)}) collective-permute-start(f32[2,72,128]{2,1,0:T(8,128)S(1)} %reverse_select_fusion.own), channel_id=1, source_target_pairs={{0,1},{1,0},{2,3},{3,2},{4,5},{5,4},{6,7},{7,6},{8,9},{9,8},{10,11... | collective-permute-start | bytes 221192 | tf_op jit(solution)/shard_map/ppermute | solution.py:614
  5.1 7.2 %collective-permute-start.4 = (f32[72,128]{1,0:T(8,128)S(1)}, f32[72,128]{1,0:T(8,128)S(1)}, u32[]{:S(2)}, u32[]{:S(2)}) collective-permute-start(f32[72,128]{1,0:T(8,128)S(1)} %get-tuple-element.78), channel_id=1, source_target_pairs={{0,12},{4,8},{8,4},{12,0},{1,13},{5,9},{9,5},{13,1},{2,14},{6,10},... | collective-permute-start | bytes 110600 | tf_op jit(solution)/shard_map/ppermute | solution.py:653
  8.7 1.3 %collective-permute-start.3 = (f32[2,72,128]{2,1,0:T(8,128)S(1)}, f32[2,72,128]{2,1,0:T(8,128)S(1)}, u32[]{:S(2)}, u32[]{:S(2)}) collective-permute-start(f32[2,72,128]{2,1,0:T(8,128)S(1)} %collective-permute-done.sides), channel_id=1, source_target_pairs={{0,1},{1,0},{2,3},{3,2},{4,5},{5,4},{6,7},{7,6},{8,9},{9,8},{10,11... | collective-permute-start | bytes 221192 | tf_op jit(solution)/shard_map/ppermute | solution.py:614
  8.9 4.6 %collective-permute-start.1 = (f32[2,72,128]{2,1,0:T(8,128)S(1)}, f32[2,72,128]{2,1,0:T(8,128)S(1)}, u32[]{:S(2)}, u32[]{:S(2)}) collective-permute-start(f32[2,72,128]{2,1,0:T(8,128)S(1)} %pad_maximum_fusion), channel_id=1, source_target_pairs={{0,4},{4,0},{8,12},{12,8},{1,5},{5,1},{9,13},{13,9},{2,6},{6,2},{1... | collective-permute-start | bytes 221192 | tf_op jit(solution)/shard_map/ppermute | solution.py:654
  12.3 1.2 %collective-permute-start.5 = (f32[72,128]{1,0:T(8,128)S(1)}, f32[72,128]{1,0:T(8,128)S(1)}, u32[]{:S(2)}, u32[]{:S(2)}) collective-permute-start(f32[72,128]{1,0:T(8,128)S(1)} %collective-permute-done.4), channel_id=1, source_target_pairs={{0,1},{1,0},{2,3},{3,2},{4,5},{5,4},{6,7},{7,6},{8,9},{9,8},{10,11... | collective-permute-start | bytes 110600 | tf_op jit(solution)/shard_map/ppermute | solution.py:614
  13.5 1.3 %collective-permute-start.7 = (f32[2,72,128]{2,1,0:T(8,128)S(1)}, f32[2,72,128]{2,1,0:T(8,128)S(1)}, u32[]{:S(2)}, u32[]{:S(2)}) collective-permute-start(f32[2,72,128]{2,1,0:T(8,128)S(1)} %collective-permute-done.1.ghost), channel_id=1, source_target_pairs={{0,1},{1,0},{2,3},{3,2},{4,5},{5,4},{6,7},{7,6},{8,9},{9,8},{10,11... | collective-permute-start | bytes 221192 | tf_op jit(solution)/shard_map/ppermute | solution.py:614
  13.5 5.3 %collective-permute-start.6 = (f32[2,72,128]{2,1,0:T(8,128)S(1)}, f32[2,72,128]{2,1,0:T(8,128)S(1)}, u32[]{:S(2)}, u32[]{:S(2)}) collective-permute-start(f32[2,72,128]{2,1,0:T(8,128)S(1)} %pad_maximum_fusion.1.refs_0_), channel_id=1, source_target_pairs={{0,2},{2,0},{1,3},{3,1},{4,6},{6,4},{5,7},{7,5},{8,10},{10,8},{9,1... | collective-permute-start | bytes 221192 | tf_op jit(solution)/shard_map/ppermute | solution.py:614
  29.8 10.2 %collective-permute-start.8 = (f32[3,4,128]{2,1,0:T(4,128)S(1)}, f32[3,4,128]{2,1,0:T(4,128)S(1)}, u32[]{:S(2)}, u32[]{:S(2)}) collective-permute-start(f32[3,4,128]{2,1,0:T(4,128)S(1)} %slice_bitcast_fusion.2), channel_id=1, source_target_pairs={{0,12},{4,8},{8,4},{12,0},{1,13},{5,9},{9,5},{13,1},{2,14},{6,10},... | collective-permute-start | bytes 18440 | tf_op jit(solution)/shard_map/ppermute | solution.py:683
  40.1 3.7 %collective-permute-start.9 = (f32[3,4,128]{2,1,0:T(4,128)S(1)}, f32[3,4,128]{2,1,0:T(4,128)S(1)}, u32[]{:S(2)}, u32[]{:S(2)}) collective-permute-start(f32[3,4,128]{2,1,0:T(4,128)S(1)} %slice_bitcast_fusion.1), channel_id=1, source_target_pairs={{0,4},{4,0},{8,12},{12,8},{1,5},{5,1},{9,13},{13,9},{2,6},{6,2},{1... | collective-permute-start | bytes 18440 | tf_op jit(solution)/shard_map/ppermute | solution.py:686
  43.8 3.7 %collective-permute-start.10 = (f32[2,3,2,128]{3,2,1,0:T(2,128)S(1)}, f32[2,3,2,128]{3,2,1,0:T(2,128)S(1)}, u32[]{:S(2)}, u32[]{:S(2)}) collective-permute-start(f32[2,3,2,128]{3,2,1,0:T(2,128)S(1)} %pad_maximum_fusion.2), channel_id=1, source_target_pairs={{0,2},{2,0},{1,3},{3,1},{4,6},{6,4},{5,7},{7,5},{8,10},{10,8},{9,1... | collective-permute-start | bytes 18440 | tf_op jit(solution)/shard_map/ppermute | solution.py:605
  47.7 1.2 %collective-permute-start.11 = (f32[2,3,2,64]{3,2,1,0:T(2,128)S(1)}, f32[2,3,2,64]{3,2,1,0:T(2,128)S(1)}, u32[]{:S(2)}, u32[]{:S(2)}) collective-permute-start(f32[2,3,2,64]{3,2,1,0:T(2,128)S(1)} %pad_maximum_fusion.3), channel_id=1, source_target_pairs={{0,1},{1,0},{2,3},{3,2},{4,5},{5,4},{6,7},{7,6},{8,9},{9,8},{10,11... | collective-permute-start | bytes 9224 | tf_op jit(solution)/shard_map/ppermute | solution.py:605

commit v6 on v5

--- a/solution.py
+++ b/solution.py
@@ -597,23 +597,30 @@
     return call(functools.partial(whole, which), RESULT, scratch, 12, 28)(*given)
 
 
-def exchange(low, high, axis, dim):
+def shifts(axis, along=None):
     size = lax.axis_size(axis)
     up = [(i, (i + 1) % size) for i in range(size)]
     down = [(j, i) for i, j in up]
-    if size == 2:
-        return lax.ppermute(jnp.concatenate([high, low], axis=dim), axis, up)
-    parts = [lax.ppermute(high, axis, up), lax.ppermute(low, axis, down)]
+    if along is None:
+        return axis, up, down
+    both_ways = ([(a * size + i, b * size + j) for a, b in along for i, j in way] for way in (up, down))
+    return ("gx", axis), *both_ways
+
+
+def exchange(low, high, axis, dim, along=None):
+    axes, up, down = shifts(axis, along)
+    if lax.axis_size(axis) == 2:
+        return lax.ppermute(jnp.concatenate([high, low], axis=dim), axes, up)
+    parts = [lax.ppermute(high, axes, up), lax.ppermute(low, axes, down)]
     return jnp.concatenate(parts, axis=dim)
 
 
-def neighbours(x, axis, width):
-    size = lax.axis_size(axis)
-    up = [(i, (i + 1) % size) for i in range(size)]
-    if size == 2:
-        return lax.ppermute(x, axis, up)
-    below = lax.ppermute(x, axis, up)
-    above = lax.ppermute(x, axis, [(j, i) for i, j in up])
+def neighbours(x, axis, width, along=None):
+    axes, up, down = shifts(axis, along)
+    if lax.axis_size(axis) == 2:
+        return lax.ppermute(x, axes, up)
+    below = lax.ppermute(x, axes, up)
+    above = lax.ppermute(x, axes, down)
     lane = jnp.arange(x.shape[-1], dtype=jnp.int32)
     return jnp.where(lane % (2 * width) < width, above, below)
 
@@ -683,9 +690,12 @@
     back0 = lax.ppermute(grad0[0], "gx", second)
     grad1, energy1 = run_rear(1, merged, out_row, *decoded[3:], grad0, *kept)
     grad1, back0 = lax.optimization_barrier((grad1, back0))
-    back1 = lax.ppermute(grad1[2], "gx", first)
-    grad = grad1[:2] + jnp.stack([back0, back1])
-    grad = grad[:, :, 1:-1] + exchange(grad[:, :, :1], grad[:, :, -1:], "gy", 2)
+    grad = grad1[:2] + jnp.stack([back0, jnp.zeros_like(back0)])
+    back_y = exchange(grad[:, :, :1], grad[:, :, -1:], "gy", 2)
+    back1 = lax.ppermute(grad1[2, :, 1:-1], "gx", first)
+    back2 = exchange(grad1[2, :, :1], grad1[2, :, -1:], "gy", 1, first)
+    back_y, back1, back2 = lax.optimization_barrier((back_y, back1, back2))
+    grad = grad[:, :, 1:-1] + back_y + jnp.stack([jnp.zeros_like(back1), back1 + back2])
     grad = grad[..., SLOTS:-SLOTS] + exchange(grad[..., :SLOTS], grad[..., -SLOTS:], "gz", 3)
     forces = -mirrored(grad).transpose(1, 0, 2, 3)
     energies = mirrored(jnp.stack([energy0[0], energy1[0]]))

time: 49.7 us -> 47.6 us (0.958)
  waiting for transfers between devices: 7.39 us -> 2.92 us
  starting transfers between devices: 13.3 us -> 15.6 us
    ppermute x9 -> x10, waiting for transfers between devices: 6.98 us -> 2.51 us  [the longest x3 1.3 us: exchange(): return lax.ppermute(jnp.concatenate([high, low], axis=dim), axes, up)]
    ppermute x9 -> x10, starting transfers between devices: 5.81 us -> 8.11 us  [the longest x6 4.48 us: neighbours(): return lax.ppermute(x, axes, up)]
  transfers between devices with their start and end apart: 12 -> 13, of which waited for: 6 -> 6; matrix products, arithmetic and copies ran while one was open for 6% -> 6% of each run, Pallas kernels for 24% -> 25%
where the time goes in v6:
time: 47.6 us; the launch traced here: 47.4 us
  Pallas kernels  22.7 us (48%)
  starting transfers between devices  15.6 us (33%)
  local copies, waits for them, and re-layouts  3.94 us (8%)
  waiting for transfers between devices  2.92 us (6%)
  other arithmetic  1.33 us (3%)
  between operations  0.95 us (2%)
    pallas_call x1, Pallas kernels, run_whole(): call(functools.partial(whole, which), RESULT, scratch, 12, 28)(*given)  11 us
    pallas_call x1, Pallas kernels, run_rear(): call(functools.partial(rear, ALONE, which), RESULT, in_vmem(STEPS + REAR)...  7.05 us
    ppermute x6, starting transfers between devices, neighbours(): return lax.ppermute(x, axes, up)  4.48 us
    pallas_call x1, Pallas kernels, run_front(): call(functools.partial(opening, which), shaped(KEPT), scratch, 5, 16)  4.03 us
    ppermute x1, starting transfers between devices, local(): outer = lax.ppermute(state[0], 'gx', second)  3.67 us
    ppermute x1, starting transfers between devices, local(): back0 = lax.ppermute(grad0[0], 'gx', second)  3.16 us
    ppermute x1, starting transfers between devices, local(): back1 = lax.ppermute(grad1[2, :, 1:-1], 'gx', first)  2.06 us
    ppermute x3, starting transfers between devices, exchange(): return lax.ppermute(jnp.concatenate([high, low], axis=dim), axes, up)  1.58 us
  transfers between devices with their start and end apart: 13, of which 6 were waited for; matrix products, arithmetic and copies ran while one was open for 6% of the time, Pallas kernels for 25%

profile of v6, /device:TPU:0, one launch (start us, length us, event | category | flops | bytes accessed | tf_op | source)
XLA Modules:
  0.0 47.4 jit_solution(15984745450449836761)
XLA Ops:
  0.8 1.1 %maximum_bitcast_fusion = f32[2,72,2,64]{3,2,0,1:T(2,128)S(1)} fusion(f32[3,2,2,64]{3,2,1,0:T(2,128)} %param.11, f32[64,2,2,64]{3,2,1,0:T(2,128)} %param.12, f32[72]{0:T(128)S(1)} %pad.16.clone), kind=kLoop, calls=%fused_computation | loop fusion | flops 36864 | bytes 142624 | tf_op jit(solution)/shard_map/transpose | solution.py:653
  1.9 0.2 reshape.38
  2.1 3.0 %collective-permute-start = (f32[2,72,128]{2,1,0:T(8,128)S(1)}, f32[2,72,128]{2,1,0:T(8,128)S(1)}, u32[]{:S(2)}, u32[]{:S(2)}) collective-permute-start(f32[2,72,128]{2,1,0:T(8,128)S(1)} %reverse_select_fusion.own), channel_id=1, source_target_pairs={{0,2},{2,0},{1,3},{3,1},{4,6},{6,4},{5,7},{7,5},{8,10},{10,8},{9,1... | collective-permute-start | bytes 221192 | tf_op jit(solution)/shard_map/ppermute | solution.py:621
  5.1 3.7 %collective-permute-start.4 = (f32[72,128]{1,0:T(8,128)S(1)}, f32[72,128]{1,0:T(8,128)S(1)}, u32[]{:S(2)}, u32[]{:S(2)}) collective-permute-start(f32[72,128]{1,0:T(8,128)S(1)} %get-tuple-element.84), channel_id=1, source_target_pairs={{0,12},{4,8},{8,4},{12,0},{1,13},{5,9},{9,5},{13,1},{2,14},{6,10},... | collective-permute-start | bytes 110600 | tf_op jit(solution)/shard_map/ppermute | solution.py:660
  8.7 0.2 collective-permute-start.3
  8.9 0.7 %collective-permute-start.1 = (f32[2,72,128]{2,1,0:T(8,128)S(1)}, f32[2,72,128]{2,1,0:T(8,128)S(1)}, u32[]{:S(2)}, u32[]{:S(2)}) collective-permute-start(f32[2,72,128]{2,1,0:T(8,128)S(1)} %pad_maximum_fusion), channel_id=1, source_target_pairs={{0,4},{4,0},{8,12},{12,8},{1,5},{5,1},{9,13},{13,9},{2,6},{6,2},{1... | collective-permute-start | bytes 221192 | tf_op jit(solution)/shard_map/ppermute | solution.py:661
  9.6 0.4 collective-permute-done.3.sides_z
  10.0 0.8 %dynamic_slice.3 = s32[2,2,2]{0,2,1:T(2,128)S(1)} dynamic-slice(s32[8,4,4]{0,2,1:T(4,128)} %param.15, s32[]{:T(128)S(6)} %select_n.78, s32[]{:T(128)S(6)} %select_n.79, s32[]{:T(128)S(6)} %select_n.80), dynamic_slice_sizes={2,2,2} | dynamic-slice | bytes 68 | tf_op jit(solution)/shard_map/dynamic_slice | solution.py:666
  10.8 0.1 copy.20
  11.0 0.1 reshape.35
  11.0 1.0 %copy.26 = s32[2,24,2,2,64]{4,0,3,1,2:T(2,128)S(1)} copy(s32[2,24,2,2,64]{4,3,2,1,0:T(2,128)} %bitcast.35) | data formatting | bytes 98304 | tf_op jit(solution)/shard_map/reshape | solution.py:676
  12.0 0.1 reshape.34
  12.2 0.1 reshape.36.limits.refs_0_.refs_2_
  12.3 0.2 collective-permute-start.5
  12.5 0.6 %shard_map.122 = (bf16[608,192]{1,0:T(8,128)(2,1)S(1)}, f32[8,72,128]{2,1,0:T(8,128)S(1)}, f32[8,64,128]{2,1,0:T(8,128)S(1)}, f32[2,64,256]{2,1,0:T(8,128)S(1)},...) custom-call(f32[2,72,128]{2,1,0:T(8,128)S(1)} %reverse_select_fusion.own, ...), custom_call_target="tpu_custom_call" | custom-call | flops 2000000000 | bytes 2000000 | tf_op jit(solution)/shard_map/pallas_call | solution.py:583
  13.1 0.4 collective-permute-done.1.ghost
  13.5 1.1 %collective-permute-start.6 = (f32[2,72,128]{2,1,0:T(8,128)S(1)}, f32[2,72,128]{2,1,0:T(8,128)S(1)}, u32[]{:S(2)}, u32[]{:S(2)}) collective-permute-start(f32[2,72,128]{2,1,0:T(8,128)S(1)} %pad_maximum_fusion.1.refs_0_), channel_id=1, source_target_pairs={{0,2},{2,0},{1,3},{3,1},{4,6},{6,4},{5,7},{7,5},{8,10},{10,8},{9,1... | collective-permute-start | bytes 221192 | tf_op jit(solution)/shard_map/ppermute | solution.py:621
  14.7 0.1 collective-permute-done.7.ghost_z
  14.8 4.0 %shard_map.123 = (f32[24,64,256]{2,1,0:T(8,128)S(1)}, f32[24,64,256]{2,1,0:T(8,128)S(1)}, f32[24,64,256]{2,1,0:T(8,128)S(1)}, f32[24,64,256]{2,1,0:T(8,128)S(1)}...) custom-call(f32[2,72,128]{2,1,0:T(8,128)S(1)} %collective-permute-done.1.ghost, ...), custom_call_target="tpu_custom_call" | custom-call | flops 5000000000 | bytes 2000000 | tf_op jit(solution)/shard_map/pallas_call | solution.py:588
  18.8 11.0 %shard_map.124 = (f32[3,3,4,128]{3,2,1,0:T(4,128)S(1)}, f32[8,256]{1,0:T(8,128)S(1)}) custom-call(f32[2,72,128]{2,1,0:T(8,128)S(1)} %pad_maximum_fusion.1.refs_0_, f32[2,72,128]{2,1,0:T(8,128)S(1)} %collective-permute-done.6.refs_1_, s32[2,1,256]{2,1,0:T(1,128)S(1)} %reshape.36.limits.refs_0_.refs_2_, ...), custom_call_target="tpu_custom_call" | custom-call | flops 12000000000 | bytes 2000000 | tf_op jit(solution)/shard_map/pallas_call | solution.py:597
  29.8 3.2 %collective-permute-start.8 = (f32[3,4,128]{2,1,0:T(4,128)S(1)}, f32[3,4,128]{2,1,0:T(4,128)S(1)}, u32[]{:S(2)}, u32[]{:S(2)}) collective-permute-start(f32[3,4,128]{2,1,0:T(4,128)S(1)} %slice_bitcast_fusion.1), channel_id=1, source_target_pairs={{0,12},{4,8},{8,4},{12,0},{1,13},{5,9},{9,5},{13,1},{2,14},{6,10},... | collective-permute-start | bytes 18440 | tf_op jit(solution)/shard_map/ppermute | solution.py:690
  33.0 7.1 %shard_map.125 = (f32[3,3,4,128]{3,2,1,0:T(4,128)S(1)}, f32[8,256]{1,0:T(8,128)S(1)}) custom-call(bf16[608,192]{1,0:T(8,128)(2,1)S(1)} %get-tuple-element.48.refs_1_.refs_3_.merged, f32[1,64]{1,0:T(1,128)S(1)} %bitcast.33, s32[2,24,256]{2,1,0:T(8,128)S(1)} %get-tuple-element.49.refs_5_.refs_7_.lane_i, ...), custom_call_target="tpu_custom_call" | custom-call | flops 20000000000 | bytes 2000000 | tf_op jit(solution)/shard_map/pallas_call | solution.py:592
  40.1 0.4 collective-permute-start.11
  40.5 1.2 %collective-permute-start.9 = (f32[2,3,2,128]{3,2,1,0:T(2,128)S(1)}, f32[2,3,2,128]{3,2,1,0:T(2,128)S(1)}, u32[]{:S(2)}, u32[]{:S(2)}) collective-permute-start(f32[2,3,2,128]{3,2,1,0:T(2,128)S(1)} %pad_maximum_fusion.2), channel_id=1, source_target_pairs={{0,2},{2,0},{1,3},{3,1},{4,6},{6,4},{5,7},{7,5},{8,10},{10,8},{9,1... | collective-permute-start | bytes 18440 | tf_op jit(solution)/shard_map/ppermute | solution.py:613
  41.7 2.1 %collective-permute-start.10 = (f32[3,2,128]{2,1,0:T(2,128)S(1)}, f32[3,2,128]{2,1,0:T(2,128)S(1)}, u32[]{:S(2)}, u32[]{:S(2)}) collective-permute-start(f32[3,2,128]{2,1,0:T(2,128)S(1)} %slice_bitcast_fusion.2), channel_id=1, source_target_pairs={{0,4},{4,0},{8,12},{12,8},{1,5},{5,1},{9,13},{13,9},{2,6},{6,2},{1... | collective-permute-start | bytes 9224 | tf_op jit(solution)/shard_map/ppermute | solution.py:695
  43.9 0.8 %collective-permute-done.11 = f32[3,2,128]{2,1,0:T(2,128)S(1)} collective-permute-done((f32[3,2,128]{2,1,0:T(2,128)S(1)}, f32[3,2,128]{2,1,0:T(2,128)S(1)}, u32[]{:S(2)}, u32[]{:S(2)}) %collective-permute-start.11) | collective-permute-done | bytes 3104 | tf_op jit(solution)/shard_map/ppermute | solution.py:613
  44.7 0.7 %collective-permute-done.10 = f32[3,2,128]{2,1,0:T(2,128)S(1)} collective-permute-done((f32[3,2,128]{2,1,0:T(2,128)S(1)}, f32[3,2,128]{2,1,0:T(2,128)S(1)}, u32[]{:S(2)}, u32[]{:S(2)}) %collective-permute-start.10) | collective-permute-done | bytes 3104 | tf_op jit(solution)/shard_map/ppermute | solution.py:695
  45.4 0.1 pad_maximum_fusion.3
  45.6 0.1 reshape.37
  45.6 0.6 %slice.77 = f32[2,2,1,64]{3,2,1,0:T(1,128)} slice(f32[2,2,2,64]{3,2,1,0:T(2,128)S(1)} %reshape.37), slice={[0:2], [0:2], [0:1], [0:64]} | slice | bytes 2048 | tf_op jit(solution)/shard_map/slice | solution.py:702
  46.2 0.5 collective-permute-done.12
  46.8 0.6 %copy.22 = f32[3,2,2,64]{3,2,1,0:T(2,128)} copy(f32[3,2,2,64]{3,2,0,1:T(2,128)S(1)} %fusion.1) | data formatting | bytes 6144
  (55 shorter events, 0.6 us)
Async XLA Ops:
  0.6 11.5 %copy-start.6 = (s32[2,2,64]{2,1,0:T(2,128)S(1)}, s32[2,2,64]{2,1,0:T(2,128)}, u32[]{:S(2)}) copy-start(s32[2,2,64]{2,1,0:T(2,128)} %param.14) | copy-start | bytes 3076
  0.6 11.8 %copy-start.5 = (f32[64]{0:T(128)S(1)}, f32[64]{0:T(128)}, u32[]{:S(2)}) copy-start(f32[64]{0:T(128)} %param.21) | copy-start | bytes 772
  0.7 11.8 %copy-start.3 = (f32[128,64]{0,1:T(8,128)S(1)}, f32[128,64]{0,1:T(8,128)}, u32[]{:S(2)}) copy-start(f32[128,64]{0,1:T(8,128)} %param.20) | copy-start | bytes 98308
  0.7 11.8 %copy-start = (f32[64,64]{1,0:T(8,128)S(1)}, f32[64,64]{1,0:T(8,128)}, u32[]{:S(2)}) copy-start(f32[64,64]{1,0:T(8,128)} %w_self.1) | copy-start | bytes 49156
  0.7 11.8 %copy-start.1 = (f32[64,64]{1,0:T(8,128)S(1)}, f32[64,64]{1,0:T(8,128)}, u32[]{:S(2)}) copy-start(f32[64,64]{1,0:T(8,128)} %w_pair.1) | copy-start | bytes 49156
  0.7 11.8 %copy-start.4 = (f32[8,64]{1,0:T(8,128)S(1)}, f32[8,64]{1,0:T(8,128)}, u32[]{:S(2)}) copy-start(f32[8,64]{1,0:T(8,128)} %w_radial.1) | copy-start | bytes 6148
  0.7 11.8 %copy-start.2 = (f32[64,64]{1,0:T(8,128)S(1)}, f32[64,64]{1,0:T(8,128)}, u32[]{:S(2)}) copy-start(f32[64,64]{1,0:T(8,128)} %w_tensor.1) | copy-start | bytes 49156
  2.1 6.7 %collective-permute-start = (f32[2,72,128]{2,1,0:T(8,128)S(1)}, f32[2,72,128]{2,1,0:T(8,128)S(1)}, u32[]{:S(2)}, u32[]{:S(2)}) collective-permute-start(f32[2,72,128]{2,1,0:T(8,128)S(1)} %reverse_select_fusion.own), channel_id=1, source_target_pairs={{0,2},{2,0},{1,3},{3,1},{4,6},{6,4},{5,7},{7,5},{8,10},{10,8},{9,1... | collective-permute-start | bytes 221192 | tf_op jit(solution)/shard_map/ppermute | solution.py:621
  5.1 7.4 %collective-permute-start.2 = (f32[2,72,128]{2,1,0:T(8,128)S(1)}, f32[2,72,128]{2,1,0:T(8,128)S(1)}, u32[]{:S(2)}, u32[]{:S(2)}) collective-permute-start(f32[2,72,128]{2,1,0:T(8,128)S(1)} %reverse_select_fusion.own), channel_id=1, source_target_pairs={{0,1},{1,0},{2,3},{3,2},{4,5},{5,4},{6,7},{7,6},{8,9},{9,8},{10,11... | collective-permute-start | bytes 221192 | tf_op jit(solution)/shard_map/ppermute | solution.py:621
  5.1 7.2 %collective-permute-start.4 = (f32[72,128]{1,0:T(8,128)S(1)}, f32[72,128]{1,0:T(8,128)S(1)}, u32[]{:S(2)}, u32[]{:S(2)}) collective-permute-start(f32[72,128]{1,0:T(8,128)S(1)} %get-tuple-element.84), channel_id=1, source_target_pairs={{0,12},{4,8},{8,4},{12,0},{1,13},{5,9},{9,5},{13,1},{2,14},{6,10},... | collective-permute-start | bytes 110600 | tf_op jit(solution)/shard_map/ppermute | solution.py:660
  8.7 1.3 %collective-permute-start.3 = (f32[2,72,128]{2,1,0:T(8,128)S(1)}, f32[2,72,128]{2,1,0:T(8,128)S(1)}, u32[]{:S(2)}, u32[]{:S(2)}) collective-permute-start(f32[2,72,128]{2,1,0:T(8,128)S(1)} %collective-permute-done.sides), channel_id=1, source_target_pairs={{0,1},{1,0},{2,3},{3,2},{4,5},{5,4},{6,7},{7,6},{8,9},{9,8},{10,11... | collective-permute-start | bytes 221192 | tf_op jit(solution)/shard_map/ppermute | solution.py:621
  8.9 4.6 %collective-permute-start.1 = (f32[2,72,128]{2,1,0:T(8,128)S(1)}, f32[2,72,128]{2,1,0:T(8,128)S(1)}, u32[]{:S(2)}, u32[]{:S(2)}) collective-permute-start(f32[2,72,128]{2,1,0:T(8,128)S(1)} %pad_maximum_fusion), channel_id=1, source_target_pairs={{0,4},{4,0},{8,12},{12,8},{1,5},{5,1},{9,13},{13,9},{2,6},{6,2},{1... | collective-permute-start | bytes 221192 | tf_op jit(solution)/shard_map/ppermute | solution.py:661
  12.3 1.2 %collective-permute-start.5 = (f32[72,128]{1,0:T(8,128)S(1)}, f32[72,128]{1,0:T(8,128)S(1)}, u32[]{:S(2)}, u32[]{:S(2)}) collective-permute-start(f32[72,128]{1,0:T(8,128)S(1)} %collective-permute-done.4), channel_id=1, source_target_pairs={{0,1},{1,0},{2,3},{3,2},{4,5},{5,4},{6,7},{7,6},{8,9},{9,8},{10,11... | collective-permute-start | bytes 110600 | tf_op jit(solution)/shard_map/ppermute | solution.py:621
  13.5 1.3 %collective-permute-start.7 = (f32[2,72,128]{2,1,0:T(8,128)S(1)}, f32[2,72,128]{2,1,0:T(8,128)S(1)}, u32[]{:S(2)}, u32[]{:S(2)}) collective-permute-start(f32[2,72,128]{2,1,0:T(8,128)S(1)} %collective-permute-done.1.ghost), channel_id=1, source_target_pairs={{0,1},{1,0},{2,3},{3,2},{4,5},{5,4},{6,7},{7,6},{8,9},{9,8},{10,11... | collective-permute-start | bytes 221192 | tf_op jit(solution)/shard_map/ppermute | solution.py:621
  13.5 5.3 %collective-permute-start.6 = (f32[2,72,128]{2,1,0:T(8,128)S(1)}, f32[2,72,128]{2,1,0:T(8,128)S(1)}, u32[]{:S(2)}, u32[]{:S(2)}) collective-permute-start(f32[2,72,128]{2,1,0:T(8,128)S(1)} %pad_maximum_fusion.1.refs_0_), channel_id=1, source_target_pairs={{0,2},{2,0},{1,3},{3,1},{4,6},{6,4},{5,7},{7,5},{8,10},{10,8},{9,1... | collective-permute-start | bytes 221192 | tf_op jit(solution)/shard_map/ppermute | solution.py:621
  29.8 10.2 %collective-permute-start.8 = (f32[3,4,128]{2,1,0:T(4,128)S(1)}, f32[3,4,128]{2,1,0:T(4,128)S(1)}, u32[]{:S(2)}, u32[]{:S(2)}) collective-permute-start(f32[3,4,128]{2,1,0:T(4,128)S(1)} %slice_bitcast_fusion.1), channel_id=1, source_target_pairs={{0,12},{4,8},{8,4},{12,0},{1,13},{5,9},{9,5},{13,1},{2,14},{6,10},... | collective-permute-start | bytes 18440 | tf_op jit(solution)/shard_map/ppermute | solution.py:690
  40.1 4.6 %collective-permute-start.11 = (f32[3,2,128]{2,1,0:T(2,128)S(1)}, f32[3,2,128]{2,1,0:T(2,128)S(1)}, u32[]{:S(2)}, u32[]{:S(2)}) collective-permute-start(f32[3,2,128]{2,1,0:T(2,128)S(1)} %pad_maximum_fusion.4), channel_id=1, source_target_pairs={{0,6},{2,4},{4,2},{6,0},{8,14},{10,12},{12,10},{14,8},{1,7},{3,5},... | collective-permute-start | bytes 9224 | tf_op jit(solution)/shard_map/ppermute | solution.py:613
  40.5 4.8 %collective-permute-start.9 = (f32[2,3,2,128]{3,2,1,0:T(2,128)S(1)}, f32[2,3,2,128]{3,2,1,0:T(2,128)S(1)}, u32[]{:S(2)}, u32[]{:S(2)}) collective-permute-start(f32[2,3,2,128]{3,2,1,0:T(2,128)S(1)} %pad_maximum_fusion.2), channel_id=1, source_target_pairs={{0,2},{2,0},{1,3},{3,1},{4,6},{6,4},{5,7},{7,5},{8,10},{10,8},{9,1... | collective-permute-start | bytes 18440 | tf_op jit(solution)/shard_map/ppermute | solution.py:613
  41.7 3.6 %collective-permute-start.10 = (f32[3,2,128]{2,1,0:T(2,128)S(1)}, f32[3,2,128]{2,1,0:T(2,128)S(1)}, u32[]{:S(2)}, u32[]{:S(2)}) collective-permute-start(f32[3,2,128]{2,1,0:T(2,128)S(1)} %slice_bitcast_fusion.2), channel_id=1, source_target_pairs={{0,4},{4,0},{8,12},{12,8},{1,5},{5,1},{9,13},{13,9},{2,6},{6,2},{1... | collective-permute-start | bytes 9224 | tf_op jit(solution)/shard_map/ppermute | solution.py:695
  45.5 1.2 %collective-permute-start.12 = (f32[2,3,2,64]{3,2,1,0:T(2,128)S(1)}, f32[2,3,2,64]{3,2,1,0:T(2,128)S(1)}, u32[]{:S(2)}, u32[]{:S(2)}) collective-permute-start(f32[2,3,2,64]{3,2,1,0:T(2,128)S(1)} %pad_maximum_fusion.3), channel_id=1, source_target_pairs={{0,1},{1,0},{2,3},{3,2},{4,5},{5,4},{6,7},{7,6},{8,9},{9,8},{10,11... | collective-permute-start | bytes 9224 | tf_op jit(solution)/shard_map/ppermute | solution.py:613

commit v7 on v6

--- a/solution.py
+++ b/solution.py
@@ -312,20 +312,20 @@
         env = row(ENV, s)
         act[s] = silu
         slope[s] = (sg + silu * (1.0 - sg)) * env
-        step_b[i] = dot(w_a[...], stacked(silu * env))
-
-    def forward_c(s, i):
-        both_t = step_b[i]
+        both_t = dot(w_a[...], stacked(silu * env))
         tens[s] = both_t[:FEAT]
         mix0[s] = both_t[FEAT : 2 * FEAT]
         e_row[pl.ds(s, 1), :] = both_t[2 * FEAT : 2 * FEAT + 1]
+
+    def forward_c(s, i):
+        pass
 
     def forward_sum(first, group):
         for k in range(9):
             part = slice(0, 32) if k < 3 else slice(32, 64)
             total = v_acc[k]
             for i in range(group):
-                total += step_b[i, part] * row(k, first + i)
+                total += tens[first + i, part] * row(k, first + i)
             v_acc[k] = total
 
     pipeline((forward_a, forward_b, forward_c), plan[0], forward_sum)
@@ -395,22 +395,22 @@
         silu = mixture * sg
         m_row[pl.ds(s, 1), :] = jnp.sum(col_w * silu, axis=0, keepdims=True)
         grad = (sg + silu * (1.0 - sg)) * row(ENV, s)
-        step_b[i, : 2 * FEAT] = dot(w_c[...], stacked(grad))
+        pulled = dot(w_c[...], stacked(grad))
+        resid[s] = pulled[:FEAT] + col_w
+        step_c[i] = pulled[FEAT:]
 
     def middle_c(s, i):
-        resid[s] = step_b[i, :FEAT] + col_w
-        dvt = step_b[i, FEAT : 2 * FEAT]
+        dvt = step_c[i]
         back[s] = dvt * back[s]
         p = dvt * tens[s]
         prod[s] = p
-        step_c[i] = p
 
     def middle_sum(first, group):
         for k in range(9):
             part = slice(0, 32) if k < 3 else slice(32, 64)
             total = dv_acc[k]
             for i in range(group):
-                total += step_c[i, part] * row(k, first + i)
+                total += prod[first + i, part] * row(k, first + i)
             dv_acc[k] = total
 
     pipeline((middle_a, middle_b, middle_c), plan[1], middle_sum)

time: 47.6 us -> 47.4 us (level)
  no operation moved by 1% of the time
where the time goes in v7:
time: 47.4 us; the launch traced here: 47.3 us
  Pallas kernels  22.5 us (47%)
  starting transfers between devices  15.6 us (33%)
  local copies, waits for them, and re-layouts  3.94 us (8%)
  waiting for transfers between devices  2.92 us (6%)
  other arithmetic  1.33 us (3%)
  between operations  0.95 us (2%)
    pallas_call x1, Pallas kernels, run_whole(): call(functools.partial(whole, which), RESULT, scratch, 12, 28)(*given)  10.8 us
    pallas_call x1, Pallas kernels, run_rear(): call(functools.partial(rear, ALONE, which), RESULT, in_vmem(STEPS + REAR)...  7.07 us
    ppermute x6, starting transfers between devices, neighbours(): return lax.ppermute(x, axes, up)  4.48 us
    pallas_call x1, Pallas kernels, run_front(): call(functools.partial(opening, which), shaped(KEPT), scratch, 5, 16)  4.03 us
    ppermute x1, starting transfers between devices, local(): outer = lax.ppermute(state[0], 'gx', second)  3.67 us
    ppermute x1, starting transfers between devices, local(): back0 = lax.ppermute(grad0[0], 'gx', second)  3.17 us
    ppermute x1, starting transfers between devices, local(): back1 = lax.ppermute(grad1[2, :, 1:-1], 'gx', first)  2.09 us
    ppermute x3, starting transfers between devices, exchange(): return lax.ppermute(jnp.concatenate([high, low], axis=dim), axes, up)  1.55 us
  transfers between devices with their start and end apart: 13, of which 6 were waited for; matrix products, arithmetic and copies ran while one was open for 6% of the time, Pallas kernels for 25%

profile of v7, /device:TPU:0, one launch (start us, length us, event | category | flops | bytes accessed | tf_op | source)
XLA Modules:
  0.0 47.3 jit_solution(9375684716517261425)
XLA Ops:
  0.8 1.1 %maximum_bitcast_fusion = f32[2,72,2,64]{3,2,0,1:T(2,128)S(1)} fusion(f32[3,2,2,64]{3,2,1,0:T(2,128)} %param.11, f32[64,2,2,64]{3,2,1,0:T(2,128)} %param.12, f32[72]{0:T(128)S(1)} %pad.16.clone), kind=kLoop, calls=%fused_computation | loop fusion | flops 36864 | bytes 142624 | tf_op jit(solution)/shard_map/transpose | solution.py:653
  1.9 0.2 reshape.38
  2.1 3.0 %collective-permute-start = (f32[2,72,128]{2,1,0:T(8,128)S(1)}, f32[2,72,128]{2,1,0:T(8,128)S(1)}, u32[]{:S(2)}, u32[]{:S(2)}) collective-permute-start(f32[2,72,128]{2,1,0:T(8,128)S(1)} %reverse_select_fusion.own), channel_id=1, source_target_pairs={{0,2},{2,0},{1,3},{3,1},{4,6},{6,4},{5,7},{7,5},{8,10},{10,8},{9,1... | collective-permute-start | bytes 221192 | tf_op jit(solution)/shard_map/ppermute | solution.py:621
  5.1 3.7 %collective-permute-start.4 = (f32[72,128]{1,0:T(8,128)S(1)}, f32[72,128]{1,0:T(8,128)S(1)}, u32[]{:S(2)}, u32[]{:S(2)}) collective-permute-start(f32[72,128]{1,0:T(8,128)S(1)} %get-tuple-element.84), channel_id=1, source_target_pairs={{0,12},{4,8},{8,4},{12,0},{1,13},{5,9},{9,5},{13,1},{2,14},{6,10},... | collective-permute-start | bytes 110600 | tf_op jit(solution)/shard_map/ppermute | solution.py:660
  8.7 0.2 collective-permute-start.3
  8.9 0.7 %collective-permute-start.1 = (f32[2,72,128]{2,1,0:T(8,128)S(1)}, f32[2,72,128]{2,1,0:T(8,128)S(1)}, u32[]{:S(2)}, u32[]{:S(2)}) collective-permute-start(f32[2,72,128]{2,1,0:T(8,128)S(1)} %pad_maximum_fusion), channel_id=1, source_target_pairs={{0,4},{4,0},{8,12},{12,8},{1,5},{5,1},{9,13},{13,9},{2,6},{6,2},{1... | collective-permute-start | bytes 221192 | tf_op jit(solution)/shard_map/ppermute | solution.py:661
  9.6 0.4 collective-permute-done.3.sides_z
  10.0 0.8 %dynamic_slice.3 = s32[2,2,2]{0,2,1:T(2,128)S(1)} dynamic-slice(s32[8,4,4]{0,2,1:T(4,128)} %param.15, s32[]{:T(128)S(6)} %select_n.78, s32[]{:T(128)S(6)} %select_n.79, s32[]{:T(128)S(6)} %select_n.80), dynamic_slice_sizes={2,2,2} | dynamic-slice | bytes 68 | tf_op jit(solution)/shard_map/dynamic_slice | solution.py:666
  10.8 0.1 copy.20
  11.0 0.1 reshape.35
  11.0 1.0 %copy.26 = s32[2,24,2,2,64]{4,0,3,1,2:T(2,128)S(1)} copy(s32[2,24,2,2,64]{4,3,2,1,0:T(2,128)} %bitcast.35) | data formatting | bytes 98304 | tf_op jit(solution)/shard_map/reshape | solution.py:676
  12.0 0.1 reshape.34
  12.2 0.1 reshape.36.limits.refs_0_.refs_2_
  12.3 0.2 collective-permute-start.5
  12.5 0.6 %shard_map.122 = (bf16[608,192]{1,0:T(8,128)(2,1)S(1)}, f32[8,72,128]{2,1,0:T(8,128)S(1)}, f32[8,64,128]{2,1,0:T(8,128)S(1)}, f32[2,64,256]{2,1,0:T(8,128)S(1)},...) custom-call(f32[2,72,128]{2,1,0:T(8,128)S(1)} %reverse_select_fusion.own, ...), custom_call_target="tpu_custom_call" | custom-call | flops 2000000000 | bytes 2000000 | tf_op jit(solution)/shard_map/pallas_call | solution.py:583
  13.1 0.4 collective-permute-done.1.ghost
  13.5 1.1 %collective-permute-start.6 = (f32[2,72,128]{2,1,0:T(8,128)S(1)}, f32[2,72,128]{2,1,0:T(8,128)S(1)}, u32[]{:S(2)}, u32[]{:S(2)}) collective-permute-start(f32[2,72,128]{2,1,0:T(8,128)S(1)} %pad_maximum_fusion.1.refs_0_), channel_id=1, source_target_pairs={{0,2},{2,0},{1,3},{3,1},{4,6},{6,4},{5,7},{7,5},{8,10},{10,8},{9,1... | collective-permute-start | bytes 221192 | tf_op jit(solution)/shard_map/ppermute | solution.py:621
  14.7 0.1 collective-permute-done.7.ghost_z
  14.8 4.0 %shard_map.123 = (f32[24,64,256]{2,1,0:T(8,128)S(1)}, f32[24,64,256]{2,1,0:T(8,128)S(1)}, f32[24,64,256]{2,1,0:T(8,128)S(1)}, f32[24,64,256]{2,1,0:T(8,128)S(1)}...) custom-call(f32[2,72,128]{2,1,0:T(8,128)S(1)} %collective-permute-done.1.ghost, ...), custom_call_target="tpu_custom_call" | custom-call | flops 5000000000 | bytes 2000000 | tf_op jit(solution)/shard_map/pallas_call | solution.py:588
  18.8 10.8 %shard_map.124 = (f32[3,3,4,128]{3,2,1,0:T(4,128)S(1)}, f32[8,256]{1,0:T(8,128)S(1)}) custom-call(f32[2,72,128]{2,1,0:T(8,128)S(1)} %pad_maximum_fusion.1.refs_0_, f32[2,72,128]{2,1,0:T(8,128)S(1)} %collective-permute-done.6.refs_1_, s32[2,1,256]{2,1,0:T(1,128)S(1)} %reshape.36.limits.refs_0_.refs_2_, ...), custom_call_target="tpu_custom_call" | custom-call | flops 12000000000 | bytes 2000000 | tf_op jit(solution)/shard_map/pallas_call | solution.py:597
  29.7 3.2 %collective-permute-start.8 = (f32[3,4,128]{2,1,0:T(4,128)S(1)}, f32[3,4,128]{2,1,0:T(4,128)S(1)}, u32[]{:S(2)}, u32[]{:S(2)}) collective-permute-start(f32[3,4,128]{2,1,0:T(4,128)S(1)} %slice_bitcast_fusion.1), channel_id=1, source_target_pairs={{0,12},{4,8},{8,4},{12,0},{1,13},{5,9},{9,5},{13,1},{2,14},{6,10},... | collective-permute-start | bytes 18440 | tf_op jit(solution)/shard_map/ppermute | solution.py:690
  32.8 7.1 %shard_map.125 = (f32[3,3,4,128]{3,2,1,0:T(4,128)S(1)}, f32[8,256]{1,0:T(8,128)S(1)}) custom-call(bf16[608,192]{1,0:T(8,128)(2,1)S(1)} %get-tuple-element.48.refs_1_.refs_3_.merged, f32[1,64]{1,0:T(1,128)S(1)} %bitcast.33, s32[2,24,256]{2,1,0:T(8,128)S(1)} %get-tuple-element.49.refs_5_.refs_7_.lane_i, ...), custom_call_target="tpu_custom_call" | custom-call | flops 20000000000 | bytes 2000000 | tf_op jit(solution)/shard_map/pallas_call | solution.py:592
  40.0 0.3 collective-permute-start.11
  40.4 1.2 %collective-permute-start.9 = (f32[2,3,2,128]{3,2,1,0:T(2,128)S(1)}, f32[2,3,2,128]{3,2,1,0:T(2,128)S(1)}, u32[]{:S(2)}, u32[]{:S(2)}) collective-permute-start(f32[2,3,2,128]{3,2,1,0:T(2,128)S(1)} %pad_maximum_fusion.2), channel_id=1, source_target_pairs={{0,2},{2,0},{1,3},{3,1},{4,6},{6,4},{5,7},{7,5},{8,10},{10,8},{9,1... | collective-permute-start | bytes 18440 | tf_op jit(solution)/shard_map/ppermute | solution.py:613
  41.6 2.1 %collective-permute-start.10 = (f32[3,2,128]{2,1,0:T(2,128)S(1)}, f32[3,2,128]{2,1,0:T(2,128)S(1)}, u32[]{:S(2)}, u32[]{:S(2)}) collective-permute-start(f32[3,2,128]{2,1,0:T(2,128)S(1)} %slice_bitcast_fusion.2), channel_id=1, source_target_pairs={{0,4},{4,0},{8,12},{12,8},{1,5},{5,1},{9,13},{13,9},{2,6},{6,2},{1... | collective-permute-start | bytes 9224 | tf_op jit(solution)/shard_map/ppermute | solution.py:695
  43.7 0.8 %collective-permute-done.11 = f32[3,2,128]{2,1,0:T(2,128)S(1)} collective-permute-done((f32[3,2,128]{2,1,0:T(2,128)S(1)}, f32[3,2,128]{2,1,0:T(2,128)S(1)}, u32[]{:S(2)}, u32[]{:S(2)}) %collective-permute-start.11) | collective-permute-done | bytes 3104 | tf_op jit(solution)/shard_map/ppermute | solution.py:613
  44.6 0.7 %collective-permute-done.10 = f32[3,2,128]{2,1,0:T(2,128)S(1)} collective-permute-done((f32[3,2,128]{2,1,0:T(2,128)S(1)}, f32[3,2,128]{2,1,0:T(2,128)S(1)}, u32[]{:S(2)}, u32[]{:S(2)}) %collective-permute-start.10) | collective-permute-done | bytes 3104 | tf_op jit(solution)/shard_map/ppermute | solution.py:695
  45.3 0.1 pad_maximum_fusion.3
  45.4 0.1 reshape.37
  45.5 0.6 %slice.77 = f32[2,2,1,64]{3,2,1,0:T(1,128)} slice(f32[2,2,2,64]{3,2,1,0:T(2,128)S(1)} %reshape.37), slice={[0:2], [0:2], [0:1], [0:64]} | slice | bytes 2048 | tf_op jit(solution)/shard_map/slice | solution.py:702
  46.1 0.5 %collective-permute-done.12 = f32[2,3,2,64]{3,2,1,0:T(2,128)S(1)} collective-permute-done((f32[2,3,2,64]{3,2,1,0:T(2,128)S(1)}, f32[2,3,2,64]{3,2,1,0:T(2,128)S(1)}, u32[]{:S(2)}, u32[]{:S(2)}) %collective-permute-start.12) | collective-permute-done | bytes 3104 | tf_op jit(solution)/shard_map/ppermute | solution.py:613
  46.7 0.6 %copy.22 = f32[3,2,2,64]{3,2,1,0:T(2,128)} copy(f32[3,2,2,64]{3,2,0,1:T(2,128)S(1)} %fusion.1) | data formatting | bytes 6144
  (55 shorter events, 0.6 us)
Async XLA Ops:
  0.6 11.5 %copy-start.6 = (s32[2,2,64]{2,1,0:T(2,128)S(1)}, s32[2,2,64]{2,1,0:T(2,128)}, u32[]{:S(2)}) copy-start(s32[2,2,64]{2,1,0:T(2,128)} %param.14) | copy-start | bytes 3076
  0.6 11.8 %copy-start.5 = (f32[64]{0:T(128)S(1)}, f32[64]{0:T(128)}, u32[]{:S(2)}) copy-start(f32[64]{0:T(128)} %param.21) | copy-start | bytes 772
  0.7 11.8 %copy-start.3 = (f32[128,64]{0,1:T(8,128)S(1)}, f32[128,64]{0,1:T(8,128)}, u32[]{:S(2)}) copy-start(f32[128,64]{0,1:T(8,128)} %param.20) | copy-start | bytes 98308
  0.7 11.8 %copy-start = (f32[64,64]{1,0:T(8,128)S(1)}, f32[64,64]{1,0:T(8,128)}, u32[]{:S(2)}) copy-start(f32[64,64]{1,0:T(8,128)} %w_self.1) | copy-start | bytes 49156
  0.7 11.8 %copy-start.1 = (f32[64,64]{1,0:T(8,128)S(1)}, f32[64,64]{1,0:T(8,128)}, u32[]{:S(2)}) copy-start(f32[64,64]{1,0:T(8,128)} %w_pair.1) | copy-start | bytes 49156
  0.7 11.8 %copy-start.4 = (f32[8,64]{1,0:T(8,128)S(1)}, f32[8,64]{1,0:T(8,128)}, u32[]{:S(2)}) copy-start(f32[8,64]{1,0:T(8,128)} %w_radial.1) | copy-start | bytes 6148
  0.7 11.8 %copy-start.2 = (f32[64,64]{1,0:T(8,128)S(1)}, f32[64,64]{1,0:T(8,128)}, u32[]{:S(2)}) copy-start(f32[64,64]{1,0:T(8,128)} %w_tensor.1) | copy-start | bytes 49156
  2.1 6.7 %collective-permute-start = (f32[2,72,128]{2,1,0:T(8,128)S(1)}, f32[2,72,128]{2,1,0:T(8,128)S(1)}, u32[]{:S(2)}, u32[]{:S(2)}) collective-permute-start(f32[2,72,128]{2,1,0:T(8,128)S(1)} %reverse_select_fusion.own), channel_id=1, source_target_pairs={{0,2},{2,0},{1,3},{3,1},{4,6},{6,4},{5,7},{7,5},{8,10},{10,8},{9,1... | collective-permute-start | bytes 221192 | tf_op jit(solution)/shard_map/ppermute | solution.py:621
  5.1 7.4 %collective-permute-start.2 = (f32[2,72,128]{2,1,0:T(8,128)S(1)}, f32[2,72,128]{2,1,0:T(8,128)S(1)}, u32[]{:S(2)}, u32[]{:S(2)}) collective-permute-start(f32[2,72,128]{2,1,0:T(8,128)S(1)} %reverse_select_fusion.own), channel_id=1, source_target_pairs={{0,1},{1,0},{2,3},{3,2},{4,5},{5,4},{6,7},{7,6},{8,9},{9,8},{10,11... | collective-permute-start | bytes 221192 | tf_op jit(solution)/shard_map/ppermute | solution.py:621
  5.1 7.2 %collective-permute-start.4 = (f32[72,128]{1,0:T(8,128)S(1)}, f32[72,128]{1,0:T(8,128)S(1)}, u32[]{:S(2)}, u32[]{:S(2)}) collective-permute-start(f32[72,128]{1,0:T(8,128)S(1)} %get-tuple-element.84), channel_id=1, source_target_pairs={{0,12},{4,8},{8,4},{12,0},{1,13},{5,9},{9,5},{13,1},{2,14},{6,10},... | collective-permute-start | bytes 110600 | tf_op jit(solution)/shard_map/ppermute | solution.py:660
  8.7 1.3 %collective-permute-start.3 = (f32[2,72,128]{2,1,0:T(8,128)S(1)}, f32[2,72,128]{2,1,0:T(8,128)S(1)}, u32[]{:S(2)}, u32[]{:S(2)}) collective-permute-start(f32[2,72,128]{2,1,0:T(8,128)S(1)} %collective-permute-done.sides), channel_id=1, source_target_pairs={{0,1},{1,0},{2,3},{3,2},{4,5},{5,4},{6,7},{7,6},{8,9},{9,8},{10,11... | collective-permute-start | bytes 221192 | tf_op jit(solution)/shard_map/ppermute | solution.py:621
  8.9 4.6 %collective-permute-start.1 = (f32[2,72,128]{2,1,0:T(8,128)S(1)}, f32[2,72,128]{2,1,0:T(8,128)S(1)}, u32[]{:S(2)}, u32[]{:S(2)}) collective-permute-start(f32[2,72,128]{2,1,0:T(8,128)S(1)} %pad_maximum_fusion), channel_id=1, source_target_pairs={{0,4},{4,0},{8,12},{12,8},{1,5},{5,1},{9,13},{13,9},{2,6},{6,2},{1... | collective-permute-start | bytes 221192 | tf_op jit(solution)/shard_map/ppermute | solution.py:661
  12.3 1.2 %collective-permute-start.5 = (f32[72,128]{1,0:T(8,128)S(1)}, f32[72,128]{1,0:T(8,128)S(1)}, u32[]{:S(2)}, u32[]{:S(2)}) collective-permute-start(f32[72,128]{1,0:T(8,128)S(1)} %collective-permute-done.4), channel_id=1, source_target_pairs={{0,1},{1,0},{2,3},{3,2},{4,5},{5,4},{6,7},{7,6},{8,9},{9,8},{10,11... | collective-permute-start | bytes 110600 | tf_op jit(solution)/shard_map/ppermute | solution.py:621
  13.5 1.3 %collective-permute-start.7 = (f32[2,72,128]{2,1,0:T(8,128)S(1)}, f32[2,72,128]{2,1,0:T(8,128)S(1)}, u32[]{:S(2)}, u32[]{:S(2)}) collective-permute-start(f32[2,72,128]{2,1,0:T(8,128)S(1)} %collective-permute-done.1.ghost), channel_id=1, source_target_pairs={{0,1},{1,0},{2,3},{3,2},{4,5},{5,4},{6,7},{7,6},{8,9},{9,8},{10,11... | collective-permute-start | bytes 221192 | tf_op jit(solution)/shard_map/ppermute | solution.py:621
  13.5 5.3 %collective-permute-start.6 = (f32[2,72,128]{2,1,0:T(8,128)S(1)}, f32[2,72,128]{2,1,0:T(8,128)S(1)}, u32[]{:S(2)}, u32[]{:S(2)}) collective-permute-start(f32[2,72,128]{2,1,0:T(8,128)S(1)} %pad_maximum_fusion.1.refs_0_), channel_id=1, source_target_pairs={{0,2},{2,0},{1,3},{3,1},{4,6},{6,4},{5,7},{7,5},{8,10},{10,8},{9,1... | collective-permute-start | bytes 221192 | tf_op jit(solution)/shard_map/ppermute | solution.py:621
  29.7 10.3 %collective-permute-start.8 = (f32[3,4,128]{2,1,0:T(4,128)S(1)}, f32[3,4,128]{2,1,0:T(4,128)S(1)}, u32[]{:S(2)}, u32[]{:S(2)}) collective-permute-start(f32[3,4,128]{2,1,0:T(4,128)S(1)} %slice_bitcast_fusion.1), channel_id=1, source_target_pairs={{0,12},{4,8},{8,4},{12,0},{1,13},{5,9},{9,5},{13,1},{2,14},{6,10},... | collective-permute-start | bytes 18440 | tf_op jit(solution)/shard_map/ppermute | solution.py:690
  40.0 4.6 %collective-permute-start.11 = (f32[3,2,128]{2,1,0:T(2,128)S(1)}, f32[3,2,128]{2,1,0:T(2,128)S(1)}, u32[]{:S(2)}, u32[]{:S(2)}) collective-permute-start(f32[3,2,128]{2,1,0:T(2,128)S(1)} %pad_maximum_fusion.4), channel_id=1, source_target_pairs={{0,6},{2,4},{4,2},{6,0},{8,14},{10,12},{12,10},{14,8},{1,7},{3,5},... | collective-permute-start | bytes 9224 | tf_op jit(solution)/shard_map/ppermute | solution.py:613
  40.4 4.9 %collective-permute-start.9 = (f32[2,3,2,128]{3,2,1,0:T(2,128)S(1)}, f32[2,3,2,128]{3,2,1,0:T(2,128)S(1)}, u32[]{:S(2)}, u32[]{:S(2)}) collective-permute-start(f32[2,3,2,128]{3,2,1,0:T(2,128)S(1)} %pad_maximum_fusion.2), channel_id=1, source_target_pairs={{0,2},{2,0},{1,3},{3,1},{4,6},{6,4},{5,7},{7,5},{8,10},{10,8},{9,1... | collective-permute-start | bytes 18440 | tf_op jit(solution)/shard_map/ppermute | solution.py:613
  41.6 3.7 %collective-permute-start.10 = (f32[3,2,128]{2,1,0:T(2,128)S(1)}, f32[3,2,128]{2,1,0:T(2,128)S(1)}, u32[]{:S(2)}, u32[]{:S(2)}) collective-permute-start(f32[3,2,128]{2,1,0:T(2,128)S(1)} %slice_bitcast_fusion.2), channel_id=1, source_target_pairs={{0,4},{4,0},{8,12},{12,8},{1,5},{5,1},{9,13},{13,9},{2,6},{6,2},{1... | collective-permute-start | bytes 9224 | tf_op jit(solution)/shard_map/ppermute | solution.py:695
  45.4 1.2 %collective-permute-start.12 = (f32[2,3,2,64]{3,2,1,0:T(2,128)S(1)}, f32[2,3,2,64]{3,2,1,0:T(2,128)S(1)}, u32[]{:S(2)}, u32[]{:S(2)}) collective-permute-start(f32[2,3,2,64]{3,2,1,0:T(2,128)S(1)} %pad_maximum_fusion.3), channel_id=1, source_target_pairs={{0,1},{1,0},{2,3},{3,2},{4,5},{5,4},{6,7},{7,6},{8,9},{9,8},{10,11... | collective-permute-start | bytes 9224 | tf_op jit(solution)/shard_map/ppermute | solution.py:613
